TPU v7x, 32 devices: a whole 2x2x4 slice. The times are simulated.
32 devices in a mesh: ctx: 2 (over x), chan: 4 (over z), dp: 4 (over y, core).
Axes of the slice: x: 2, y: 2, z: 4, core: 2. Of those that a mesh axis runs over, the one named last changes fastest.
Arguments:
- projected: bfloat16 [3, 1024, 8192], P(None, ('dp', 'ctx'), 'chan'), parts along dimension 1, may hold values from -6 to 6
- short_weight: float32 [7, 3, 8192], P(None, None, 'chan'), may hold values from -2 to 2
- pos_in: float32 [33, 64], replicated, may hold values from -1 to 1
- pos_bias: float32 [64], replicated, may hold values from -4 to 4
- sine_freq: float32 [64], replicated, may hold values from 1.5 to 3
- pos_mid: float32 [64, 64], replicated, may hold values from -0.75 to 0.75
- pos_out: float32 [64, 8192], P(None, 'chan'), may hold values from -0.75 to 0.75
- decay_rate: float32 [8192], P('chan'), may hold values from 0.000390625 to 0.05
- skip_gain: float32 [8192], P('chan'), may hold values from -4 to 4
Outputs:
- mixed: bfloat16 [1024, 8192], P(('dp', 'ctx'), 'chan'), parts along dimension 0
There are 4 independent parts, one for each index of `dp`. A program takes and returns all parts, laid end to end along the dimension named above; an argument that names none is the same for every part. Nothing has to cross between parts.
All inputs are finite; a program needn't handle non-finite values.
Results may differ from a plain program's by a relative error of at most 0.001.
Values may be sent and summed in bfloat16 or wider, within the bound.
No kernel may reach another device: no remote copies, remote signals or barrier semaphores. Data moves between devices by JAX's collectives and lax.ppermute only.
A program may use at most 128 MiB of HBM per device.

v0:
```python
import functools
import math

import jax
import jax.numpy as jnp
import numpy as np
from jax import lax
from jax.experimental import pallas as pl
from jax.experimental.pallas import tpu as pltpu
from jax.sharding import PartitionSpec as P

BANDS = 16
TAPS = 7
SPAN = 250.0
TINY = 1e-30

HIGHEST = lax.Precision.HIGHEST


def shifted(x, axis, by):
    size = lax.axis_size(axis)
    pairs = [(i, i + by) for i in range(size) if 0 <= i + by < size]
    return lax.ppermute(x, axis, pairs)


def features(positions, total_len):
    band_ids = jnp.arange(1, BANDS + 1, dtype=jnp.float32)
    angles = positions[:, None] * band_ids[None, :] * (2.0 * math.pi / total_len)
    return jnp.concatenate(
        [positions[:, None] / total_len, jnp.cos(angles), jnp.sin(angles)], axis=1
    )


def second_rows(positions, total_len, pos_in, pos_bias, sine_freq, pos_mid):
    inputs = features(positions, total_len)
    first_layer = jnp.sin(
        sine_freq
        * (
            jnp.dot(inputs, pos_in, precision=HIGHEST, preferred_element_type=jnp.float32)
            + pos_bias
        )
    )
    return jnp.sin(
        sine_freq
        * jnp.dot(first_layer, pos_mid, precision=HIGHEST, preferred_element_type=jnp.float32)
    )


def filter_rows(positions, total_len, pos_in, pos_bias, sine_freq, pos_mid, pos_out, decay_rate):
    second_layer = second_rows(positions, total_len, pos_in, pos_bias, sine_freq, pos_mid)
    raw_filter = jnp.dot(
        second_layer, pos_out, precision=HIGHEST, preferred_element_type=jnp.float32
    )
    return raw_filter * jnp.exp(-decay_rate[None, :] * positions[:, None])


def halves(x):
    high = x.astype(jnp.bfloat16)
    low = (x - high.astype(jnp.float32)).astype(jnp.bfloat16)
    return high, low


def parity_order(rows):
    place = np.arange(rows)
    parity, inner = place // (rows // 2), place % (rows // 2)
    return rows // 8 * (inner % 8) + inner // 8 * 2 + parity


def table_columns(table):
    high = table.astype(jnp.bfloat16)
    low = (table - high.astype(np.float32)).astype(jnp.bfloat16)
    return np.concatenate([high, high, low], axis=1)


def odd_tables(rows):
    half = rows // 2
    order = np.concatenate([np.arange(0, half, 2), np.arange(1, half, 2)])
    turns = (2 * order[:, None] + 1) * parity_order(rows)[None, :] % (4 * rows)
    angles = turns * (np.pi / (2 * rows))
    forward = np.concatenate([np.cos(angles), -np.sin(angles)], axis=0).astype(np.float32)
    pieces = [forward[:, :half], forward[:, half:]]
    return (
        np.concatenate([table_columns(piece) for piece in pieces], axis=0),
        np.concatenate([table_columns(piece.T / np.float32(rows)) for piece in pieces], axis=0),
    )


def each_tile(tiles, unroll, action):
    count = math.gcd(tiles, unroll)

    def step(at, _):
        for number in range(count):
            action(at * count + number, number)
        return 0

    if tiles == count:
        step(0, 0)
    else:
        lax.fori_loop(0, tiles // count, step, 0)


def put_halves(ref, parity, row, cols, value):
    size = ref.shape[1] // 2
    high, low = halves(value)
    count = value.shape[0]
    ref[parity, row : row + count, cols] = high
    ref[parity, size + row : size + row + count, cols] = low


def three_pass(table, ref, parity):
    size = ref.shape[1] // 2
    both = jnp.concatenate([ref[parity], ref[parity, :size]], axis=0)
    return jnp.dot(table, both, preferred_element_type=jnp.float32)


def forward_dots(forward_ref, parts_ref, spec_ref):
    rows = spec_ref.shape[1]
    for parity in range(2):
        spec_ref[parity] = three_pass(forward_ref[parity * rows : (parity + 1) * rows], parts_ref, parity)


def backward_dots(backward_ref, bins_ref, conv_ref):
    half = conv_ref.shape[0] // 2
    for parity in range(2):
        rows = slice(parity * half, (parity + 1) * half)
        conv_ref[rows] = three_pass(backward_ref[rows], bins_ref, parity)


def unfolded(spec_ref, row, cols):
    half = spec_ref.shape[1] // 2
    even_cos, odd_cos = spec_ref[0, row : row + 16, cols], spec_ref[1, row : row + 16, cols]
    sine = slice(half + row, half + row + 16)
    even_sin, odd_sin = spec_ref[0, sine, cols], spec_ref[1, sine, cols]
    return even_cos + odd_cos, even_sin + odd_sin, even_cos - odd_cos, odd_sin - even_sin


def filtered(spec_ref, filter_ref, bins_ref, cols, filter_cols):
    half = spec_ref.shape[1] // 2
    for row in range(0, half, 16):
        real, imag, real_far, imag_far = unfolded(spec_ref, row, cols)
        taps = [filter_ref[at * half + row : at * half + row + 16, filter_cols] for at in range(4)]
        out_real, out_imag = real * taps[0] - imag * taps[1], real * taps[1] + imag * taps[0]
        far_real = real_far * taps[2] - imag_far * taps[3]
        far_imag = real_far * taps[3] + imag_far * taps[2]
        put_halves(bins_ref, 0, row, cols, out_real + far_real)
        put_halves(bins_ref, 0, half + row, cols, out_imag - far_imag)
        put_halves(bins_ref, 1, row, cols, out_real - far_real)
        put_halves(bins_ref, 1, half + row, cols, out_imag + far_imag)


def strided_rows(values, buf):
    buf[...] = values.astype(jnp.float32)
    count = buf.shape[0] // 8
    return [buf[pl.ds(v, 8, stride=count), :] for v in range(count)]


def short_sum(parts, rim, taps_ref, at, cols):
    top = lax.broadcasted_iota(jnp.int32, (8, 128), 0) == 0
    before = {}
    for back in range(1, TAPS):
        edge = 0.0 if rim is None else rim[8 - back : 9 - back]
        before[-back] = jnp.where(top, edge, pltpu.roll(parts[-back], 1, 0))
    taps = [jnp.broadcast_to(taps_ref[at, k : k + 1, cols], (8, 128)) for k in range(TAPS)]
    sums = []
    for v in range(len(parts)):
        terms = [taps[k] * (parts[v - k] if v >= k else before[v - k]) for k in range(TAPS)]
        sums.append(((terms[0] + terms[1]) + (terms[2] + terms[3])) + ((terms[4] + terms[5]) + terms[6]))
    return sums


def parity_rows(parts):
    ordered = parts[0::2] + parts[1::2]
    return [jnp.concatenate(ordered[i : i + 2], axis=0) for i in range(0, len(ordered), 2)]


def natural_rows(ref_rows, buf):
    count = buf.shape[0] // 8
    for at, value in enumerate(ref_rows):
        for piece in range(2):
            number = 2 * at + piece
            v = number % (count // 2) * 2 + number // (count // 2)
            buf[pl.ds(v, 8, stride=count), :] = value[8 * piece : 8 * piece + 8]
    return buf[...]


def tile_lanes(tile, first=0):
    return pl.ds(pl.multiple_of(first + tile * 128, 128), 128)


def tile_rows(tile, row, count=16):
    return pl.ds(pl.multiple_of(tile * 128 + row, 16), count)


def place_level(peak, tile, peak_buf, levels_buf):
    for step in (1, 2, 4):
        peak = jnp.maximum(peak, pltpu.roll(peak, step, 0))
    level = jnp.maximum(peak, TINY)
    wide = level * 65537.0
    level = wide - (wide - level)
    peak_buf[:, tile_lanes(tile)] = SPAN / level
    levels_buf[pl.ds(tile, 1), :] = level[0:1]


def put_coded(coded_ref, tile, row, value, gain):
    coded = jnp.exp2(jnp.abs(value) * gain - SPAN / 2)
    coded_ref[tile_rows(tile, row), :] = jnp.where(value < 0, -coded, coded).astype(jnp.bfloat16)


def decoder(levels_buf, tile):
    level = levels_buf[pl.ds(tile, 1), :]
    slope = jnp.broadcast_to(level * (1.0 / (math.log(2.0) * SPAN)), (16, 128))
    middle = jnp.broadcast_to(level / 2, (16, 128))

    def decode(coded):
        coded = coded.astype(jnp.float32)
        size = jnp.log(jnp.abs(coded)) * slope + middle
        return jnp.where(coded < 0, -size, size)

    return decode


def encode_kernel(
    first, projected_ref, taps_ref, coded_ref, driven_ref, rows_buf, rim_buf, taps_buf, strided_buf, peak_buf,
    levels_buf, sems,
):
    rows, size = rows_buf.shape[1:]
    tiles = size // 128
    span = pl.ds(first, size)
    with_rims = coded_ref.shape[0] > tiles * rows + 16

    @pl.when(lax.axis_index("ctx") == 0)
    def _():
        copies = [
            pltpu.make_async_copy(taps_ref.at[:, :, span], taps_buf, sems.at[0]),
            pltpu.make_async_copy(projected_ref.at[0, :, span], rows_buf.at[0], sems.at[1]),
            pltpu.make_async_copy(projected_ref.at[2, :, span], rows_buf.at[1], sems.at[2]),
        ]
        if with_rims:
            copies.append(pltpu.make_async_copy(projected_ref.at[:, pl.ds(rows - 16, 16)], rim_buf, sems.at[3]))
        for copy in copies:
            copy.start()
        for copy in copies:
            copy.wait()

        def drive(tile, number):
            cols = tile_lanes(tile)
            sums = [
                short_sum(
                    strided_rows(rows_buf[way, :, cols], strided_buf.at[number, way]), None, taps_buf, 2 * way, cols
                )
                for way in range(2)
            ]
            driven = [one * two for one, two in zip(*sums)]
            for row, value in enumerate(parity_rows(driven)):
                driven_ref[16 * row : 16 * row + 16, cols] = value
            peak_buf[:, cols] = functools.reduce(jnp.maximum, [jnp.abs(value) for value in driven])

        each_tile(tiles, strided_buf.shape[0], drive)
        each_tile(
            tiles, 4, lambda tile, _: place_level(peak_buf[:, tile_lanes(tile)], tile, peak_buf, levels_buf)
        )
        coded_ref[tiles * rows : tiles * rows + 16] = levels_buf[...].astype(jnp.bfloat16)

        def code(tile, _):
            cols = tile_lanes(tile)
            gain = peak_buf[:, cols]
            gain = jnp.concatenate([gain, gain], axis=0)
            for row in range(0, rows, 16):
                put_coded(coded_ref, tile, row, driven_ref[row : row + 16, cols], gain)

        each_tile(tiles, 4, code)
        if with_rims:

            def rims(pair, _):
                for at in range(3):
                    values = [
                        rim_buf[at, :, tile_lanes(2 * pair + way)].astype(jnp.float32)[8:] for way in range(2)
                    ]
                    there = pl.ds(pl.multiple_of(tiles * rows + 16 + pair * 48 + at * 16, 16), 16)
                    coded_ref[there, :] = jnp.concatenate(values, axis=0).astype(jnp.bfloat16)

            each_tile(rim_buf.shape[2] // 256, 4, rims)


def filter_kernel(
    second_ref, out_ref, decay_ref, skip_ref, places_ref, forward_ref, near_ref, far_ref, raw_buf, parts_buf, spec_buf,
    scale_buf,
):
    rows, width = near_ref.shape[0] // 2, near_ref.shape[1]
    half = rows // 2
    second_high, second_low = halves(second_ref[...])
    second = jnp.concatenate([second_high, second_high, second_low], axis=1)
    out_high, out_low = halves(out_ref[...])
    raw_buf[...] = jnp.dot(
        second, jnp.concatenate([out_high, out_low, out_high], axis=0), preferred_element_type=jnp.float32
    )

    def decay(tile, _):
        cols = tile_lanes(tile)
        fall = -decay_ref[:, cols]
        total = jnp.zeros((8, 128), jnp.float32)
        for row in range(0, 2 * rows, 16):
            taps = raw_buf[row : row + 16, cols] * jnp.exp(fall * places_ref[row : row + 16])
            total = total + (taps[:8] * taps[:8] + taps[8:] * taps[8:])
            parity = row % rows // half
            put_halves(parts_buf, parity, row % half, tile_lanes(tile, row // rows * width), taps)
        for step in (1, 2, 4):
            total = total + pltpu.roll(total, step, 0)
        scale_buf[:, cols] = 1.0 / jnp.sqrt(total + 1e-05)

    each_tile(width // 128, 4, decay)
    forward_dots(forward_ref, parts_buf, spec_buf)

    def shape(tile, _):
        cols = tile_lanes(tile)
        scale = scale_buf[:, cols]
        scale = jnp.concatenate([scale, scale], axis=0)
        skip = skip_ref[:, cols]
        for row in range(0, half, 16):
            low = [value * scale for value in unfolded(spec_buf, row, cols)]
            high = [value * scale for value in unfolded(spec_buf, row, tile_lanes(tile, width))]
            sign = 1 if row < half // 2 else -1
            turned = [-sign * low[1], sign * low[0], sign * low[3], -sign * low[2]]
            low = [low[0] + skip, low[1], low[2] + skip, low[3]]
            for at in range(4):
                near_ref[at * half + row : at * half + row + 16, cols] = low[at]
                far_ref[at * half + row : at * half + row + 16, cols] = high[at] + turned[at]

    each_tile(width // 128, 4, shape)


def own_kernel(
    first, send, projected_ref, rims_ref, taps_ref, near_ref, far_ref, forward_ref, backward_ref, *refs
):
    if send:
        base_ref, right_ref, mixed_ref, coded_ref, *bufs = refs
    else:
        *driven_refs, _, base_ref, right_ref, mixed_ref = refs[:6]
        bufs = refs[6:]
    strided_buf, parts_buf, spec_buf, bins_buf, mixed_buf, sems = bufs[:6]
    rows, width = base_ref.shape
    half = rows // 2
    tiles = width // 128
    first_tile = first // 128
    rims_at = rims_ref.shape[0] - projected_ref.shape[2] // 128 * 24
    place = lax.axis_index("ctx")

    def sums_of(tile, number, ats):
        cols = tile_lanes(tile, first)
        far_tile = tile + first_tile
        sums = []
        for at in ats:
            pair = pl.ds(pl.multiple_of(rims_at + far_tile // 2 * 48 + at * 16, 16), 16)
            rim = rims_ref[pair, :].astype(jnp.float32)
            rim = jnp.where(far_tile % 2 == 0, rim[:8], rim[8:])
            parts = strided_rows(projected_ref[at, :, cols], strided_buf.at[number, at])
            sums.append(short_sum(parts, rim, taps_ref, at, cols))
        return sums

    def put_right(tile, values):
        for at, value in enumerate(parity_rows(values)):
            right_ref[16 * at : 16 * at + 16, tile_lanes(tile)] = value

    def drive(tile, number):
        sums = sums_of(tile, number, range(3))
        put_right(tile, sums[1])
        driven = [one * two for one, two in zip(sums[0], sums[2])]
        for at, value in enumerate(parity_rows(driven)):
            put_halves(parts_buf, 16 * at // half, 16 * at % half, tile_lanes(tile), value)

    if send:
        each_tile(tiles, strided_buf.shape[0], drive)
    else:

        @pl.when(place != 0)
        def _():
            each_tile(tiles, strided_buf.shape[0], drive)

        @pl.when(place == 0)
        def _():
            each_tile(tiles, strided_buf.shape[0], lambda tile, number: put_right(tile, sums_of(tile, number, [1])[0]))
            start = 0
            for ref in driven_refs:

                def recall(tile, _, ref=ref, start=start):
                    for row in range(0, rows, 16):
                        value = ref[row : row + 16, tile_lanes(tile)]
                        put_halves(parts_buf, row // half, row % half, tile_lanes(tile, start), value)

                each_tile(ref.shape[1] // 128, 4, recall)
                start += ref.shape[1]

    forward_dots(forward_ref, parts_buf, spec_buf)
    if send:
        conv_buf, peak_buf, levels_buf = bufs[6:]

        @pl.when(place == 0)
        def _():
            each_tile(
                tiles, 4,
                lambda tile, _: filtered(spec_buf, far_ref, bins_buf, tile_lanes(tile), tile_lanes(tile, first)),
            )
            backward_dots(backward_ref, bins_buf, conv_buf)

            def peaks(tile, _):
                cols = tile_lanes(tile)
                peak = functools.reduce(
                    jnp.maximum, [jnp.abs(conv_buf[row : row + 8, cols]) for row in range(0, rows, 8)]
                )
                place_level(peak, tile, peak_buf, levels_buf)

            each_tile(tiles, 4, peaks)
            coded_ref[tiles * rows : tiles * rows + 16] = levels_buf[...].astype(jnp.bfloat16)

            def code(tile, _):
                cols = tile_lanes(tile)
                gain = peak_buf[:, cols]
                gain = jnp.concatenate([gain, gain], axis=0)
                for row in range(0, rows, 16):
                    put_coded(coded_ref, tile, row, conv_buf[row : row + 16, cols], gain)

            each_tile(tiles, 4, code)

    each_tile(
        tiles, 4, lambda tile, _: filtered(spec_buf, near_ref, bins_buf, tile_lanes(tile), tile_lanes(tile, first))
    )
    backward_dots(backward_ref, bins_buf, base_ref)

    @pl.when(place == 0)
    def _():
        def mix(tile, number):
            cols = tile_lanes(tile)
            values = [right_ref[at : at + 16, cols] * base_ref[at : at + 16, cols] for at in range(0, rows, 16)]
            mixed_buf[:, cols] = natural_rows(values, strided_buf.at[number, 0]).astype(jnp.bfloat16)

        each_tile(tiles, strided_buf.shape[0], mix)
        copy = pltpu.make_async_copy(mixed_buf, mixed_ref.at[:, pl.ds(first, width)], sems.at[0])
        copy.start()
        copy.wait()


def read_levels(coded_ref, levels_buf, tiles, rows):
    levels_buf[...] = coded_ref[tiles * rows : tiles * rows + 16].astype(jnp.float32)


def join_kernel(
    one_ref, two_ref, far_ref, base_ref, right_ref, forward_ref, backward_ref, sofar_ref, mixed_ref,
    parts_buf, spec_buf, bins_buf, conv_buf, strided_buf, buf, levels_buf, sems,
):
    rows, width = base_ref.shape
    half = rows // 2
    tiles = width // 128
    later = (two_ref.shape[0] - 16) // rows
    counts = [tiles - later, later]

    @pl.when(lax.axis_index("ctx") != 0)
    def _():
        start = 0
        for at, ref in enumerate((one_ref, two_ref)):
            read_levels(ref, levels_buf.at[at], counts[at], rows)

            def spread_out(tile, _, ref=ref, at=at, start=start):
                decode = decoder(levels_buf.at[at], tile)
                for row in range(0, rows, 16):
                    value = decode(ref[tile_rows(tile, row), :])
                    put_halves(parts_buf, row // half, row % half, tile_lanes(tile, start), value)

            each_tile(counts[at], 4, spread_out)
            start += counts[at] * 128
        forward_dots(forward_ref, parts_buf, spec_buf)
        each_tile(
            tiles, 4, lambda tile, _: filtered(spec_buf, far_ref, bins_buf, tile_lanes(tile), tile_lanes(tile))
        )
        backward_dots(backward_ref, bins_buf, conv_buf)

        def mix(tile, number):
            cols = tile_lanes(tile)
            values = [
                right_ref[at : at + 16, cols] * (conv_buf[at : at + 16, cols] + base_ref[at : at + 16, cols])
                for at in range(0, rows, 16)
            ]
            buf[:, cols] = natural_rows(values, strided_buf.at[number]).astype(jnp.bfloat16)

        each_tile(tiles, strided_buf.shape[0], mix)
        copy = pltpu.make_async_copy(buf, mixed_ref.at[:, pl.ds(0, width)], sems.at[0])
        copy.start()
        copy.wait()


def last_kernel(
    first, coded_ref, base_ref, right_ref, sofar_ref, mixed_ref, strided_buf, buf, levels_buf, sems
):
    rows, width = base_ref.shape
    tiles = width // 128

    @pl.when(lax.axis_index("ctx") != 0)
    def _():
        read_levels(coded_ref, levels_buf, tiles, rows)

        def mix(tile, number):
            cols = tile_lanes(tile)
            decode = decoder(levels_buf, tile)
            values = [
                right_ref[at : at + 16, cols] * (decode(coded_ref[tile_rows(tile, at), :]) + base_ref[at : at + 16, cols])
                for at in range(0, rows, 16)
            ]
            buf[:, cols] = natural_rows(values, strided_buf.at[number]).astype(jnp.bfloat16)

        each_tile(tiles, strided_buf.shape[0], mix)
        copy = pltpu.make_async_copy(buf, mixed_ref.at[:, pl.ds(first, width)], sems.at[0])
        copy.start()
        copy.wait()


def params(mib=40):
    return pltpu.CompilerParams(vmem_limit_bytes=mib * 1024 * 1024)


def cost(us):
    return pl.CostEstimate(flops=int(us * 1e9), bytes_accessed=int(us * 3e6), transcendentals=0)


def one_way(
    projected, short_weight, pos_in, pos_bias, sine_freq, pos_mid, pos_out, decay_rate, skip_gain
):
    _, rows, width = projected.shape
    half = rows // 2
    total_len = 2 * rows
    ahead = [width // 8, width * 5 // 8]
    middle = sum(ahead)
    behind = width - middle
    forward, backward = odd_tables(rows)
    taps = jnp.transpose(short_weight, (1, 0, 2))
    in_vmem = pl.BlockSpec(memory_space=pltpu.VMEM)
    in_hbm = pl.BlockSpec(memory_space=pltpu.HBM)
    floats, shorts = functools.partial(pltpu.VMEM, dtype=jnp.float32), functools.partial(pltpu.VMEM, dtype=jnp.bfloat16)
    pairs = [(0, 1)]

    def arrays(*shapes, dtype=jnp.float32):
        return [jax.ShapeDtypeStruct(shape, dtype) for shape in shapes]

    def message(size, more=0):
        return arrays((size // 128 * rows + 16 + more, 128), dtype=jnp.bfloat16)

    coded, driven = [], []
    for at, size in enumerate(ahead):
        code, signal = pl.pallas_call(
            functools.partial(encode_kernel, sum(ahead[:at])),
            in_specs=[in_hbm, in_hbm],
            out_specs=[in_vmem] * 2,
            out_shape=message(size, width // 128 * 24 if at == 0 else 0) + arrays((rows, size)),
            scratch_shapes=[
                shorts((2, rows, size)),
                shorts((3, 16, width)),
                floats((3, TAPS, size)),
                floats((2, 2, rows, 128)),
                floats((8, size)),
                floats((16, 128)),
                pltpu.SemaphoreType.DMA((4,)),
            ],
            compiler_params=params(),
            cost_estimate=cost(1),
            name="encode",
        )(
            pltpu.with_memory_space_constraint(projected, pltpu.HBM),
            pltpu.with_memory_space_constraint(taps, pltpu.HBM),
        )
        coded.append(lax.ppermute(code, "ctx", pairs))
        driven.append(signal)

    order = parity_order(rows)
    places = np.concatenate([order, order + rows]).astype(np.float32)
    second = second_rows(jnp.asarray(places), total_len, pos_in, pos_bias, sine_freq, pos_mid)
    near, far = pl.pallas_call(
        filter_kernel,
        in_specs=[in_vmem] * 6,
        out_specs=[in_vmem] * 2,
        out_shape=arrays((total_len, width), (total_len, width)),
        scratch_shapes=[
            floats((total_len, width)),
            shorts((2, rows, 2 * width)),
            floats((2, rows, 2 * width)),
            floats((8, width)),
        ],
        compiler_params=params(),
        cost_estimate=cost(3),
        name="filter",
    )(second, pos_out, decay_rate[None, :], skip_gain[None, :], jnp.asarray(np.repeat(places[:, None], 128, 1)), forward)

    def own(first, size, send, *more):
        return pl.pallas_call(
            functools.partial(own_kernel, first, send),
            in_specs=[in_vmem] * 7 + [in_vmem, in_vmem, in_hbm][: len(more)],
            out_specs=[in_vmem, in_vmem, in_hbm] + [in_vmem] * send,
            out_shape=arrays((rows, size), (rows, size))
            + arrays((rows, width), dtype=jnp.bfloat16)
            + message(size) * send,
            input_output_aliases={} if send else {9: 2},
            scratch_shapes=[
                floats((2, 3, rows, 128)),
                shorts((2, rows, size)),
                floats((2, rows, size)),
                shorts((2, 2 * rows, size)),
                shorts((rows, size)),
                pltpu.SemaphoreType.DMA((1,)),
            ]
            + [floats((rows, size)), floats((8, size)), floats((16, 128))] * send,
            compiler_params=params(),
            cost_estimate=cost(2),
            name="own",
        )(projected, coded[0], taps, near, far, forward, backward, *more)

    last_base, last_right, mixed, code = own(middle, behind, True)
    last_code = lax.ppermute(code, "ctx", pairs)
    base, right, mixed = own(0, middle, False, *driven, mixed)
    mixed = pl.pallas_call(
        join_kernel,
        in_specs=[in_vmem] * 7 + [in_hbm],
        out_specs=in_hbm,
        out_shape=jax.ShapeDtypeStruct((rows, width), jnp.bfloat16),
        input_output_aliases={7: 0},
        scratch_shapes=[
            shorts((2, rows, middle)),
            floats((2, rows, middle)),
            shorts((2, 2 * rows, middle)),
            floats((rows, middle)),
            floats((4, rows, 128)),
            shorts((rows, middle)),
            floats((2, 16, 128)),
            pltpu.SemaphoreType.DMA((1,)),
        ],
        compiler_params=params(),
        cost_estimate=cost(2),
        name="join",
    )(*coded, far, base, right, forward, backward, mixed)
    return pl.pallas_call(
        functools.partial(last_kernel, middle),
        in_specs=[in_vmem] * 3 + [in_hbm],
        out_specs=in_hbm,
        out_shape=jax.ShapeDtypeStruct((rows, width), jnp.bfloat16),
        input_output_aliases={3: 0},
        scratch_shapes=[
            floats((4, rows, 128)),
            shorts((rows, behind)),
            floats((16, 128)),
            pltpu.SemaphoreType.DMA((1,)),
        ],
        compiler_params=params(),
        cost_estimate=cost(1),
        name="last",
    )(last_code, last_base, last_right, mixed)


def turn_table(outer_ids, inner_ids, modulus):
    product_grid = outer_ids[:, None] * inner_ids[None, :] % modulus
    angles = product_grid.astype(jnp.float32) * (2.0 * math.pi / modulus)
    return (jnp.cos(angles), jnp.sin(angles))


def section_outer(table, data):
    return jnp.einsum(
        "ka,cab->ckb", table, data, precision=HIGHEST, preferred_element_type=jnp.float32
    )


def section_inner(table, data):
    return jnp.einsum(
        "ckb,bj->ckj", data, table, precision=HIGHEST, preferred_element_type=jnp.float32
    )


def padded_spectrum(signal, outer_count, inner_count, tables):
    cos_half, sin_half, cos_twist, sin_twist, cos_inner, sin_inner = tables
    shaped = signal.reshape(signal.shape[0], outer_count // 2, inner_count)
    real_one = section_outer(cos_half, shaped)
    imag_one = -section_outer(sin_half, shaped)
    real_two = real_one * cos_twist + imag_one * sin_twist
    imag_two = imag_one * cos_twist - real_one * sin_twist
    spec_real = section_inner(cos_inner, real_two) + section_inner(sin_inner, imag_two)
    spec_imag = section_inner(cos_inner, imag_two) - section_inner(sin_inner, real_two)
    return (spec_real, spec_imag)


def causal_local(driven_cols, normed_cols, total_len):
    full_len = 2 * total_len
    inner_count = math.gcd(total_len, 128)
    outer_count = full_len // inner_count
    outer_full = jnp.arange(outer_count, dtype=jnp.int32)
    outer_half = jnp.arange(outer_count // 2, dtype=jnp.int32)
    inner_ids = jnp.arange(inner_count, dtype=jnp.int32)
    cos_half, sin_half = turn_table(outer_full, outer_half, outer_count)
    cos_twist, sin_twist = turn_table(outer_full, inner_ids, full_len)
    cos_inner, sin_inner = turn_table(inner_ids, inner_ids, inner_count)
    tables = (cos_half, sin_half, cos_twist, sin_twist, cos_inner, sin_inner)
    sig_real, sig_imag = padded_spectrum(driven_cols, outer_count, inner_count, tables)
    fil_real, fil_imag = padded_spectrum(normed_cols, outer_count, inner_count, tables)
    prod_real = sig_real * fil_real - sig_imag * fil_imag
    prod_imag = sig_real * fil_imag + sig_imag * fil_real
    back_real = section_inner(cos_inner, prod_real) - section_inner(sin_inner, prod_imag)
    back_imag = section_inner(sin_inner, prod_real) + section_inner(cos_inner, prod_imag)
    turned_real = back_real * cos_twist - back_imag * sin_twist
    turned_imag = back_real * sin_twist + back_imag * cos_twist
    cos_last, sin_last = turn_table(outer_half, outer_full, outer_count)
    result = (
        section_outer(cos_last, turned_real) - section_outer(sin_last, turned_imag)
    ) / full_len
    return result.reshape(driven_cols.shape[0], total_len)


def exchanged(
    projected, short_weight, pos_in, pos_bias, sine_freq, pos_mid, pos_out, decay_rate, skip_gain
):
    ctx_count = lax.axis_size("ctx")
    ctx_place = lax.axis_index("ctx")
    block_rows = projected.shape[1]
    total_len = block_rows * ctx_count
    rim_rows = shifted(projected[:, block_rows - (TAPS - 1) :, :], "ctx", 1)
    extended = jnp.concatenate([rim_rows, projected], axis=1)
    short_out = jnp.zeros(projected.shape, jnp.float32)
    for tap_index in range(TAPS):
        offset = TAPS - 1 - tap_index
        short_out = short_out + short_weight[tap_index][:, None, :] * extended[
            :, offset : offset + block_rows, :
        ].astype(jnp.float32)
    left_gate, right_gate, value_stream = (short_out[0], short_out[1], short_out[2])
    driven = left_gate * value_stream
    own_width = driven.shape[1] // ctx_count
    driven_cols = lax.all_to_all(driven.T, "ctx", split_axis=0, concat_axis=1, tiled=True)
    own_out = lax.dynamic_slice_in_dim(pos_out, ctx_place * own_width, own_width, 1)
    own_decay = lax.dynamic_slice_in_dim(decay_rate, ctx_place * own_width, own_width, 0)
    positions = jnp.arange(total_len, dtype=jnp.int32).astype(jnp.float32)
    long_filter = filter_rows(
        positions, total_len, pos_in, pos_bias, sine_freq, pos_mid, own_out, own_decay
    )
    normed = long_filter / jnp.sqrt(jnp.sum(long_filter * long_filter, axis=0) + 1e-05)
    conv_cols = causal_local(driven_cols, normed.T, total_len)
    long_conv = lax.all_to_all(conv_cols, "ctx", split_axis=1, concat_axis=0, tiled=True).T
    return (right_gate * (long_conv + skip_gain[None, :] * driven)).astype(jnp.bfloat16)


def body(projected, *others):
    if lax.axis_size("ctx") == 2:
        return one_way(projected, *others)
    return exchanged(projected, *others)


def solution(mesh):
    placed = (
        P(None, ("dp", "ctx"), "chan"),
        P(None, None, "chan"),
        P(),
        P(),
        P(),
        P(),
        P(None, "chan"),
        P("chan"),
        P("chan"),
    )
    return jax.shard_map(
        body, mesh=mesh, in_specs=placed, out_specs=P(("dp", "ctx"), "chan"), check_vma=False
    )
```

profile of v0, /device:TPU:0, one launch (start us, length us, event | category | flops | bytes accessed | tf_op | source)
XLA Modules:
  0.0 21.4 jit_solution(6154180946452982076)
XLA Ops:
  0.0 1.4 %encode.2 = (bf16[656,128]{1,0:T(8,128)(2,1)S(1)}, f32[128,256]{1,0:T(8,128)S(1)}) custom-call(bf16[3,128,2048]{2,1,0:T(8,128)(2,1)} %projected_ref.7, f32[3,7,2048]{2,1,0:T(8,128)} %bitcast.6), custom_call_target="tpu_custom_call" | custom-call | flops 1000000000 | bytes 3000000 | tf_op jit(solution)/shard_map/encode/pallas_call | solution.py:547
  1.4 0.0 copy-start.12
  1.4 0.0 copy-start.9
  1.4 0.0 copy-start.10
  1.4 0.0 copy-start.11
  1.4 0.0 copy-start.13
  1.4 0.0 copy-start.3
  1.4 0.0 copy-start.5
  1.5 0.0 copy-start.6
  1.5 0.0 copy-start.7
  1.5 0.0 copy-start.8
  1.5 3.7 %collective-permute-start = (bf16[656,128]{1,0:T(8,128)(2,1)S(1)}, bf16[656,128]{1,0:T(8,128)(2,1)S(1)}, u32[]{:S(2)}, u32[]{:S(2)}) collective-permute-start(bf16[656,128]{1,0:T(8,128)(2,1)S(1)} %get-tuple-element.18), channel_id=1, source_target_pairs={{0,16},{1,17},{2,18},{3,19},{4,20},{5,21},{6,22},{7,23},{8,24},{9,... | collective-permute-start | bytes 503816 | tf_op jit(solution)/shard_map/ppermute | solution.py:568
  5.2 2.5 %encode.3 = (bf16[1296,128]{1,0:T(8,128)(2,1)S(1)}, f32[128,1280]{1,0:T(8,128)S(1)}) custom-call(bf16[3,128,2048]{2,1,0:T(8,128)(2,1)} %projected_ref.7, f32[3,7,2048]{2,1,0:T(8,128)} %bitcast.7), custom_call_target="tpu_custom_call" | custom-call | flops 1000000000 | bytes 3000000 | tf_op jit(solution)/shard_map/encode/pallas_call | solution.py:547
  7.7 1.3 %collective-permute-start.2 = (bf16[1296,128]{1,0:T(8,128)(2,1)S(1)}, bf16[1296,128]{1,0:T(8,128)(2,1)S(1)}, u32[]{:S(2)}, u32[]{:S(2)}) collective-permute-start(bf16[1296,128]{1,0:T(8,128)(2,1)S(1)} %get-tuple-element.24), channel_id=1, source_target_pairs={{0,16},{1,17},{2,18},{3,19},{4,20},{5,21},{6,22},{7,23},{8,24},{9,... | collective-permute-start | bytes 995336 | tf_op jit(solution)/shard_map/ppermute | solution.py:568
  9.0 0.1 fusion.9
  9.2 0.8 %fusion.2 = f32[256,64]{1,0:T(8,128)S(1)} fusion(f32[33,64]{1,0:T(8,128)S(1)} %copy-done.9, f32[64]{0:T(128)S(1)} %copy-done.13, f32[64]{0:T(128)S(1)} %copy-done.10, f32[256,16]{0,1:T(8,128)S(1)} %get-tuple-element.32, f32[256,16]{0,1:T(8,128)S(1)} %get-tuple-element.31, f32[256,1]{0,1:T(1,128)S(1)} %copy-done.11), kind=kOutput, calls=%fused_computation.4 | convolution fusion | flops 6537728 | bytes 108288 | tf_op jit(solution)/shard_map/dot_general | solution.py:39
  10.0 0.7 %fusion.second_ref = f32[256,64]{1,0:T(8,128)S(1)} fusion(f32[256,64]{1,0:T(8,128)S(1)} %fusion.2, f32[64,64]{1,0:T(8,128)S(1)} %copy-done, f32[64]{0:T(128)S(1)} %copy-done.10), kind=kOutput, calls=%fused_computation.1 | convolution fusion | flops 12599296 | bytes 147712 | tf_op jit(solution)/shard_map/dot_general | solution.py:45
  10.7 0.0 copy-start.1
  10.8 0.0 copy-start.2
  10.8 0.0 copy-start.4
  10.8 3.0 %filter.1 = (f32[256,2048]{1,0:T(8,128)S(1)}, f32[256,2048]{1,0:T(8,128)S(1)}) custom-call(f32[256,64]{1,0:T(8,128)S(1)} %fusion.second_ref, f32[64,2048]{1,0:T(8,128)S(1)} %copy-done.5, f32[1,2048]{1,0:T(1,128)S(1)} %bitcast.10, f32[1,2048]{1,0:T(1,128)S(1)} %bitcast.11, f32[256,128]{1,0:T(8,128)S(1)} %copy-done.8, bf16[256,192]{1,0:T(8,128)(2,1)S(1)} %copy-done.3), custom_call_target="tpu_custom_call" | custom-call | flops 3000000000 | bytes 9000000 | tf_op jit(solution)/shard_map/filter/pallas_call | solution.py:574
  13.8 2.7 %own.2 = (f32[128,512]{1,0:T(8,128)S(1)}, f32[128,512]{1,0:T(8,128)S(1)}, bf16[128,2048]{1,0:T(8,128)(2,1)}, bf16[528,128]{1,0:T(8,128)(2,1)S(1)}) custom-call(bf16[3,128,2048]{2,1,0:T(8,128)(2,1)S(1)} %copy-done.1, bf16[656,128]{1,0:T(8,128)(2,1)S(1)} %collective-permute-done.rims_ref.one_ref, f32[3,7,2048]{2,1,0:T(8,128)S(1)} %bitcast.8, ...), custom_call_target="tpu_custom_call" | custom-call | flops 2000000000 | bytes 6000000 | tf_op jit(solution)/shard_map/own/pallas_call | solution.py:591
  16.6 1.3 %collective-permute-start.1 = (bf16[528,128]{1,0:T(8,128)(2,1)S(1)}, bf16[528,128]{1,0:T(8,128)(2,1)S(1)}, u32[]{:S(2)}, u32[]{:S(2)}) collective-permute-start(bf16[528,128]{1,0:T(8,128)(2,1)S(1)} %get-tuple-element.21), channel_id=1, source_target_pairs={{0,16},{1,17},{2,18},{3,19},{4,20},{5,21},{6,22},{7,23},{8,24},{9,... | collective-permute-start | bytes 405512 | tf_op jit(solution)/shard_map/ppermute | solution.py:614
  17.9 3.4 %own.3 = (f32[128,1536]{1,0:T(8,128)S(1)}, f32[128,1536]{1,0:T(8,128)S(1)}, bf16[128,2048]{1,0:T(8,128)(2,1)}) custom-call(bf16[3,128,2048]{2,1,0:T(8,128)(2,1)S(1)} %copy-done.1, bf16[656,128]{1,0:T(8,128)(2,1)S(1)} %collective-permute-done.rims_ref.one_ref, f32[3,7,2048]{2,1,0:T(8,128)S(1)} %bitcast.9, ...), custom_call_target="tpu_custom_call", output_to_operand_aliasing={{2}: (9, {})} | custom-call | flops 2000000000 | bytes 6000000 | tf_op jit(solution)/shard_map/own/pallas_call | solution.py:591
  (21 shorter events, 0.1 us)
Async XLA Ops:
  0.0 10.0 %copy-start = (f32[64,64]{1,0:T(8,128)S(1)}, f32[64,64]{1,0:T(8,128)}, u32[]{:S(2)}) copy-start(f32[64,64]{1,0:T(8,128)} %param.18) | copy-start | bytes 49156
  1.4 7.7 %copy-start.12 = (f32[256]{0:T(256)S(1)}, f32[256]{0:T(256)}, u32[]{:S(2)}) copy-start(f32[256]{0:T(256)} %constant.15.clone) | copy-start | bytes 3076
  1.4 7.8 %copy-start.9 = (f32[33,64]{1,0:T(8,128)S(1)}, f32[33,64]{1,0:T(8,128)}, u32[]{:S(2)}) copy-start(f32[33,64]{1,0:T(8,128)} %param.15) | copy-start | bytes 25348
  1.4 7.8 %copy-start.10 = (f32[64]{0:T(128)S(1)}, f32[64]{0:T(128)}, u32[]{:S(2)}) copy-start(f32[64]{0:T(128)} %param.17) | copy-start | bytes 772
  1.4 7.8 %copy-start.11 = (f32[256,1]{0,1:T(1,128)S(1)}, f32[256,1]{0,1:T(1,128)}, u32[]{:S(2)}) copy-start(f32[256,1]{0,1:T(1,128)} %constant.20) | copy-start | bytes 3076
  1.4 7.8 %copy-start.13 = (f32[64]{0:T(128)S(1)}, f32[64]{0:T(128)}, u32[]{:S(2)}) copy-start(f32[64]{0:T(128)} %param.16) | copy-start | bytes 772
  1.4 9.3 %copy-start.3 = (bf16[256,192]{1,0:T(8,128)(2,1)S(1)}, bf16[256,192]{1,0:T(8,128)(2,1)}, u32[]{:S(2)}) copy-start(bf16[256,192]{1,0:T(8,128)(2,1)} %constant.17.clone.forward_ref) | copy-start | bytes 294916
  1.4 9.3 %copy-start.5 = (f32[64,2048]{1,0:T(8,128)S(1)}, f32[64,2048]{1,0:T(8,128)}, u32[]{:S(2)}) copy-start(f32[64,2048]{1,0:T(8,128)} %out_ref.1) | copy-start | bytes 1572868
  1.5 9.3 %copy-start.6 = (f32[2048]{0:T(1024)S(1)}, f32[2048]{0:T(1024)}, u32[]{:S(2)}) copy-start(f32[2048]{0:T(1024)} %param.20) | copy-start | bytes 24580
  1.5 9.3 %copy-start.7 = (f32[2048]{0:T(1024)S(1)}, f32[2048]{0:T(1024)}, u32[]{:S(2)}) copy-start(f32[2048]{0:T(1024)} %param.21) | copy-start | bytes 24580
  1.5 9.3 %copy-start.8 = (f32[256,128]{1,0:T(8,128)S(1)}, f32[256,128]{1,0:T(8,128)}, u32[]{:S(2)}) copy-start(f32[256,128]{1,0:T(8,128)} %constant.16.clone.places_ref) | copy-start | bytes 393220
  1.5 12.3 %collective-permute-start = (bf16[656,128]{1,0:T(8,128)(2,1)S(1)}, bf16[656,128]{1,0:T(8,128)(2,1)S(1)}, u32[]{:S(2)}, u32[]{:S(2)}) collective-permute-start(bf16[656,128]{1,0:T(8,128)(2,1)S(1)} %get-tuple-element.18), channel_id=1, source_target_pairs={{0,16},{1,17},{2,18},{3,19},{4,20},{5,21},{6,22},{7,23},{8,24},{9,... | collective-permute-start | bytes 503816 | tf_op jit(solution)/shard_map/ppermute | solution.py:568
  7.7 13.6 %collective-permute-start.2 = (bf16[1296,128]{1,0:T(8,128)(2,1)S(1)}, bf16[1296,128]{1,0:T(8,128)(2,1)S(1)}, u32[]{:S(2)}, u32[]{:S(2)}) collective-permute-start(bf16[1296,128]{1,0:T(8,128)(2,1)S(1)} %get-tuple-element.24), channel_id=1, source_target_pairs={{0,16},{1,17},{2,18},{3,19},{4,20},{5,21},{6,22},{7,23},{8,24},{9,... | collective-permute-start | bytes 995336 | tf_op jit(solution)/shard_map/ppermute | solution.py:568
  10.7 3.1 %copy-start.1 = (bf16[3,128,2048]{2,1,0:T(8,128)(2,1)S(1)}, bf16[3,128,2048]{2,1,0:T(8,128)(2,1)}, u32[]{:S(2)}) copy-start(bf16[3,128,2048]{2,1,0:T(8,128)(2,1)} %projected_ref.7) | copy-start | bytes 4718596
  10.8 3.1 %copy-start.2 = (f32[7,3,2048]{2,0,1:T(8,128)S(1)}, f32[7,3,2048]{2,0,1:T(8,128)}, u32[]{:S(2)}) copy-start(f32[7,3,2048]{2,0,1:T(8,128)} %param.14) | copy-start | bytes 516100
  10.8 3.1 %copy-start.4 = (bf16[128,384]{1,0:T(8,128)(2,1)S(1)}, bf16[128,384]{1,0:T(8,128)(2,1)}, u32[]{:S(2)}) copy-start(bf16[128,384]{1,0:T(8,128)(2,1)} %constant.18.clone.backward_ref) | copy-start | bytes 294916
  16.6 4.8 %collective-permute-start.1 = (bf16[528,128]{1,0:T(8,128)(2,1)S(1)}, bf16[528,128]{1,0:T(8,128)(2,1)S(1)}, u32[]{:S(2)}, u32[]{:S(2)}) collective-permute-start(bf16[528,128]{1,0:T(8,128)(2,1)S(1)} %get-tuple-element.21), channel_id=1, source_target_pairs={{0,16},{1,17},{2,18},{3,19},{4,20},{5,21},{6,22},{7,23},{8,24},{9,... | collective-permute-start | bytes 405512 | tf_op jit(solution)/shard_map/ppermute | solution.py:614
where the time goes:
time: 21.6 us; the launch traced here: 21.4 us
  Pallas kernels  13.1 us (61%)
  starting transfers between devices  6.28 us (29%)
  matrix products  1.45 us (7%)
  between operations  0.33 us (2%)
    pallas_call x2, Pallas kernels, own(): pl.pallas_call(functools.partial(own_kernel, first, send), in_specs=[in_v...  6.14 us
    ppermute x2, starting transfers between devices, one_way(): coded.append(lax.ppermute(code, 'ctx', pairs))  4.98 us
    pallas_call x2, Pallas kernels, one_way(): pl.pallas_call(functools.partial(encode_kernel, sum(ahead[:at])), in_spec...  3.87 us
    pallas_call x1, Pallas kernels, one_way(): pl.pallas_call(filter_kernel, in_specs=[in_vmem] * 6, out_specs=[in_vmem]...  3.01 us
    ppermute x1, starting transfers between devices, one_way(): last_code = lax.ppermute(code, 'ctx', pairs)  1.3 us
    dot_general x1, matrix products, second_rows(): jnp.dot(inputs, pos_in, precision=HIGHEST, preferred_element_type=jnp.flo...  0.78 us
    dot_general x1, matrix products, second_rows(): jnp.dot(first_layer, pos_mid, precision=HIGHEST, preferred_element_type=j...  0.66 us
  transfers between devices with their start and end apart: 3, of which 0 were waited for; matrix products, arithmetic and copies ran while one was open for 7% of the time, Pallas kernels for 55%

commit v1 on v0

--- a/solution.py
+++ b/solution.py
@@ -58,6 +58,15 @@
     high = x.astype(jnp.bfloat16)
     low = (x - high.astype(jnp.float32)).astype(jnp.bfloat16)
     return high, low
+
+
+def feature_table(places, total_len):
+    bands = np.arange(1, BANDS + 1, dtype=np.float32)
+    angles = places[:, None] * bands[None, :] * np.float32(2.0 * math.pi / total_len)
+    first = places[:, None] / np.float32(total_len)
+    table = np.concatenate([first, np.cos(angles), np.sin(angles), np.ones_like(first)], axis=1)
+    spare = np.zeros((places.shape[0], -table.shape[1] % 8))
+    return np.concatenate([table, spare], axis=1).astype(np.float32).T.copy()
 
 
 def parity_order(rows):
@@ -219,85 +228,170 @@
     return decode
 
 
-def encode_kernel(
-    first, projected_ref, taps_ref, coded_ref, driven_ref, rows_buf, rim_buf, taps_buf, strided_buf, peak_buf,
-    levels_buf, sems,
+def second_layer(feats_ref, in_ref, bias_ref, freq_ref, mid_ref, scaled_buf):
+    dot = functools.partial(
+        lax.dot_general,
+        dimension_numbers=(((0,), (0,)), ((), ())),
+        precision=HIGHEST,
+        preferred_element_type=jnp.float32,
+    )
+    count = in_ref.shape[0]
+    freq = freq_ref[...]
+    scaled_buf[...] = jnp.zeros_like(scaled_buf)
+    scaled_buf[0:count] = in_ref[...] * freq
+    scaled_buf[count : count + 1] = bias_ref[...] * freq
+    layer = jnp.sin(dot(scaled_buf[...], feats_ref[...]))
+    return jnp.sin(dot(mid_ref[...] * freq, layer)).T
+
+
+def encode_tiles(tiles, rows, streams, taps_ref, taps_first, coded_ref, driven_ref, strided_buf, peak_buf, levels_buf):
+    def drive(tile, number):
+        cols = tile_lanes(tile)
+        sums = [
+            short_sum(
+                strided_rows(streams(way, tile), strided_buf.at[number, way]),
+                None, taps_ref, 2 * way, tile_lanes(tile, taps_first),
+            )
+            for way in range(2)
+        ]
+        driven = [one * two for one, two in zip(*sums)]
+        for row, value in enumerate(parity_rows(driven)):
+            driven_ref[16 * row : 16 * row + 16, cols] = value
+        peak_buf[:, cols] = functools.reduce(jnp.maximum, [jnp.abs(value) for value in driven])
+
+    each_tile(tiles, strided_buf.shape[0], drive)
+    code_tiles(tiles, rows, coded_ref, driven_ref, peak_buf, levels_buf)
+
+
+def code_tiles(tiles, rows, coded_ref, values_ref, peak_buf, levels_buf):
+    each_tile(tiles, 4, lambda tile, _: place_level(peak_buf[:, tile_lanes(tile)], tile, peak_buf, levels_buf))
+    coded_ref[tiles * rows : tiles * rows + 16] = levels_buf[...].astype(jnp.bfloat16)
+
+    def code(tile, _):
+        cols = tile_lanes(tile)
+        gain = peak_buf[:, cols]
+        gain = jnp.concatenate([gain, gain], axis=0)
+        for row in range(0, rows, 16):
+            put_coded(coded_ref, tile, row, values_ref[row : row + 16, cols], gain)
+
+    each_tile(tiles, 4, code)
+
+
+def first_kernel(
+    projected_ref, taps_ref, feats_ref, in_ref, bias_ref, freq_ref, mid_ref, coded_ref, driven_ref, second_ref,
+    rows_buf, rim_buf, taps_buf, strided_buf, peak_buf, levels_buf, feats_buf, in_buf, bias_buf, freq_buf, mid_buf,
+    scaled_buf, sems, layer_sems,
 ):
     rows, size = rows_buf.shape[1:]
     tiles = size // 128
-    span = pl.ds(first, size)
-    with_rims = coded_ref.shape[0] > tiles * rows + 16
 
     @pl.when(lax.axis_index("ctx") == 0)
     def _():
+        span = pl.ds(0, size)
         copies = [
             pltpu.make_async_copy(taps_ref.at[:, :, span], taps_buf, sems.at[0]),
             pltpu.make_async_copy(projected_ref.at[0, :, span], rows_buf.at[0], sems.at[1]),
             pltpu.make_async_copy(projected_ref.at[2, :, span], rows_buf.at[1], sems.at[2]),
+            pltpu.make_async_copy(projected_ref.at[:, pl.ds(rows - 16, 16)], rim_buf, sems.at[3]),
         ]
-        if with_rims:
-            copies.append(pltpu.make_async_copy(projected_ref.at[:, pl.ds(rows - 16, 16)], rim_buf, sems.at[3]))
-        for copy in copies:
+        layer_bufs = (feats_buf, in_buf, bias_buf, freq_buf, mid_buf)
+        layer_copies = [
+            pltpu.make_async_copy(ref, buf, layer_sems.at[at])
+            for at, (ref, buf) in enumerate(zip((feats_ref, in_ref, bias_ref, freq_ref, mid_ref), layer_bufs))
+        ]
+        for copy in layer_copies + copies:
             copy.start()
+        for copy in layer_copies:
+            copy.wait()
+        second_ref[...] = second_layer(*layer_bufs, scaled_buf)
         for copy in copies:
             copy.wait()
-
-        def drive(tile, number):
-            cols = tile_lanes(tile)
-            sums = [
-                short_sum(
-                    strided_rows(rows_buf[way, :, cols], strided_buf.at[number, way]), None, taps_buf, 2 * way, cols
-                )
-                for way in range(2)
-            ]
-            driven = [one * two for one, two in zip(*sums)]
-            for row, value in enumerate(parity_rows(driven)):
-                driven_ref[16 * row : 16 * row + 16, cols] = value
-            peak_buf[:, cols] = functools.reduce(jnp.maximum, [jnp.abs(value) for value in driven])
-
-        each_tile(tiles, strided_buf.shape[0], drive)
-        each_tile(
-            tiles, 4, lambda tile, _: place_level(peak_buf[:, tile_lanes(tile)], tile, peak_buf, levels_buf)
+        encode_tiles(
+            tiles, rows, lambda way, tile: rows_buf[way, :, tile_lanes(tile)], taps_buf, 0, coded_ref, driven_ref,
+            strided_buf, peak_buf, levels_buf,
         )
-        coded_ref[tiles * rows : tiles * rows + 16] = levels_buf[...].astype(jnp.bfloat16)
-
-        def code(tile, _):
-            cols = tile_lanes(tile)
-            gain = peak_buf[:, cols]
-            gain = jnp.concatenate([gain, gain], axis=0)
-            for row in range(0, rows, 16):
-                put_coded(coded_ref, tile, row, driven_ref[row : row + 16, cols], gain)
-
-        each_tile(tiles, 4, code)
-        if with_rims:
-
-            def rims(pair, _):
-                for at in range(3):
-                    values = [
-                        rim_buf[at, :, tile_lanes(2 * pair + way)].astype(jnp.float32)[8:] for way in range(2)
-                    ]
-                    there = pl.ds(pl.multiple_of(tiles * rows + 16 + pair * 48 + at * 16, 16), 16)
-                    coded_ref[there, :] = jnp.concatenate(values, axis=0).astype(jnp.bfloat16)
-
-            each_tile(rim_buf.shape[2] // 256, 4, rims)
-
-
-def filter_kernel(
-    second_ref, out_ref, decay_ref, skip_ref, places_ref, forward_ref, near_ref, far_ref, raw_buf, parts_buf, spec_buf,
-    scale_buf,
+
+        for at in range(3):
+            for group in range(rim_buf.shape[2] // 1024):
+                there = tiles * rows + 16 + (3 * group + at) * 48
+                values = [
+                    rim_buf[at, :, (8 * group + way) * 128 : (8 * group + way + 1) * 128].astype(jnp.float32)[8:]
+                    for way in range(8)
+                ]
+                values = pack_rims(values)
+                for pair in range(3):
+                    both = jnp.concatenate(values[2 * pair : 2 * pair + 2], axis=0)
+                    coded_ref[there + 16 * pair : there + 16 * pair + 16] = both.astype(jnp.bfloat16)
+
+
+def pack_rims(values):
+    top = lax.broadcasted_iota(jnp.int32, (8, 128), 0) < 2
+    return [
+        jnp.where(top, pltpu.roll(values[6 + at // 3], 6 - 2 * (at % 3), 0), values[at]) for at in range(6)
+    ]
+
+
+def unpack_rims(values):
+    place = lax.broadcasted_iota(jnp.int32, (8, 128), 0)
+    rest = []
+    for at in range(2):
+        turned = [pltpu.roll(values[3 * at + way], 2 + 2 * way, 0) for way in range(3)]
+        rest.append(jnp.where(place < 4, turned[0], jnp.where(place < 6, turned[1], turned[2])))
+    return values + rest
+
+
+def read_rims(coded_ref, rims_buf):
+    groups = rims_buf.shape[2] // 1024
+    start = coded_ref.shape[0] - groups * 144
+    for at in range(3):
+        for group in range(groups):
+            there = start + (3 * group + at) * 48
+            packed = coded_ref[there : there + 48].astype(jnp.float32)
+            values = unpack_rims([packed[8 * way : 8 * way + 8] for way in range(6)])
+            for way, value in enumerate(values):
+                rims_buf[at, :, (8 * group + way) * 128 : (8 * group + way + 1) * 128] = value
+
+
+def encode_kernel(
+    first, projected_ref, taps_ref, coded_ref, driven_ref, strided_buf, peak_buf, levels_buf
 ):
+    rows, size = driven_ref.shape
+
+    @pl.when(lax.axis_index("ctx") == 0)
+    def _():
+        encode_tiles(
+            size // 128, rows, lambda way, tile: projected_ref[2 * way, :, tile_lanes(tile, first)], taps_ref, first,
+            coded_ref, driven_ref, strided_buf, peak_buf, levels_buf,
+        )
+
+
+def filter_kernel(first, fresh, out_ref, decay_ref, skip_ref, places_ref, forward_ref, *refs):
+    if fresh:
+        *layer_refs, second_ref, near_ref, far_ref, halves_ref, raw_buf, parts_buf, spec_buf, scale_buf, second_buf, scaled_buf = refs
+        place = lax.axis_index("ctx")
+
+        @pl.when(place == 0)
+        def _():
+            second_buf[...] = second_ref[...]
+
+        @pl.when(place != 0)
+        def _():
+            second_buf[...] = second_layer(*layer_refs, scaled_buf)
+
+        second_high, second_low = halves(second_buf[...])
+        halves_ref[...] = jnp.concatenate([second_high, second_high, second_low], axis=1)
+    else:
+        halves_ref, near_ref, far_ref, raw_buf, parts_buf, spec_buf, scale_buf = refs
     rows, width = near_ref.shape[0] // 2, near_ref.shape[1]
     half = rows // 2
-    second_high, second_low = halves(second_ref[...])
-    second = jnp.concatenate([second_high, second_high, second_low], axis=1)
-    out_high, out_low = halves(out_ref[...])
+    out_high, out_low = halves(out_ref[:, first : first + width])
     raw_buf[...] = jnp.dot(
-        second, jnp.concatenate([out_high, out_low, out_high], axis=0), preferred_element_type=jnp.float32
+        halves_ref[...], jnp.concatenate([out_high, out_low, out_high], axis=0), preferred_element_type=jnp.float32
     )
 
     def decay(tile, _):
         cols = tile_lanes(tile)
-        fall = -decay_ref[:, cols]
+        fall = -decay_ref[:, tile_lanes(tile, first)]
         total = jnp.zeros((8, 128), jnp.float32)
         for row in range(0, 2 * rows, 16):
             taps = raw_buf[row : row + 16, cols] * jnp.exp(fall * places_ref[row : row + 16])
@@ -315,7 +409,7 @@
         cols = tile_lanes(tile)
         scale = scale_buf[:, cols]
         scale = jnp.concatenate([scale, scale], axis=0)
-        skip = skip_ref[:, cols]
+        skip = skip_ref[:, tile_lanes(tile, first)]
         for row in range(0, half, 16):
             low = [value * scale for value in unfolded(spec_buf, row, cols)]
             high = [value * scale for value in unfolded(spec_buf, row, tile_lanes(tile, width))]
@@ -337,24 +431,19 @@
     else:
         *driven_refs, _, base_ref, right_ref, mixed_ref = refs[:6]
         bufs = refs[6:]
-    strided_buf, parts_buf, spec_buf, bins_buf, mixed_buf, sems = bufs[:6]
+    rims_buf, strided_buf, parts_buf, spec_buf, bins_buf, mixed_buf, sems = bufs[:7]
     rows, width = base_ref.shape
     half = rows // 2
     tiles = width // 128
-    first_tile = first // 128
-    rims_at = rims_ref.shape[0] - projected_ref.shape[2] // 128 * 24
+    read_rims(rims_ref, rims_buf)
     place = lax.axis_index("ctx")
 
     def sums_of(tile, number, ats):
         cols = tile_lanes(tile, first)
-        far_tile = tile + first_tile
         sums = []
         for at in ats:
-            pair = pl.ds(pl.multiple_of(rims_at + far_tile // 2 * 48 + at * 16, 16), 16)
-            rim = rims_ref[pair, :].astype(jnp.float32)
-            rim = jnp.where(far_tile % 2 == 0, rim[:8], rim[8:])
             parts = strided_rows(projected_ref[at, :, cols], strided_buf.at[number, at])
-            sums.append(short_sum(parts, rim, taps_ref, at, cols))
+            sums.append(short_sum(parts, rims_buf[at, :, cols], taps_ref, at, cols))
         return sums
 
     def put_right(tile, values):
@@ -392,50 +481,56 @@
 
     forward_dots(forward_ref, parts_buf, spec_buf)
     if send:
-        conv_buf, peak_buf, levels_buf = bufs[6:]
+        conv_buf, peak_buf, levels_buf = bufs[7:]
 
         @pl.when(place == 0)
         def _():
             each_tile(
                 tiles, 4,
-                lambda tile, _: filtered(spec_buf, far_ref, bins_buf, tile_lanes(tile), tile_lanes(tile, first)),
+                lambda tile, _: filtered(spec_buf, far_ref, bins_buf, tile_lanes(tile), tile_lanes(tile)),
             )
             backward_dots(backward_ref, bins_buf, conv_buf)
 
             def peaks(tile, _):
                 cols = tile_lanes(tile)
-                peak = functools.reduce(
+                peak_buf[:, cols] = functools.reduce(
                     jnp.maximum, [jnp.abs(conv_buf[row : row + 8, cols]) for row in range(0, rows, 8)]
                 )
-                place_level(peak, tile, peak_buf, levels_buf)
 
             each_tile(tiles, 4, peaks)
-            coded_ref[tiles * rows : tiles * rows + 16] = levels_buf[...].astype(jnp.bfloat16)
-
-            def code(tile, _):
-                cols = tile_lanes(tile)
-                gain = peak_buf[:, cols]
-                gain = jnp.concatenate([gain, gain], axis=0)
-                for row in range(0, rows, 16):
-                    put_coded(coded_ref, tile, row, conv_buf[row : row + 16, cols], gain)
-
-            each_tile(tiles, 4, code)
+            code_tiles(tiles, rows, coded_ref, conv_buf, peak_buf, levels_buf)
 
     each_tile(
-        tiles, 4, lambda tile, _: filtered(spec_buf, near_ref, bins_buf, tile_lanes(tile), tile_lanes(tile, first))
+        tiles, 4, lambda tile, _: filtered(spec_buf, near_ref, bins_buf, tile_lanes(tile), tile_lanes(tile))
     )
     backward_dots(backward_ref, bins_buf, base_ref)
 
     @pl.when(place == 0)
     def _():
-        def mix(tile, number):
+        def mix(tile):
             cols = tile_lanes(tile)
-            values = [right_ref[at : at + 16, cols] * base_ref[at : at + 16, cols] for at in range(0, rows, 16)]
-            mixed_buf[:, cols] = natural_rows(values, strided_buf.at[number, 0]).astype(jnp.bfloat16)
-
-        each_tile(tiles, strided_buf.shape[0], mix)
-        copy = pltpu.make_async_copy(mixed_buf, mixed_ref.at[:, pl.ds(first, width)], sems.at[0])
+            return [right_ref[at : at + 16, cols] * base_ref[at : at + 16, cols] for at in range(0, rows, 16)]
+
+        mix_out(mix, tiles, first, mixed_ref, mixed_buf, strided_buf.at[:, 0], sems)
+
+
+def mix_out(mix, tiles, first, mixed_ref, buf, strided_buf, sems):
+    parts = sems.shape[0]
+    copies = []
+    for part in range(parts):
+        start, count = part * (tiles // parts), tiles // parts
+
+        def one(tile, number, start=start):
+            buf[:, tile_lanes(start + tile)] = natural_rows(mix(start + tile), strided_buf.at[number]).astype(jnp.bfloat16)
+
+        each_tile(count, strided_buf.shape[0], one)
+        span = slice(start * 128, (start + count) * 128)
+        copy = pltpu.make_async_copy(
+            buf.at[:, span], mixed_ref.at[:, pl.ds(first + start * 128, count * 128)], sems.at[part]
+        )
         copy.start()
+        copies.append(copy)
+    for copy in copies:
         copy.wait()
 
 
@@ -444,47 +539,38 @@
 
 
 def join_kernel(
-    one_ref, two_ref, far_ref, base_ref, right_ref, forward_ref, backward_ref, sofar_ref, mixed_ref,
+    first, coded_ref, far_ref, base_ref, right_ref, forward_ref, backward_ref, sofar_ref, mixed_ref,
     parts_buf, spec_buf, bins_buf, conv_buf, strided_buf, buf, levels_buf, sems,
 ):
-    rows, width = base_ref.shape
+    rows, width = conv_buf.shape
     half = rows // 2
     tiles = width // 128
-    later = (two_ref.shape[0] - 16) // rows
-    counts = [tiles - later, later]
 
     @pl.when(lax.axis_index("ctx") != 0)
     def _():
-        start = 0
-        for at, ref in enumerate((one_ref, two_ref)):
-            read_levels(ref, levels_buf.at[at], counts[at], rows)
-
-            def spread_out(tile, _, ref=ref, at=at, start=start):
-                decode = decoder(levels_buf.at[at], tile)
-                for row in range(0, rows, 16):
-                    value = decode(ref[tile_rows(tile, row), :])
-                    put_halves(parts_buf, row // half, row % half, tile_lanes(tile, start), value)
-
-            each_tile(counts[at], 4, spread_out)
-            start += counts[at] * 128
+        read_levels(coded_ref, levels_buf, tiles, rows)
+
+        def spread_out(tile, _):
+            decode = decoder(levels_buf, tile)
+            for row in range(0, rows, 16):
+                value = decode(coded_ref[tile_rows(tile, row), :])
+                put_halves(parts_buf, row // half, row % half, tile_lanes(tile), value)
+
+        each_tile(tiles, 4, spread_out)
         forward_dots(forward_ref, parts_buf, spec_buf)
         each_tile(
-            tiles, 4, lambda tile, _: filtered(spec_buf, far_ref, bins_buf, tile_lanes(tile), tile_lanes(tile))
+            tiles, 4, lambda tile, _: filtered(spec_buf, far_ref, bins_buf, tile_lanes(tile), tile_lanes(tile, first))
         )
         backward_dots(backward_ref, bins_buf, conv_buf)
 
-        def mix(tile, number):
-            cols = tile_lanes(tile)
-            values = [
-                right_ref[at : at + 16, cols] * (conv_buf[at : at + 16, cols] + base_ref[at : at + 16, cols])
+        def mix(tile):
+            cols = tile_lanes(tile, first)
+            return [
+                right_ref[at : at + 16, cols] * (conv_buf[at : at + 16, tile_lanes(tile)] + base_ref[at : at + 16, cols])
                 for at in range(0, rows, 16)
             ]
-            buf[:, cols] = natural_rows(values, strided_buf.at[number]).astype(jnp.bfloat16)
-
-        each_tile(tiles, strided_buf.shape[0], mix)
-        copy = pltpu.make_async_copy(buf, mixed_ref.at[:, pl.ds(0, width)], sems.at[0])
-        copy.start()
-        copy.wait()
+
+        mix_out(mix, tiles, first, mixed_ref, buf, strided_buf, sems)
 
 
 def last_kernel(
@@ -497,19 +583,15 @@
     def _():
         read_levels(coded_ref, levels_buf, tiles, rows)
 
-        def mix(tile, number):
+        def mix(tile):
             cols = tile_lanes(tile)
             decode = decoder(levels_buf, tile)
-            values = [
+            return [
                 right_ref[at : at + 16, cols] * (decode(coded_ref[tile_rows(tile, at), :]) + base_ref[at : at + 16, cols])
                 for at in range(0, rows, 16)
             ]
-            buf[:, cols] = natural_rows(values, strided_buf.at[number]).astype(jnp.bfloat16)
-
-        each_tile(tiles, strided_buf.shape[0], mix)
-        copy = pltpu.make_async_copy(buf, mixed_ref.at[:, pl.ds(first, width)], sems.at[0])
-        copy.start()
-        copy.wait()
+
+        mix_out(mix, tiles, first, mixed_ref, buf, strided_buf, sems)
 
 
 def params(mib=40):
@@ -542,52 +624,63 @@
     def message(size, more=0):
         return arrays((size // 128 * rows + 16 + more, 128), dtype=jnp.bfloat16)
 
-    coded, driven = [], []
-    for at, size in enumerate(ahead):
-        code, signal = pl.pallas_call(
-            functools.partial(encode_kernel, sum(ahead[:at])),
-            in_specs=[in_hbm, in_hbm],
-            out_specs=[in_vmem] * 2,
-            out_shape=message(size, width // 128 * 24 if at == 0 else 0) + arrays((rows, size)),
-            scratch_shapes=[
-                shorts((2, rows, size)),
-                shorts((3, 16, width)),
-                floats((3, TAPS, size)),
-                floats((2, 2, rows, 128)),
-                floats((8, size)),
-                floats((16, 128)),
-                pltpu.SemaphoreType.DMA((4,)),
-            ],
-            compiler_params=params(),
-            cost_estimate=cost(1),
-            name="encode",
-        )(
-            pltpu.with_memory_space_constraint(projected, pltpu.HBM),
-            pltpu.with_memory_space_constraint(taps, pltpu.HBM),
-        )
-        coded.append(lax.ppermute(code, "ctx", pairs))
-        driven.append(signal)
-
     order = parity_order(rows)
     places = np.concatenate([order, order + rows]).astype(np.float32)
-    second = second_rows(jnp.asarray(places), total_len, pos_in, pos_bias, sine_freq, pos_mid)
-    near, far = pl.pallas_call(
-        filter_kernel,
-        in_specs=[in_vmem] * 6,
+    feats = feature_table(places, total_len)
+    places = np.repeat(places[:, None], 128, 1)
+    layers = (feats, pos_in, pos_bias[None, :], sine_freq[None, :], pos_mid)
+    tile_bufs = [floats((2, 2, rows, 128)), floats((8, width)), floats((16, 128))]
+    one, two = ahead
+    one_code, one_driven, second = pl.pallas_call(
+        first_kernel,
+        in_specs=[in_hbm] * 7,
+        out_specs=[in_vmem] * 3,
+        out_shape=message(one, width // 128 * 18) + arrays((rows, one), (total_len, pos_mid.shape[1])),
+        scratch_shapes=[shorts((2, rows, one)), shorts((3, 16, width)), floats((3, TAPS, one))]
+        + tile_bufs
+        + [floats(array.shape) for array in layers]
+        + [floats((feats.shape[0], pos_in.shape[1]))]
+        + [pltpu.SemaphoreType.DMA((4,)), pltpu.SemaphoreType.DMA((5,))],
+        compiler_params=params(),
+        cost_estimate=cost(1),
+        name="first",
+    )(*[pltpu.with_memory_space_constraint(jnp.asarray(array), pltpu.HBM) for array in (projected, taps, *layers)])
+    one_code = lax.ppermute(one_code, "ctx", pairs)
+    two_code, two_driven = pl.pallas_call(
+        functools.partial(encode_kernel, one),
+        in_specs=[in_vmem] * 2,
         out_specs=[in_vmem] * 2,
-        out_shape=arrays((total_len, width), (total_len, width)),
-        scratch_shapes=[
-            floats((total_len, width)),
-            shorts((2, rows, 2 * width)),
-            floats((2, rows, 2 * width)),
-            floats((8, width)),
-        ],
+        out_shape=message(two) + arrays((rows, two)),
+        scratch_shapes=tile_bufs,
         compiler_params=params(),
-        cost_estimate=cost(3),
-        name="filter",
-    )(second, pos_out, decay_rate[None, :], skip_gain[None, :], jnp.asarray(np.repeat(places[:, None], 128, 1)), forward)
-
-    def own(first, size, send, *more):
+        cost_estimate=cost(1),
+        name="encode",
+    )(projected, taps)
+    two_code = lax.ppermute(two_code, "ctx", pairs)
+
+    def spectra(first, size, *more):
+        fresh = len(more) > 1
+        return pl.pallas_call(
+            functools.partial(filter_kernel, first, fresh),
+            in_specs=[in_vmem] * (5 + len(more)),
+            out_specs=[in_vmem] * (2 + fresh),
+            out_shape=arrays((total_len, size), (total_len, size))
+            + arrays((total_len, 3 * pos_mid.shape[1]), dtype=jnp.bfloat16) * fresh,
+            scratch_shapes=[
+                floats((total_len, size)),
+                shorts((2, rows, 2 * size)),
+                floats((2, rows, 2 * size)),
+                floats((8, size)),
+            ]
+            + [floats((total_len, pos_mid.shape[1])), floats((feats.shape[0], pos_in.shape[1]))] * fresh,
+            compiler_params=params(),
+            cost_estimate=cost(2),
+            name="filter",
+        )(pos_out, decay_rate[None, :], skip_gain[None, :], places, forward, *more)
+
+    last_near, last_far, second_halves = spectra(middle, behind, *layers, second)
+
+    def own(first, size, send, near, far, *more):
         return pl.pallas_call(
             functools.partial(own_kernel, first, send),
             in_specs=[in_vmem] * 7 + [in_vmem, in_vmem, in_hbm][: len(more)],
@@ -597,42 +690,45 @@
             + message(size) * send,
             input_output_aliases={} if send else {9: 2},
             scratch_shapes=[
+                floats((3, 8, width)),
                 floats((2, 3, rows, 128)),
                 shorts((2, rows, size)),
                 floats((2, rows, size)),
                 shorts((2, 2 * rows, size)),
                 shorts((rows, size)),
-                pltpu.SemaphoreType.DMA((1,)),
+                pltpu.SemaphoreType.DMA((2,)),
             ]
             + [floats((rows, size)), floats((8, size)), floats((16, 128))] * send,
             compiler_params=params(),
             cost_estimate=cost(2),
             name="own",
-        )(projected, coded[0], taps, near, far, forward, backward, *more)
-
-    last_base, last_right, mixed, code = own(middle, behind, True)
+        )(projected, one_code, taps, near, far, forward, backward, *more)
+
+    last_base, last_right, mixed, code = own(middle, behind, True, last_near, last_far)
     last_code = lax.ppermute(code, "ctx", pairs)
-    base, right, mixed = own(0, middle, False, *driven, mixed)
-    mixed = pl.pallas_call(
-        join_kernel,
-        in_specs=[in_vmem] * 7 + [in_hbm],
-        out_specs=in_hbm,
-        out_shape=jax.ShapeDtypeStruct((rows, width), jnp.bfloat16),
-        input_output_aliases={7: 0},
-        scratch_shapes=[
-            shorts((2, rows, middle)),
-            floats((2, rows, middle)),
-            shorts((2, 2 * rows, middle)),
-            floats((rows, middle)),
-            floats((4, rows, 128)),
-            shorts((rows, middle)),
-            floats((2, 16, 128)),
-            pltpu.SemaphoreType.DMA((1,)),
-        ],
-        compiler_params=params(),
-        cost_estimate=cost(2),
-        name="join",
-    )(*coded, far, base, right, forward, backward, mixed)
+    near, far = spectra(0, middle, second_halves)
+    base, right, mixed = own(0, middle, False, near, far, one_driven, two_driven, mixed)
+    for first, size, code in ((0, one, one_code), (one, two, two_code)):
+        mixed = pl.pallas_call(
+            functools.partial(join_kernel, first),
+            in_specs=[in_vmem] * 6 + [in_hbm],
+            out_specs=in_hbm,
+            out_shape=jax.ShapeDtypeStruct((rows, width), jnp.bfloat16),
+            input_output_aliases={6: 0},
+            scratch_shapes=[
+                shorts((2, rows, size)),
+                floats((2, rows, size)),
+                shorts((2, 2 * rows, size)),
+                floats((rows, size)),
+                floats((4, rows, 128)),
+                shorts((rows, size)),
+                floats((16, 128)),
+                pltpu.SemaphoreType.DMA((2,)),
+            ],
+            compiler_params=params(),
+            cost_estimate=cost(1),
+            name="join",
+        )(code, far, base, right, forward, backward, mixed)
     return pl.pallas_call(
         functools.partial(last_kernel, middle),
         in_specs=[in_vmem] * 3 + [in_hbm],
@@ -643,7 +739,7 @@
             floats((4, rows, 128)),
             shorts((rows, behind)),
             floats((16, 128)),
-            pltpu.SemaphoreType.DMA((1,)),
+            pltpu.SemaphoreType.DMA((2,)),
         ],
         compiler_params=params(),
         cost_estimate=cost(1),

time: 21.6 us -> 19.4 us (0.90)
  the two profiles are of different devices: /device:TPU:0 before, /device:TPU:6 now
where the time goes in v1:
time: 19.4 us; the launch traced here: 19.2 us
  Pallas kernels  13.5 us (70%)
  starting transfers between devices  4.01 us (21%)
  waiting for transfers between devices  1.38 us (7%)
  between operations  0.28 us (1%)
    pallas_call x2, Pallas kernels, own(): pl.pallas_call(functools.partial(own_kernel, first, send), in_specs=[in_v...  4.67 us
    pallas_call x2, Pallas kernels, spectra(): pl.pallas_call(functools.partial(filter_kernel, first, fresh), in_specs=[...  3.96 us
    pallas_call x2, Pallas kernels, one_way(): pl.pallas_call(functools.partial(join_kernel, first), in_specs=[in_vmem]...  3.92 us
    ppermute x1, starting transfers between devices, one_way(): one_code = lax.ppermute(one_code, 'ctx', pairs)  1.42 us
    ppermute x1, waiting for transfers between devices, one_way(): one_code = lax.ppermute(one_code, 'ctx', pairs)  1.36 us
    ppermute x1, starting transfers between devices, one_way(): last_code = lax.ppermute(code, 'ctx', pairs)  1.29 us
    ppermute x1, starting transfers between devices, one_way(): two_code = lax.ppermute(two_code, 'ctx', pairs)  1.29 us
    pallas_call x1, Pallas kernels, one_way(): pl.pallas_call(functools.partial(last_kernel, middle), in_specs=[in_vmem]...  0.83 us
  transfers between devices with their start and end apart: 3, of which 1 were waited for; matrix products, arithmetic and copies ran while one was open for 0% of the time, Pallas kernels for 65%

profile of v1, /device:TPU:6, one launch (start us, length us, event | category | flops | bytes accessed | tf_op | source)
XLA Modules:
  0.0 19.2 jit_solution(3400499488177287377)
XLA Ops:
  0.0 0.1 first.1
  0.1 0.0 copy-start
  0.1 0.0 copy-start.3
  0.1 0.0 copy-start.5
  0.1 0.0 copy-start.6
  0.1 0.0 copy-start.7
  0.2 0.0 copy-start.8
  0.2 0.0 copy-start.9
  0.2 0.0 copy-start.10
  0.2 0.0 copy-start.11
  0.2 0.0 copy-start.12
  0.2 1.4 %collective-permute-start = (bf16[560,128]{1,0:T(8,128)(2,1)S(1)}, bf16[560,128]{1,0:T(8,128)(2,1)S(1)}, u32[]{:S(2)}, u32[]{:S(2)}) collective-permute-start(bf16[560,128]{1,0:T(8,128)(2,1)S(1)} %get-tuple-element.22), channel_id=1, source_target_pairs={{0,16},{1,17},{2,18},{3,19},{4,20},{5,21},{6,22},{7,23},{8,24},{9,... | collective-permute-start | bytes 430088 | tf_op jit(solution)/shard_map/ppermute | solution.py:648
  1.7 1.3 %collective-permute-start.2 = (bf16[1296,128]{1,0:T(8,128)(2,1)S(1)}, bf16[1296,128]{1,0:T(8,128)(2,1)S(1)}, u32[]{:S(2)}, u32[]{:S(2)}) collective-permute-start(bf16[1296,128]{1,0:T(8,128)(2,1)S(1)} %get-tuple-element.29), channel_id=1, source_target_pairs={{0,16},{1,17},{2,18},{3,19},{4,20},{5,21},{6,22},{7,23},{8,24},{9,... | collective-permute-start | bytes 995336 | tf_op jit(solution)/shard_map/ppermute | solution.py:659
  3.1 1.7 %filter.2 = (f32[256,512]{1,0:T(8,128)S(1)}, f32[256,512]{1,0:T(8,128)S(1)}, bf16[256,192]{1,0:T(8,128)(2,1)S(1)}) custom-call(f32[64,2048]{1,0:T(8,128)S(1)} %copy-done.3, f32[1,2048]{1,0:T(1,128)S(1)} %bitcast.9, f32[1,2048]{1,0:T(1,128)S(1)} %bitcast.11, f32[256,128]{1,0:T(8,128)S(1)} %copy-done.11, bf16[256,192]{1,0:T(8,128)(2,1)S(1)} %copy-done, ...), custom_call_target="tpu_custom_call" | custom-call | flops 2000000000 | bytes 6000000 | tf_op jit(solution)/shard_map/filter/pallas_call | solution.py:663
  4.8 0.0 copy-start.1
  4.8 2.2 %filter.3 = (f32[256,1536]{1,0:T(8,128)S(1)}, f32[256,1536]{1,0:T(8,128)S(1)}) custom-call(f32[64,2048]{1,0:T(8,128)S(1)} %copy-done.3, f32[1,2048]{1,0:T(1,128)S(1)} %bitcast.10, f32[1,2048]{1,0:T(1,128)S(1)} %bitcast.12, f32[256,128]{1,0:T(8,128)S(1)} %copy-done.11, bf16[256,192]{1,0:T(8,128)(2,1)S(1)} %copy-done, ...), custom_call_target="tpu_custom_call" | custom-call | flops 2000000000 | bytes 6000000 | tf_op jit(solution)/shard_map/filter/pallas_call | solution.py:663
  7.1 1.4 %collective-permute-done.rims_ref.coded_ref = bf16[560,128]{1,0:T(8,128)(2,1)S(1)} collective-permute-done((bf16[560,128]{1,0:T(8,128)(2,1)S(1)}, bf16[560,128]{1,0:T(8,128)(2,1)S(1)}, u32[]{:S(2)}, u32[]{:S(2)}) %collective-permute-start) | collective-permute-done | bytes 143392 | tf_op jit(solution)/shard_map/ppermute | solution.py:648
  8.4 1.3 %own.2 = (f32[128,512]{1,0:T(8,128)S(1)}, f32[128,512]{1,0:T(8,128)S(1)}, bf16[128,2048]{1,0:T(8,128)(2,1)}, bf16[528,128]{1,0:T(8,128)(2,1)S(1)}) custom-call(bf16[3,128,2048]{2,1,0:T(8,128)(2,1)S(1)} %copy-done.2, bf16[560,128]{1,0:T(8,128)(2,1)S(1)} %collective-permute-done.rims_ref.coded_ref, f32[3,7,2048]{2,1,0:T(8,128)S(1)} %bitcast.7, ...), custom_call_target="tpu_custom_call" | custom-call | flops 2000000000 | bytes 6000000 | tf_op jit(solution)/shard_map/own/pallas_call | solution.py:684
  9.8 1.3 %collective-permute-start.1 = (bf16[528,128]{1,0:T(8,128)(2,1)S(1)}, bf16[528,128]{1,0:T(8,128)(2,1)S(1)}, u32[]{:S(2)}, u32[]{:S(2)}) collective-permute-start(bf16[528,128]{1,0:T(8,128)(2,1)S(1)} %get-tuple-element.26), channel_id=1, source_target_pairs={{0,16},{1,17},{2,18},{3,19},{4,20},{5,21},{6,22},{7,23},{8,24},{9,... | collective-permute-start | bytes 405512 | tf_op jit(solution)/shard_map/ppermute | solution.py:708
  11.1 3.3 %own.3 = (f32[128,1536]{1,0:T(8,128)S(1)}, f32[128,1536]{1,0:T(8,128)S(1)}, bf16[128,2048]{1,0:T(8,128)(2,1)}) custom-call(bf16[3,128,2048]{2,1,0:T(8,128)(2,1)S(1)} %copy-done.2, bf16[560,128]{1,0:T(8,128)(2,1)S(1)} %collective-permute-done.rims_ref.coded_ref, f32[3,7,2048]{2,1,0:T(8,128)S(1)} %bitcast.8, ...), custom_call_target="tpu_custom_call", output_to_operand_aliasing={{2}: (9, {})} | custom-call | flops 2000000000 | bytes 6000000 | tf_op jit(solution)/shard_map/own/pallas_call | solution.py:684
  14.4 1.2 %join.2.sofar_ref = bf16[128,2048]{1,0:T(8,128)(2,1)} custom-call(bf16[560,128]{1,0:T(8,128)(2,1)S(1)} %collective-permute-done.rims_ref.coded_ref, f32[256,1536]{1,0:T(8,128)S(1)} %get-tuple-element.31.far_ref, f32[128,1536]{1,0:T(8,128)S(1)} %get-tuple-element.36.base_ref, ...), custom_call_target="tpu_custom_call", output_to_operand_aliasing={{}: (6, {})} | custom-call | flops 1000000000 | bytes 3000000 | tf_op jit(solution)/shard_map/join/pallas_call | solution.py:712
  15.6 0.0 collective-permute-done.2.coded_ref
  15.7 2.7 %join.3.sofar_ref = bf16[128,2048]{1,0:T(8,128)(2,1)} custom-call(bf16[1296,128]{1,0:T(8,128)(2,1)S(1)} %collective-permute-done.2.coded_ref, f32[256,1536]{1,0:T(8,128)S(1)} %get-tuple-element.31.far_ref, f32[128,1536]{1,0:T(8,128)S(1)} %get-tuple-element.36.base_ref, f32[128,1536]{1,0:T(8,128)S(1)} %get-tuple-element.37.right_ref, ...), custom_call_target="tpu_custom_call", output_to_operand_aliasing={{}: (6, {})} | custom-call | flops 1000000000 | bytes 3000000 | tf_op jit(solution)/shard_map/join/pallas_call | solution.py:712
  18.4 0.8 %last.1 = bf16[128,2048]{1,0:T(8,128)(2,1)} custom-call(bf16[528,128]{1,0:T(8,128)(2,1)S(1)} %collective-permute-done.1.coded_ref, f32[128,512]{1,0:T(8,128)S(1)} %get-tuple-element.27.base_ref, f32[128,512]{1,0:T(8,128)S(1)} %get-tuple-element.28.right_ref, bf16[128,2048]{1,0:T(8,128)(2,1)} %join.3.sofar_ref), custom_call_target="tpu_custom_call", output_to_operand_aliasing={{}: (3, {})} | custom-call | flops 1000000000 | bytes 3000000 | tf_op jit(solution)/shard_map/last/pallas_call | solution.py:732
  (17 shorter events, 0.0 us)
Async XLA Ops:
  0.0 1.6 %copy-start.2 = (bf16[3,128,2048]{2,1,0:T(8,128)(2,1)S(1)}, bf16[3,128,2048]{2,1,0:T(8,128)(2,1)}, u32[]{:S(2)}) copy-start(bf16[3,128,2048]{2,1,0:T(8,128)(2,1)} %projected_ref.7) | copy-start | bytes 4718596
  0.0 1.7 %copy-start.4 = (f32[7,3,2048]{2,0,1:T(8,128)S(1)}, f32[7,3,2048]{2,0,1:T(8,128)}, u32[]{:S(2)}) copy-start(f32[7,3,2048]{2,0,1:T(8,128)} %param.14) | copy-start | bytes 516100
  0.1 2.9 %copy-start = (bf16[256,192]{1,0:T(8,128)(2,1)S(1)}, bf16[256,192]{1,0:T(8,128)(2,1)}, u32[]{:S(2)}) copy-start(bf16[256,192]{1,0:T(8,128)(2,1)} %constant.10.clone.forward_ref) | copy-start | bytes 294916
  0.1 2.9 %copy-start.3 = (f32[64,2048]{1,0:T(8,128)S(1)}, f32[64,2048]{1,0:T(8,128)}, u32[]{:S(2)}) copy-start(f32[64,2048]{1,0:T(8,128)} %out_ref.3) | copy-start | bytes 1572868
  0.1 2.9 %copy-start.5 = (f32[64,64]{1,0:T(8,128)S(1)}, f32[64,64]{1,0:T(8,128)}, u32[]{:S(2)}) copy-start(f32[64,64]{1,0:T(8,128)} %refs_4_.1) | copy-start | bytes 49156
  0.1 2.9 %copy-start.6 = (f32[33,64]{1,0:T(8,128)S(1)}, f32[33,64]{1,0:T(8,128)}, u32[]{:S(2)}) copy-start(f32[33,64]{1,0:T(8,128)} %refs_1_.1) | copy-start | bytes 25348
  0.1 2.9 %copy-start.7 = (f32[2048]{0:T(1024)S(1)}, f32[2048]{0:T(1024)}, u32[]{:S(2)}) copy-start(f32[2048]{0:T(1024)} %param.20) | copy-start | bytes 24580
  0.2 2.9 %copy-start.8 = (f32[2048]{0:T(1024)S(1)}, f32[2048]{0:T(1024)}, u32[]{:S(2)}) copy-start(f32[2048]{0:T(1024)} %param.21) | copy-start | bytes 24580
  0.2 2.9 %copy-start.9 = (f32[64]{0:T(128)S(1)}, f32[64]{0:T(128)}, u32[]{:S(2)}) copy-start(f32[64]{0:T(128)} %param.16) | copy-start | bytes 772
  0.2 2.9 %copy-start.10 = (f32[64]{0:T(128)S(1)}, f32[64]{0:T(128)}, u32[]{:S(2)}) copy-start(f32[64]{0:T(128)} %param.17) | copy-start | bytes 772
  0.2 2.9 %copy-start.11 = (f32[256,128]{1,0:T(8,128)S(1)}, f32[256,128]{1,0:T(8,128)}, u32[]{:S(2)}) copy-start(f32[256,128]{1,0:T(8,128)} %constant.9.clone.places_ref) | copy-start | bytes 393220
  0.2 2.9 %copy-start.12 = (f32[40,256]{1,0:T(8,128)S(1)}, f32[40,256]{1,0:T(8,128)}, u32[]{:S(2)}) copy-start(f32[40,256]{1,0:T(8,128)} %constant.8.clone.feats_ref.refs_0_) | copy-start | bytes 122884
  0.2 8.2 %collective-permute-start = (bf16[560,128]{1,0:T(8,128)(2,1)S(1)}, bf16[560,128]{1,0:T(8,128)(2,1)S(1)}, u32[]{:S(2)}, u32[]{:S(2)}) collective-permute-start(bf16[560,128]{1,0:T(8,128)(2,1)S(1)} %get-tuple-element.22), channel_id=1, source_target_pairs={{0,16},{1,17},{2,18},{3,19},{4,20},{5,21},{6,22},{7,23},{8,24},{9,... | collective-permute-start | bytes 430088 | tf_op jit(solution)/shard_map/ppermute | solution.py:648
  1.7 14.0 %collective-permute-start.2 = (bf16[1296,128]{1,0:T(8,128)(2,1)S(1)}, bf16[1296,128]{1,0:T(8,128)(2,1)S(1)}, u32[]{:S(2)}, u32[]{:S(2)}) collective-permute-start(bf16[1296,128]{1,0:T(8,128)(2,1)S(1)} %get-tuple-element.29), channel_id=1, source_target_pairs={{0,16},{1,17},{2,18},{3,19},{4,20},{5,21},{6,22},{7,23},{8,24},{9,... | collective-permute-start | bytes 995336 | tf_op jit(solution)/shard_map/ppermute | solution.py:659
  4.8 3.6 %copy-start.1 = (bf16[128,384]{1,0:T(8,128)(2,1)S(1)}, bf16[128,384]{1,0:T(8,128)(2,1)}, u32[]{:S(2)}) copy-start(bf16[128,384]{1,0:T(8,128)(2,1)} %constant.11.clone.backward_ref) | copy-start | bytes 294916
  9.8 8.6 %collective-permute-start.1 = (bf16[528,128]{1,0:T(8,128)(2,1)S(1)}, bf16[528,128]{1,0:T(8,128)(2,1)S(1)}, u32[]{:S(2)}, u32[]{:S(2)}) collective-permute-start(bf16[528,128]{1,0:T(8,128)(2,1)S(1)} %get-tuple-element.26), channel_id=1, source_target_pairs={{0,16},{1,17},{2,18},{3,19},{4,20},{5,21},{6,22},{7,23},{8,24},{9,... | collective-permute-start | bytes 405512 | tf_op jit(solution)/shard_map/ppermute | solution.py:708

commit v2 on v1

--- a/solution.py
+++ b/solution.py
@@ -278,9 +278,7 @@
 
 
 def first_kernel(
-    projected_ref, taps_ref, feats_ref, in_ref, bias_ref, freq_ref, mid_ref, coded_ref, driven_ref, second_ref,
-    rows_buf, rim_buf, taps_buf, strided_buf, peak_buf, levels_buf, feats_buf, in_buf, bias_buf, freq_buf, mid_buf,
-    scaled_buf, sems, layer_sems,
+    projected_ref, taps_ref, coded_ref, driven_ref, rows_buf, rim_buf, taps_buf, strided_buf, peak_buf, levels_buf, sems
 ):
     rows, size = rows_buf.shape[1:]
     tiles = size // 128
@@ -294,16 +292,8 @@
             pltpu.make_async_copy(projected_ref.at[2, :, span], rows_buf.at[1], sems.at[2]),
             pltpu.make_async_copy(projected_ref.at[:, pl.ds(rows - 16, 16)], rim_buf, sems.at[3]),
         ]
-        layer_bufs = (feats_buf, in_buf, bias_buf, freq_buf, mid_buf)
-        layer_copies = [
-            pltpu.make_async_copy(ref, buf, layer_sems.at[at])
-            for at, (ref, buf) in enumerate(zip((feats_ref, in_ref, bias_ref, freq_ref, mid_ref), layer_bufs))
-        ]
-        for copy in layer_copies + copies:
+        for copy in copies:
             copy.start()
-        for copy in layer_copies:
-            copy.wait()
-        second_ref[...] = second_layer(*layer_bufs, scaled_buf)
         for copy in copies:
             copy.wait()
         encode_tiles(
@@ -349,6 +339,7 @@
             packed = coded_ref[there : there + 48].astype(jnp.float32)
             values = unpack_rims([packed[8 * way : 8 * way + 8] for way in range(6)])
             for way, value in enumerate(values):
+                value = jnp.where(lax.axis_index("ctx") == 0, 0.0, value)
                 rims_buf[at, :, (8 * group + way) * 128 : (8 * group + way + 1) * 128] = value
 
 
@@ -367,18 +358,8 @@
 
 def filter_kernel(first, fresh, out_ref, decay_ref, skip_ref, places_ref, forward_ref, *refs):
     if fresh:
-        *layer_refs, second_ref, near_ref, far_ref, halves_ref, raw_buf, parts_buf, spec_buf, scale_buf, second_buf, scaled_buf = refs
-        place = lax.axis_index("ctx")
-
-        @pl.when(place == 0)
-        def _():
-            second_buf[...] = second_ref[...]
-
-        @pl.when(place != 0)
-        def _():
-            second_buf[...] = second_layer(*layer_refs, scaled_buf)
-
-        second_high, second_low = halves(second_buf[...])
+        *layer_refs, near_ref, far_ref, halves_ref, raw_buf, parts_buf, spec_buf, scale_buf, scaled_buf = refs
+        second_high, second_low = halves(second_layer(*layer_refs, scaled_buf))
         halves_ref[...] = jnp.concatenate([second_high, second_high, second_low], axis=1)
     else:
         halves_ref, near_ref, far_ref, raw_buf, parts_buf, spec_buf, scale_buf = refs
@@ -539,7 +520,7 @@
 
 
 def join_kernel(
-    first, coded_ref, far_ref, base_ref, right_ref, forward_ref, backward_ref, sofar_ref, mixed_ref,
+    coded_refs, far_ref, base_ref, right_ref, forward_ref, backward_ref, mixed_ref,
     parts_buf, spec_buf, bins_buf, conv_buf, strided_buf, buf, levels_buf, sems,
 ):
     rows, width = conv_buf.shape
@@ -548,29 +529,33 @@
 
     @pl.when(lax.axis_index("ctx") != 0)
     def _():
-        read_levels(coded_ref, levels_buf, tiles, rows)
-
-        def spread_out(tile, _):
-            decode = decoder(levels_buf, tile)
-            for row in range(0, rows, 16):
-                value = decode(coded_ref[tile_rows(tile, row), :])
-                put_halves(parts_buf, row // half, row % half, tile_lanes(tile), value)
-
-        each_tile(tiles, 4, spread_out)
+        counts = [coded_refs[0].shape[0] // rows, coded_refs[1].shape[0] // rows]
+        counts[0] = tiles - counts[1]
+        for at, ref in enumerate(coded_refs):
+            start = counts[0] * 128 * at
+            read_levels(ref, levels_buf.at[at], counts[at], rows)
+
+            def spread_out(tile, _, ref=ref, at=at, start=start):
+                decode = decoder(levels_buf.at[at], tile)
+                for row in range(0, rows, 16):
+                    value = decode(ref[tile_rows(tile, row), :])
+                    put_halves(parts_buf, row // half, row % half, tile_lanes(tile, start), value)
+
+            each_tile(counts[at], 4, spread_out)
         forward_dots(forward_ref, parts_buf, spec_buf)
         each_tile(
-            tiles, 4, lambda tile, _: filtered(spec_buf, far_ref, bins_buf, tile_lanes(tile), tile_lanes(tile, first))
+            tiles, 4, lambda tile, _: filtered(spec_buf, far_ref, bins_buf, tile_lanes(tile), tile_lanes(tile))
         )
         backward_dots(backward_ref, bins_buf, conv_buf)
 
         def mix(tile):
-            cols = tile_lanes(tile, first)
+            cols = tile_lanes(tile)
             return [
-                right_ref[at : at + 16, cols] * (conv_buf[at : at + 16, tile_lanes(tile)] + base_ref[at : at + 16, cols])
+                right_ref[at : at + 16, cols] * (conv_buf[at : at + 16, cols] + base_ref[at : at + 16, cols])
                 for at in range(0, rows, 16)
             ]
 
-        mix_out(mix, tiles, first, mixed_ref, buf, strided_buf, sems)
+        mix_out(mix, tiles, 0, mixed_ref, buf, strided_buf, sems)
 
 
 def last_kernel(
@@ -631,21 +616,19 @@
     layers = (feats, pos_in, pos_bias[None, :], sine_freq[None, :], pos_mid)
     tile_bufs = [floats((2, 2, rows, 128)), floats((8, width)), floats((16, 128))]
     one, two = ahead
-    one_code, one_driven, second = pl.pallas_call(
+    one_code, one_driven = pl.pallas_call(
         first_kernel,
-        in_specs=[in_hbm] * 7,
-        out_specs=[in_vmem] * 3,
-        out_shape=message(one, width // 128 * 18) + arrays((rows, one), (total_len, pos_mid.shape[1])),
+        in_specs=[in_hbm] * 2,
+        out_specs=[in_vmem] * 2,
+        out_shape=message(one, width // 128 * 18) + arrays((rows, one)),
         scratch_shapes=[shorts((2, rows, one)), shorts((3, 16, width)), floats((3, TAPS, one))]
         + tile_bufs
-        + [floats(array.shape) for array in layers]
-        + [floats((feats.shape[0], pos_in.shape[1]))]
-        + [pltpu.SemaphoreType.DMA((4,)), pltpu.SemaphoreType.DMA((5,))],
+        + [pltpu.SemaphoreType.DMA((4,))],
         compiler_params=params(),
         cost_estimate=cost(1),
         name="first",
-    )(*[pltpu.with_memory_space_constraint(jnp.asarray(array), pltpu.HBM) for array in (projected, taps, *layers)])
-    one_code = lax.ppermute(one_code, "ctx", pairs)
+    )(*[pltpu.with_memory_space_constraint(array, pltpu.HBM) for array in (projected, taps)])
+    one_code = lax.ppermute(one_code, "ctx", [(0, 1), (1, 0)])
     two_code, two_driven = pl.pallas_call(
         functools.partial(encode_kernel, one),
         in_specs=[in_vmem] * 2,
@@ -656,7 +639,7 @@
         cost_estimate=cost(1),
         name="encode",
     )(projected, taps)
-    two_code = lax.ppermute(two_code, "ctx", pairs)
+    two_code = lax.ppermute(two_code, "ctx", [(0, 1), (1, 0)])
 
     def spectra(first, size, *more):
         fresh = len(more) > 1
@@ -672,13 +655,13 @@
                 floats((2, rows, 2 * size)),
                 floats((8, size)),
             ]
-            + [floats((total_len, pos_mid.shape[1])), floats((feats.shape[0], pos_in.shape[1]))] * fresh,
+            + [floats((feats.shape[0], pos_in.shape[1]))] * fresh,
             compiler_params=params(),
             cost_estimate=cost(2),
             name="filter",
         )(pos_out, decay_rate[None, :], skip_gain[None, :], places, forward, *more)
 
-    last_near, last_far, second_halves = spectra(middle, behind, *layers, second)
+    last_near, last_far, second_halves = spectra(middle, behind, *layers)
 
     def own(first, size, send, near, far, *more):
         return pl.pallas_call(
@@ -708,27 +691,26 @@
     last_code = lax.ppermute(code, "ctx", pairs)
     near, far = spectra(0, middle, second_halves)
     base, right, mixed = own(0, middle, False, near, far, one_driven, two_driven, mixed)
-    for first, size, code in ((0, one, one_code), (one, two, two_code)):
-        mixed = pl.pallas_call(
-            functools.partial(join_kernel, first),
-            in_specs=[in_vmem] * 6 + [in_hbm],
-            out_specs=in_hbm,
-            out_shape=jax.ShapeDtypeStruct((rows, width), jnp.bfloat16),
-            input_output_aliases={6: 0},
-            scratch_shapes=[
-                shorts((2, rows, size)),
-                floats((2, rows, size)),
-                shorts((2, 2 * rows, size)),
-                floats((rows, size)),
-                floats((4, rows, 128)),
-                shorts((rows, size)),
-                floats((16, 128)),
-                pltpu.SemaphoreType.DMA((2,)),
-            ],
-            compiler_params=params(),
-            cost_estimate=cost(1),
-            name="join",
-        )(code, far, base, right, forward, backward, mixed)
+    mixed = pl.pallas_call(
+        lambda one_ref, two_ref, *refs: join_kernel((one_ref, two_ref), *refs[:5], *refs[6:]),
+        in_specs=[in_vmem] * 7 + [in_hbm],
+        out_specs=in_hbm,
+        out_shape=jax.ShapeDtypeStruct((rows, width), jnp.bfloat16),
+        input_output_aliases={7: 0},
+        scratch_shapes=[
+            shorts((2, rows, middle)),
+            floats((2, rows, middle)),
+            shorts((2, 2 * rows, middle)),
+            floats((rows, middle)),
+            floats((4, rows, 128)),
+            shorts((rows, middle)),
+            floats((2, 16, 128)),
+            pltpu.SemaphoreType.DMA((3,)),
+        ],
+        compiler_params=params(),
+        cost_estimate=cost(2),
+        name="join",
+    )(one_code, two_code, far, base, right, forward, backward, mixed)
     return pl.pallas_call(
         functools.partial(last_kernel, middle),
         in_specs=[in_vmem] * 3 + [in_hbm],

time: 19.4 us -> 17.7 us (0.912)
  waiting for transfers between devices: 1.38 us -> 0.01 us
  Pallas kernels: 13.5 us -> 12.3 us
  starting transfers between devices: 4.01 us -> 4.89 us
    ppermute x2, waiting for transfers between devices: 1.37 us -> 0.01 us  [the longest x1 0.01 us: one_way(): one_code = lax.ppermute(one_code, 'ctx', [(0, 1), (1, 0)])]
    pallas_call x3 -> x2, Pallas kernels: 4 us -> 2.9 us  [the longest x1 2.87 us: one_way(): pl.pallas_call(lambda one_ref, two_ref, *refs: join_kernel((one_ref, two_...]
    ppermute x2, starting transfers between devices: 2.72 us -> 3.59 us  [the longest x1 2 us: one_way(): one_code = lax.ppermute(one_code, 'ctx', [(0, 1), (1, 0)])]
  transfers between devices with their start and end apart: 3 -> 3, of which waited for: 1 -> 0; matrix products, arithmetic and copies ran while one was open for 0% -> 0% of each run, Pallas kernels for 65% -> 66%
where the time goes in v2:
time: 17.7 us; the launch traced here: 17.5 us
  Pallas kernels  12.3 us (69%)
  starting transfers between devices  4.89 us (28%)
  between operations  0.23 us (1%)
    pallas_call x2, Pallas kernels, own(): pl.pallas_call(functools.partial(own_kernel, first, send), in_specs=[in_v...  4.69 us
    pallas_call x2, Pallas kernels, spectra(): pl.pallas_call(functools.partial(filter_kernel, first, fresh), in_specs=[...  3.91 us
    pallas_call x1, Pallas kernels, one_way(): pl.pallas_call(lambda one_ref, two_ref, *refs: join_kernel((one_ref, two_...  2.87 us
    ppermute x1, starting transfers between devices, one_way(): one_code = lax.ppermute(one_code, 'ctx', [(0, 1), (1, 0)])  2 us
    ppermute x1, starting transfers between devices, one_way(): two_code = lax.ppermute(two_code, 'ctx', [(0, 1), (1, 0)])  1.6 us
    ppermute x1, starting transfers between devices, one_way(): last_code = lax.ppermute(code, 'ctx', pairs)  1.29 us
    pallas_call x1, Pallas kernels, one_way(): pl.pallas_call(functools.partial(last_kernel, middle), in_specs=[in_vmem]...  0.83 us
  transfers between devices with their start and end apart: 3, of which 0 were waited for; matrix products, arithmetic and copies ran while one was open for 0% of the time, Pallas kernels for 66%

profile of v2, /device:TPU:6, one launch (start us, length us, event | category | flops | bytes accessed | tf_op | source)
XLA Modules:
  0.0 17.5 jit_solution(5791427800075479455)
XLA Ops:
  0.0 0.0 copy-start.1
  0.1 0.0 copy-start.3
  0.1 0.0 copy-start.4
  0.1 0.0 copy-start.5
  0.1 0.0 copy-start.6
  0.1 0.0 copy-start.7
  0.1 0.0 copy-start.8
  0.1 0.0 copy-start.9
  0.1 0.0 copy-start.10
  0.2 0.0 copy-start.12
  0.2 2.0 %collective-permute-start = (bf16[560,128]{1,0:T(8,128)(2,1)S(1)}, bf16[560,128]{1,0:T(8,128)(2,1)S(1)}, u32[]{:S(2)}, u32[]{:S(2)}) collective-permute-start(bf16[560,128]{1,0:T(8,128)(2,1)S(1)} %get-tuple-element.21), channel_id=1, source_target_pairs={{0,16},{16,0},{1,17},{17,1},{2,18},{18,2},{3,19},{19,3},{4,20},{20... | collective-permute-start | bytes 430088 | tf_op jit(solution)/shard_map/ppermute | solution.py:631
  2.2 1.6 %collective-permute-start.2 = (bf16[1296,128]{1,0:T(8,128)(2,1)S(1)}, bf16[1296,128]{1,0:T(8,128)(2,1)S(1)}, u32[]{:S(2)}, u32[]{:S(2)}) collective-permute-start(bf16[1296,128]{1,0:T(8,128)(2,1)S(1)} %get-tuple-element.27), channel_id=1, source_target_pairs={{0,16},{16,0},{1,17},{17,1},{2,18},{18,2},{3,19},{19,3},{4,20},{20... | collective-permute-start | bytes 995336 | tf_op jit(solution)/shard_map/ppermute | solution.py:642
  3.8 0.0 copy-done.4
  3.8 1.6 %filter.2 = (f32[256,512]{1,0:T(8,128)S(1)}, f32[256,512]{1,0:T(8,128)S(1)}, bf16[256,192]{1,0:T(8,128)(2,1)S(1)}) custom-call(f32[64,2048]{1,0:T(8,128)S(1)} %copy-done.1, f32[1,2048]{1,0:T(1,128)S(1)} %bitcast.9, f32[1,2048]{1,0:T(1,128)S(1)} %bitcast.11, f32[256,128]{1,0:T(8,128)S(1)} %copy-done.10, bf16[256,192]{1,0:T(8,128)(2,1)S(1)} %copy-done.9, ...), custom_call_target="tpu_custom_call" | custom-call | flops 2000000000 | bytes 6000000 | tf_op jit(solution)/shard_map/filter/pallas_call | solution.py:646
  5.5 0.0 copy-start.11
  5.5 2.3 %filter.3 = (f32[256,1536]{1,0:T(8,128)S(1)}, f32[256,1536]{1,0:T(8,128)S(1)}) custom-call(f32[64,2048]{1,0:T(8,128)S(1)} %copy-done.1, f32[1,2048]{1,0:T(1,128)S(1)} %bitcast.10, f32[1,2048]{1,0:T(1,128)S(1)} %bitcast.12, f32[256,128]{1,0:T(8,128)S(1)} %copy-done.10, bf16[256,192]{1,0:T(8,128)(2,1)S(1)} %copy-done.9, ...), custom_call_target="tpu_custom_call" | custom-call | flops 2000000000 | bytes 6000000 | tf_op jit(solution)/shard_map/filter/pallas_call | solution.py:646
  7.8 0.0 collective-permute-done.rims_ref.one_ref
  7.8 1.3 %own.2 = (f32[128,512]{1,0:T(8,128)S(1)}, f32[128,512]{1,0:T(8,128)S(1)}, bf16[128,2048]{1,0:T(8,128)(2,1)}, bf16[528,128]{1,0:T(8,128)(2,1)S(1)}) custom-call(bf16[3,128,2048]{2,1,0:T(8,128)(2,1)S(1)} %copy-done, bf16[560,128]{1,0:T(8,128)(2,1)S(1)} %collective-permute-done.rims_ref.one_ref, f32[3,7,2048]{2,1,0:T(8,128)S(1)} %bitcast.7, ...), custom_call_target="tpu_custom_call" | custom-call | flops 2000000000 | bytes 6000000 | tf_op jit(solution)/shard_map/own/pallas_call | solution.py:667
  9.1 1.3 %collective-permute-start.1 = (bf16[528,128]{1,0:T(8,128)(2,1)S(1)}, bf16[528,128]{1,0:T(8,128)(2,1)S(1)}, u32[]{:S(2)}, u32[]{:S(2)}) collective-permute-start(bf16[528,128]{1,0:T(8,128)(2,1)S(1)} %get-tuple-element.24), channel_id=1, source_target_pairs={{0,16},{1,17},{2,18},{3,19},{4,20},{5,21},{6,22},{7,23},{8,24},{9,... | collective-permute-start | bytes 405512 | tf_op jit(solution)/shard_map/ppermute | solution.py:691
  10.4 3.4 %own.3 = (f32[128,1536]{1,0:T(8,128)S(1)}, f32[128,1536]{1,0:T(8,128)S(1)}, bf16[128,2048]{1,0:T(8,128)(2,1)}) custom-call(bf16[3,128,2048]{2,1,0:T(8,128)(2,1)S(1)} %copy-done, bf16[560,128]{1,0:T(8,128)(2,1)S(1)} %collective-permute-done.rims_ref.one_ref, f32[3,7,2048]{2,1,0:T(8,128)S(1)} %bitcast.8, ...), custom_call_target="tpu_custom_call", output_to_operand_aliasing={{2}: (9, {})} | custom-call | flops 2000000000 | bytes 6000000 | tf_op jit(solution)/shard_map/own/pallas_call | solution.py:667
  13.8 0.0 collective-permute-done.2.two_ref
  13.8 2.9 %join.1.sofar_ref = bf16[128,2048]{1,0:T(8,128)(2,1)} custom-call(bf16[560,128]{1,0:T(8,128)(2,1)S(1)} %collective-permute-done.rims_ref.one_ref, bf16[1296,128]{1,0:T(8,128)(2,1)S(1)} %collective-permute-done.2.two_ref, f32[256,1536]{1,0:T(8,128)S(1)} %get-tuple-element.29.far_ref.refs_0_, ...), custom_call_target="tpu_custom_call", output_to_operand_aliasing={{}: (7, {})} | custom-call | flops 2000000000 | bytes 6000000 | tf_op jit(solution)/shard_map/join/pallas_call | solution.py:694
  16.7 0.0 collective-permute-done.1.coded_ref
  16.7 0.8 %last.1 = bf16[128,2048]{1,0:T(8,128)(2,1)} custom-call(bf16[528,128]{1,0:T(8,128)(2,1)S(1)} %collective-permute-done.1.coded_ref, f32[128,512]{1,0:T(8,128)S(1)} %get-tuple-element.25.base_ref, f32[128,512]{1,0:T(8,128)S(1)} %get-tuple-element.26.right_ref, bf16[128,2048]{1,0:T(8,128)(2,1)} %join.1.sofar_ref), custom_call_target="tpu_custom_call", output_to_operand_aliasing={{}: (3, {})} | custom-call | flops 1000000000 | bytes 3000000 | tf_op jit(solution)/shard_map/last/pallas_call | solution.py:714
  (16 shorter events, 0.1 us)
Async XLA Ops:
  0.0 2.2 %copy-start = (bf16[3,128,2048]{2,1,0:T(8,128)(2,1)S(1)}, bf16[3,128,2048]{2,1,0:T(8,128)(2,1)}, u32[]{:S(2)}) copy-start(bf16[3,128,2048]{2,1,0:T(8,128)(2,1)} %projected_ref.7) | copy-start | bytes 4718596
  0.0 2.2 %copy-start.2 = (f32[7,3,2048]{2,0,1:T(8,128)S(1)}, f32[7,3,2048]{2,0,1:T(8,128)}, u32[]{:S(2)}) copy-start(f32[7,3,2048]{2,0,1:T(8,128)} %param.14) | copy-start | bytes 516100
  0.0 3.7 %copy-start.1 = (f32[64,2048]{1,0:T(8,128)S(1)}, f32[64,2048]{1,0:T(8,128)}, u32[]{:S(2)}) copy-start(f32[64,2048]{1,0:T(8,128)} %out_ref.3) | copy-start | bytes 1572868
  0.1 3.7 %copy-start.3 = (f32[64,64]{1,0:T(8,128)S(1)}, f32[64,64]{1,0:T(8,128)}, u32[]{:S(2)}) copy-start(f32[64,64]{1,0:T(8,128)} %refs_4_.2) | copy-start | bytes 49156
  0.1 3.7 %copy-start.4 = (f32[33,64]{1,0:T(8,128)S(1)}, f32[33,64]{1,0:T(8,128)}, u32[]{:S(2)}) copy-start(f32[33,64]{1,0:T(8,128)} %refs_1_.1) | copy-start | bytes 25348
  0.1 3.7 %copy-start.5 = (f32[2048]{0:T(1024)S(1)}, f32[2048]{0:T(1024)}, u32[]{:S(2)}) copy-start(f32[2048]{0:T(1024)} %param.20) | copy-start | bytes 24580
  0.1 3.7 %copy-start.6 = (f32[2048]{0:T(1024)S(1)}, f32[2048]{0:T(1024)}, u32[]{:S(2)}) copy-start(f32[2048]{0:T(1024)} %param.21) | copy-start | bytes 24580
  0.1 3.7 %copy-start.7 = (f32[64]{0:T(128)S(1)}, f32[64]{0:T(128)}, u32[]{:S(2)}) copy-start(f32[64]{0:T(128)} %param.16) | copy-start | bytes 772
  0.1 3.7 %copy-start.8 = (f32[64]{0:T(128)S(1)}, f32[64]{0:T(128)}, u32[]{:S(2)}) copy-start(f32[64]{0:T(128)} %param.17) | copy-start | bytes 772
  0.1 3.7 %copy-start.9 = (bf16[256,192]{1,0:T(8,128)(2,1)S(1)}, bf16[256,192]{1,0:T(8,128)(2,1)}, u32[]{:S(2)}) copy-start(bf16[256,192]{1,0:T(8,128)(2,1)} %constant.9.clone.forward_ref.refs_3_) | copy-start | bytes 294916
  0.1 3.7 %copy-start.10 = (f32[256,128]{1,0:T(8,128)S(1)}, f32[256,128]{1,0:T(8,128)}, u32[]{:S(2)}) copy-start(f32[256,128]{1,0:T(8,128)} %constant.8.clone.places_ref) | copy-start | bytes 393220
  0.2 3.7 %copy-start.12 = (f32[40,256]{1,0:T(8,128)S(1)}, f32[40,256]{1,0:T(8,128)}, u32[]{:S(2)}) copy-start(f32[40,256]{1,0:T(8,128)} %constant.10.clone.refs_0_) | copy-start | bytes 122884
  0.2 7.6 %collective-permute-start = (bf16[560,128]{1,0:T(8,128)(2,1)S(1)}, bf16[560,128]{1,0:T(8,128)(2,1)S(1)}, u32[]{:S(2)}, u32[]{:S(2)}) collective-permute-start(bf16[560,128]{1,0:T(8,128)(2,1)S(1)} %get-tuple-element.21), channel_id=1, source_target_pairs={{0,16},{16,0},{1,17},{17,1},{2,18},{18,2},{3,19},{19,3},{4,20},{20... | collective-permute-start | bytes 430088 | tf_op jit(solution)/shard_map/ppermute | solution.py:631
  2.2 11.6 %collective-permute-start.2 = (bf16[1296,128]{1,0:T(8,128)(2,1)S(1)}, bf16[1296,128]{1,0:T(8,128)(2,1)S(1)}, u32[]{:S(2)}, u32[]{:S(2)}) collective-permute-start(bf16[1296,128]{1,0:T(8,128)(2,1)S(1)} %get-tuple-element.27), channel_id=1, source_target_pairs={{0,16},{16,0},{1,17},{17,1},{2,18},{18,2},{3,19},{19,3},{4,20},{20... | collective-permute-start | bytes 995336 | tf_op jit(solution)/shard_map/ppermute | solution.py:642
  5.5 2.3 %copy-start.11 = (bf16[128,384]{1,0:T(8,128)(2,1)S(1)}, bf16[128,384]{1,0:T(8,128)(2,1)}, u32[]{:S(2)}) copy-start(bf16[128,384]{1,0:T(8,128)(2,1)} %constant.11.clone.backward_ref.refs_4_) | copy-start | bytes 294916
  9.1 7.6 %collective-permute-start.1 = (bf16[528,128]{1,0:T(8,128)(2,1)S(1)}, bf16[528,128]{1,0:T(8,128)(2,1)S(1)}, u32[]{:S(2)}, u32[]{:S(2)}) collective-permute-start(bf16[528,128]{1,0:T(8,128)(2,1)S(1)} %get-tuple-element.24), channel_id=1, source_target_pairs={{0,16},{1,17},{2,18},{3,19},{4,20},{5,21},{6,22},{7,23},{8,24},{9,... | collective-permute-start | bytes 405512 | tf_op jit(solution)/shard_map/ppermute | solution.py:691

commit v3 on v2

--- a/solution.py
+++ b/solution.py
@@ -143,18 +143,25 @@
     return even_cos + odd_cos, even_sin + odd_sin, even_cos - odd_cos, odd_sin - even_sin
 
 
+def folded_products(spec_ref, filter_ref, row, cols, filter_cols):
+    half = spec_ref.shape[1] // 2
+    real, imag, real_far, imag_far = unfolded(spec_ref, row, cols)
+    taps = [filter_ref[at * half + row : at * half + row + 16, filter_cols] for at in range(4)]
+    out_real, out_imag = real * taps[0] - imag * taps[1], real * taps[1] + imag * taps[0]
+    far_real = real_far * taps[2] - imag_far * taps[3]
+    far_imag = real_far * taps[3] + imag_far * taps[2]
+    return out_real + far_real, out_imag - far_imag, out_real - far_real, out_imag + far_imag
+
+
+def put_bins(bins_ref, row, cols, products):
+    half = bins_ref.shape[1] // 4
+    for at, value in enumerate(products):
+        put_halves(bins_ref, at // 2, at % 2 * half + row, cols, value)
+
+
 def filtered(spec_ref, filter_ref, bins_ref, cols, filter_cols):
-    half = spec_ref.shape[1] // 2
-    for row in range(0, half, 16):
-        real, imag, real_far, imag_far = unfolded(spec_ref, row, cols)
-        taps = [filter_ref[at * half + row : at * half + row + 16, filter_cols] for at in range(4)]
-        out_real, out_imag = real * taps[0] - imag * taps[1], real * taps[1] + imag * taps[0]
-        far_real = real_far * taps[2] - imag_far * taps[3]
-        far_imag = real_far * taps[3] + imag_far * taps[2]
-        put_halves(bins_ref, 0, row, cols, out_real + far_real)
-        put_halves(bins_ref, 0, half + row, cols, out_imag - far_imag)
-        put_halves(bins_ref, 1, row, cols, out_real - far_real)
-        put_halves(bins_ref, 1, half + row, cols, out_imag + far_imag)
+    for row in range(0, spec_ref.shape[1] // 2, 16):
+        put_bins(bins_ref, row, cols, folded_products(spec_ref, filter_ref, row, cols, filter_cols))
 
 
 def strided_rows(values, buf):
@@ -339,7 +346,6 @@
             packed = coded_ref[there : there + 48].astype(jnp.float32)
             values = unpack_rims([packed[8 * way : 8 * way + 8] for way in range(6)])
             for way, value in enumerate(values):
-                value = jnp.where(lax.axis_index("ctx") == 0, 0.0, value)
                 rims_buf[at, :, (8 * group + way) * 128 : (8 * group + way + 1) * 128] = value
 
 
@@ -404,95 +410,140 @@
     each_tile(width // 128, 4, shape)
 
 
+def driven_parts(driven, parts_buf, cols):
+    half = parts_buf.shape[1] // 2
+    for at, value in enumerate(parity_rows(driven)):
+        put_halves(parts_buf, 16 * at // half, 16 * at % half, cols, value)
+
+
+def put_rows(ref, cols, values):
+    for at, value in enumerate(parity_rows(values)):
+        ref[16 * at : 16 * at + 16, cols] = value
+
+
+def send_kernel(
+    first, projected_ref, taps_ref, near_ref, far_ref, forward_ref, backward_ref, coded_ref, mixed_ref, gates_ref,
+    strided_buf, parts_buf, spec_buf, bins_buf, right_buf, conv_buf, peak_buf, levels_buf, mixed_buf, sems,
+):
+    rows, width = right_buf.shape
+    tiles = width // 128
+
+    @pl.when(lax.axis_index("ctx") == 0)
+    def _():
+        def drive(tile, number):
+            cols = tile_lanes(tile, first)
+            sums = [
+                short_sum(
+                    strided_rows(projected_ref[at, :, cols], strided_buf.at[number, at]), None, taps_ref, at, cols
+                )
+                for at in range(3)
+            ]
+            put_rows(right_buf, tile_lanes(tile), sums[1])
+            driven_parts([one * two for one, two in zip(sums[0], sums[2])], parts_buf, tile_lanes(tile))
+
+        each_tile(tiles, strided_buf.shape[0], drive)
+        forward_dots(forward_ref, parts_buf, spec_buf)
+        each_tile(
+            tiles, 4, lambda tile, _: filtered(spec_buf, far_ref, bins_buf, tile_lanes(tile), tile_lanes(tile))
+        )
+        backward_dots(backward_ref, bins_buf, conv_buf)
+
+        def peaks(tile, _):
+            cols = tile_lanes(tile)
+            peak_buf[:, cols] = functools.reduce(
+                jnp.maximum, [jnp.abs(conv_buf[row : row + 8, cols]) for row in range(0, rows, 8)]
+            )
+
+        each_tile(tiles, 4, peaks)
+        code_tiles(tiles, rows, coded_ref, conv_buf, peak_buf, levels_buf)
+        each_tile(
+            tiles, 4, lambda tile, _: filtered(spec_buf, near_ref, bins_buf, tile_lanes(tile), tile_lanes(tile))
+        )
+        backward_dots(backward_ref, bins_buf, conv_buf)
+
+        def mix(tile):
+            cols = tile_lanes(tile)
+            return [right_buf[at : at + 16, cols] * conv_buf[at : at + 16, cols] for at in range(0, rows, 16)]
+
+        def gate(tile, number):
+            cols = tile_lanes(tile)
+            parts = strided_rows(projected_ref[1, :, cols], strided_buf.at[number, 1])
+            put_rows(gates_ref, cols, short_sum(parts, None, taps_ref, 1, cols))
+
+        each_tile(first // 128, strided_buf.shape[0], gate)
+        mix_out(mix, tiles, first, mixed_ref, mixed_buf, strided_buf.at[:, 0], sems)
+
+
 def own_kernel(
-    first, send, projected_ref, rims_ref, taps_ref, near_ref, far_ref, forward_ref, backward_ref, *refs
+    projected_ref, rims_ref, taps_ref, near_ref, last_near_ref, forward_ref, backward_ref, one_ref, two_ref, gates_ref,
+    _, right_ref, bins_ref, base_ref, mixed_ref,
+    rims_buf, strided_buf, parts_buf, spec_buf, bins_buf, conv_buf, mixed_buf, sems,
 ):
-    if send:
-        base_ref, right_ref, mixed_ref, coded_ref, *bufs = refs
-    else:
-        *driven_refs, _, base_ref, right_ref, mixed_ref = refs[:6]
-        bufs = refs[6:]
-    rims_buf, strided_buf, parts_buf, spec_buf, bins_buf, mixed_buf, sems = bufs[:7]
-    rows, width = base_ref.shape
+    rows, width = right_ref.shape
     half = rows // 2
-    tiles = width // 128
-    read_rims(rims_ref, rims_buf)
+    middle = near_ref.shape[1]
     place = lax.axis_index("ctx")
-
-    def sums_of(tile, number, ats):
-        cols = tile_lanes(tile, first)
-        sums = []
-        for at in ats:
-            parts = strided_rows(projected_ref[at, :, cols], strided_buf.at[number, at])
-            sums.append(short_sum(parts, rims_buf[at, :, cols], taps_ref, at, cols))
-        return sums
-
-    def put_right(tile, values):
-        for at, value in enumerate(parity_rows(values)):
-            right_ref[16 * at : 16 * at + 16, tile_lanes(tile)] = value
-
-    def drive(tile, number):
-        sums = sums_of(tile, number, range(3))
-        put_right(tile, sums[1])
-        driven = [one * two for one, two in zip(sums[0], sums[2])]
-        for at, value in enumerate(parity_rows(driven)):
-            put_halves(parts_buf, 16 * at // half, 16 * at % half, tile_lanes(tile), value)
-
-    if send:
-        each_tile(tiles, strided_buf.shape[0], drive)
-    else:
-
-        @pl.when(place != 0)
-        def _():
-            each_tile(tiles, strided_buf.shape[0], drive)
-
-        @pl.when(place == 0)
-        def _():
-            each_tile(tiles, strided_buf.shape[0], lambda tile, number: put_right(tile, sums_of(tile, number, [1])[0]))
-            start = 0
-            for ref in driven_refs:
-
-                def recall(tile, _, ref=ref, start=start):
-                    for row in range(0, rows, 16):
-                        value = ref[row : row + 16, tile_lanes(tile)]
-                        put_halves(parts_buf, row // half, row % half, tile_lanes(tile, start), value)
-
-                each_tile(ref.shape[1] // 128, 4, recall)
-                start += ref.shape[1]
-
-    forward_dots(forward_ref, parts_buf, spec_buf)
-    if send:
-        conv_buf, peak_buf, levels_buf = bufs[7:]
-
-        @pl.when(place == 0)
-        def _():
-            each_tile(
-                tiles, 4,
-                lambda tile, _: filtered(spec_buf, far_ref, bins_buf, tile_lanes(tile), tile_lanes(tile)),
-            )
-            backward_dots(backward_ref, bins_buf, conv_buf)
-
-            def peaks(tile, _):
-                cols = tile_lanes(tile)
-                peak_buf[:, cols] = functools.reduce(
-                    jnp.maximum, [jnp.abs(conv_buf[row : row + 8, cols]) for row in range(0, rows, 8)]
-                )
-
-            each_tile(tiles, 4, peaks)
-            code_tiles(tiles, rows, coded_ref, conv_buf, peak_buf, levels_buf)
-
-    each_tile(
-        tiles, 4, lambda tile, _: filtered(spec_buf, near_ref, bins_buf, tile_lanes(tile), tile_lanes(tile))
-    )
-    backward_dots(backward_ref, bins_buf, base_ref)
 
     @pl.when(place == 0)
     def _():
+        tiles = middle // 128
+        start = 0
+        for ref in (one_ref, two_ref):
+
+            def recall(tile, _, ref=ref, start=start):
+                for row in range(0, rows, 16):
+                    value = ref[row : row + 16, tile_lanes(tile)]
+                    put_halves(parts_buf, row // half, row % half, tile_lanes(tile, start), value)
+
+            each_tile(ref.shape[1] // 128, 4, recall)
+            start += ref.shape[1]
+        forward_dots(forward_ref, parts_buf.at[:, :, 0:middle], spec_buf.at[:, :, 0:middle])
+        each_tile(
+            tiles, 4, lambda tile, _: filtered(spec_buf, near_ref, bins_buf, tile_lanes(tile), tile_lanes(tile))
+        )
+        backward_dots(backward_ref, bins_buf, conv_buf)
+
         def mix(tile):
             cols = tile_lanes(tile)
-            return [right_ref[at : at + 16, cols] * base_ref[at : at + 16, cols] for at in range(0, rows, 16)]
-
-        mix_out(mix, tiles, first, mixed_ref, mixed_buf, strided_buf.at[:, 0], sems)
+            return [gates_ref[at : at + 16, cols] * conv_buf[at : at + 16, cols] for at in range(0, rows, 16)]
+
+        mix_out(mix, tiles, 0, mixed_ref, mixed_buf, strided_buf.at[:, 0], sems)
+
+    @pl.when(place != 0)
+    def _():
+        read_rims(rims_ref, rims_buf)
+
+        def drive(tile, number):
+            cols = tile_lanes(tile)
+            sums = [
+                short_sum(
+                    strided_rows(projected_ref[at, :, cols], strided_buf.at[number, at]),
+                    rims_buf[at, :, cols], taps_ref, at, cols,
+                )
+                for at in range(3)
+            ]
+            put_rows(right_ref, cols, sums[1])
+            driven_parts([one * two for one, two in zip(sums[0], sums[2])], parts_buf, cols)
+
+        each_tile(width // 128, strided_buf.shape[0], drive)
+        forward_dots(forward_ref, parts_buf, spec_buf)
+
+        def keep(tile, _):
+            cols = tile_lanes(tile)
+            for row in range(0, half, 16):
+                for at, value in enumerate(folded_products(spec_buf, near_ref, row, cols, cols)):
+                    bins_ref[at * half + row : at * half + row + 16, cols] = value
+
+        each_tile(middle // 128, 4, keep)
+        behind = width - middle
+
+        def finish(tile, _):
+            there, cols = tile_lanes(tile, middle), tile_lanes(tile)
+            for row in range(0, half, 16):
+                put_bins(bins_buf, row, cols, folded_products(spec_buf, last_near_ref, row, there, cols))
+
+        each_tile(behind // 128, 4, finish)
+        backward_dots(backward_ref, bins_buf.at[:, :, 0:behind], base_ref)
 
 
 def mix_out(mix, tiles, first, mixed_ref, buf, strided_buf, sems):
@@ -520,7 +571,7 @@
 
 
 def join_kernel(
-    coded_refs, far_ref, base_ref, right_ref, forward_ref, backward_ref, mixed_ref,
+    coded_refs, far_ref, own_bins_ref, right_ref, forward_ref, backward_ref, mixed_ref,
     parts_buf, spec_buf, bins_buf, conv_buf, strided_buf, buf, levels_buf, sems,
 ):
     rows, width = conv_buf.shape
@@ -543,17 +594,22 @@
 
             each_tile(counts[at], 4, spread_out)
         forward_dots(forward_ref, parts_buf, spec_buf)
-        each_tile(
-            tiles, 4, lambda tile, _: filtered(spec_buf, far_ref, bins_buf, tile_lanes(tile), tile_lanes(tile))
-        )
+
+        def add(tile, _):
+            cols = tile_lanes(tile)
+            for row in range(0, half, 16):
+                products = [
+                    value + own_bins_ref[at * half + row : at * half + row + 16, cols]
+                    for at, value in enumerate(folded_products(spec_buf, far_ref, row, cols, cols))
+                ]
+                put_bins(bins_buf, row, cols, products)
+
+        each_tile(tiles, 4, add)
         backward_dots(backward_ref, bins_buf, conv_buf)
 
         def mix(tile):
             cols = tile_lanes(tile)
-            return [
-                right_ref[at : at + 16, cols] * (conv_buf[at : at + 16, cols] + base_ref[at : at + 16, cols])
-                for at in range(0, rows, 16)
-            ]
+            return [right_ref[at : at + 16, cols] * conv_buf[at : at + 16, cols] for at in range(0, rows, 16)]
 
         mix_out(mix, tiles, 0, mixed_ref, buf, strided_buf, sems)
 
@@ -572,7 +628,7 @@
             cols = tile_lanes(tile)
             decode = decoder(levels_buf, tile)
             return [
-                right_ref[at : at + 16, cols] * (decode(coded_ref[tile_rows(tile, at), :]) + base_ref[at : at + 16, cols])
+                right_ref[at : at + 16, tile_lanes(tile, first)] * (decode(coded_ref[tile_rows(tile, at), :]) + base_ref[at : at + 16, cols])
                 for at in range(0, rows, 16)
             ]
 
@@ -663,34 +719,51 @@
 
     last_near, last_far, second_halves = spectra(middle, behind, *layers)
 
-    def own(first, size, send, near, far, *more):
-        return pl.pallas_call(
-            functools.partial(own_kernel, first, send),
-            in_specs=[in_vmem] * 7 + [in_vmem, in_vmem, in_hbm][: len(more)],
-            out_specs=[in_vmem, in_vmem, in_hbm] + [in_vmem] * send,
-            out_shape=arrays((rows, size), (rows, size))
-            + arrays((rows, width), dtype=jnp.bfloat16)
-            + message(size) * send,
-            input_output_aliases={} if send else {9: 2},
-            scratch_shapes=[
-                floats((3, 8, width)),
-                floats((2, 3, rows, 128)),
-                shorts((2, rows, size)),
-                floats((2, rows, size)),
-                shorts((2, 2 * rows, size)),
-                shorts((rows, size)),
-                pltpu.SemaphoreType.DMA((2,)),
-            ]
-            + [floats((rows, size)), floats((8, size)), floats((16, 128))] * send,
-            compiler_params=params(),
-            cost_estimate=cost(2),
-            name="own",
-        )(projected, one_code, taps, near, far, forward, backward, *more)
-
-    last_base, last_right, mixed, code = own(middle, behind, True, last_near, last_far)
-    last_code = lax.ppermute(code, "ctx", pairs)
     near, far = spectra(0, middle, second_halves)
-    base, right, mixed = own(0, middle, False, near, far, one_driven, two_driven, mixed)
+    last_near, near = lax.optimization_barrier((last_near, near))
+    last_code, mixed, gates = pl.pallas_call(
+        functools.partial(send_kernel, middle),
+        in_specs=[in_vmem] * 6,
+        out_specs=[in_vmem, in_hbm, in_vmem],
+        out_shape=message(behind) + arrays((rows, width), dtype=jnp.bfloat16) + arrays((rows, middle)),
+        scratch_shapes=[
+            floats((2, 3, rows, 128)),
+            shorts((2, rows, behind)),
+            floats((2, rows, behind)),
+            shorts((2, 2 * rows, behind)),
+            floats((rows, behind)),
+            floats((rows, behind)),
+            floats((8, behind)),
+            floats((16, 128)),
+            shorts((rows, behind)),
+            pltpu.SemaphoreType.DMA((2,)),
+        ],
+        compiler_params=params(),
+        cost_estimate=cost(2),
+        name="send",
+    )(projected, taps, last_near, last_far, forward, backward)
+    last_code = lax.ppermute(last_code, "ctx", pairs)
+    right, own_bins, last_base, mixed = pl.pallas_call(
+        own_kernel,
+        in_specs=[in_vmem] * 10 + [in_hbm],
+        out_specs=[in_vmem] * 3 + [in_hbm],
+        out_shape=arrays((rows, width), (total_len, middle), (rows, behind))
+        + arrays((rows, width), dtype=jnp.bfloat16),
+        input_output_aliases={10: 3},
+        scratch_shapes=[
+            floats((3, 8, width)),
+            floats((2, 3, rows, 128)),
+            shorts((2, rows, width)),
+            floats((2, rows, width)),
+            shorts((2, 2 * rows, middle)),
+            floats((rows, middle)),
+            shorts((rows, middle)),
+            pltpu.SemaphoreType.DMA((2,)),
+        ],
+        compiler_params=params(),
+        cost_estimate=cost(4),
+        name="own",
+    )(projected, one_code, taps, near, last_near, forward, backward, one_driven, two_driven, gates, mixed)
     mixed = pl.pallas_call(
         lambda one_ref, two_ref, *refs: join_kernel((one_ref, two_ref), *refs[:5], *refs[6:]),
         in_specs=[in_vmem] * 7 + [in_hbm],
@@ -710,7 +783,7 @@
         compiler_params=params(),
         cost_estimate=cost(2),
         name="join",
-    )(one_code, two_code, far, base, right, forward, backward, mixed)
+    )(one_code, two_code, far, own_bins, right, forward, backward, mixed)
     return pl.pallas_call(
         functools.partial(last_kernel, middle),
         in_specs=[in_vmem] * 3 + [in_hbm],
@@ -726,7 +799,7 @@
         compiler_params=params(),
         cost_estimate=cost(1),
         name="last",
-    )(last_code, last_base, last_right, mixed)
+    )(last_code, last_base, right, mixed)
 
 
 def turn_table(outer_ids, inner_ids, modulus):

time: 17.7 us -> 17.1 us (0.966)
  Pallas kernels: 12.3 us -> 11.7 us
    pallas_call x2, Pallas kernels: 4.69 us -> 4 us  [the longest x1 3.96 us: one_way(): pl.pallas_call(own_kernel, in_specs=[in_vmem] * 10 + [in_hbm], out_specs=...]
  transfers between devices with their start and end apart: 3 -> 3, of which waited for: 0 -> 0; matrix products, arithmetic and copies ran while one was open for 0% -> 0% of each run, Pallas kernels for 66% -> 64%
where the time goes in v3:
time: 17.1 us; the launch traced here: 16.9 us
  Pallas kernels  11.7 us (68%)
  starting transfers between devices  4.88 us (29%)
  between operations  0.22 us (1%)
    pallas_call x1, Pallas kernels, one_way(): pl.pallas_call(own_kernel, in_specs=[in_vmem] * 10 + [in_hbm], out_specs=...  3.96 us
    pallas_call x2, Pallas kernels, spectra(): pl.pallas_call(functools.partial(filter_kernel, first, fresh), in_specs=[...  3.95 us
    pallas_call x1, Pallas kernels, one_way(): pl.pallas_call(lambda one_ref, two_ref, *refs: join_kernel((one_ref, two_...  2.89 us
    ppermute x1, starting transfers between devices, one_way(): one_code = lax.ppermute(one_code, 'ctx', [(0, 1), (1, 0)])  2 us
    ppermute x1, starting transfers between devices, one_way(): two_code = lax.ppermute(two_code, 'ctx', [(0, 1), (1, 0)])  1.59 us
    ppermute x1, starting transfers between devices, one_way(): last_code = lax.ppermute(last_code, 'ctx', pairs)  1.29 us
    pallas_call x1, Pallas kernels, one_way(): pl.pallas_call(functools.partial(last_kernel, middle), in_specs=[in_vmem]...  0.83 us
  transfers between devices with their start and end apart: 3, of which 0 were waited for; matrix products, arithmetic and copies ran while one was open for 0% of the time, Pallas kernels for 64%

profile of v3, /device:TPU:6, one launch (start us, length us, event | category | flops | bytes accessed | tf_op | source)
XLA Modules:
  0.0 16.9 jit_solution(2235787034811125420)
XLA Ops:
  0.0 0.0 copy-start.1
  0.1 0.0 copy-start.3
  0.1 0.0 copy-start.4
  0.1 0.0 copy-start.5
  0.1 0.0 copy-start.6
  0.1 0.0 copy-start.7
  0.1 0.0 copy-start.8
  0.1 0.0 copy-start.9
  0.1 0.0 copy-start.10
  0.2 0.0 copy-start.12
  0.2 2.0 %collective-permute-start.1 = (bf16[560,128]{1,0:T(8,128)(2,1)S(1)}, bf16[560,128]{1,0:T(8,128)(2,1)S(1)}, u32[]{:S(2)}, u32[]{:S(2)}) collective-permute-start(bf16[560,128]{1,0:T(8,128)(2,1)S(1)} %get-tuple-element.29), channel_id=1, source_target_pairs={{0,16},{16,0},{1,17},{17,1},{2,18},{18,2},{3,19},{19,3},{4,20},{20... | collective-permute-start | bytes 430088 | tf_op jit(solution)/shard_map/ppermute | solution.py:687
  2.2 1.6 %collective-permute-start.2 = (bf16[1296,128]{1,0:T(8,128)(2,1)S(1)}, bf16[1296,128]{1,0:T(8,128)(2,1)S(1)}, u32[]{:S(2)}, u32[]{:S(2)}) collective-permute-start(bf16[1296,128]{1,0:T(8,128)(2,1)S(1)} %get-tuple-element.37), channel_id=1, source_target_pairs={{0,16},{16,0},{1,17},{17,1},{2,18},{18,2},{3,19},{19,3},{4,20},{20... | collective-permute-start | bytes 995336 | tf_op jit(solution)/shard_map/ppermute | solution.py:698
  3.8 0.0 copy-done.1
  3.8 0.0 copy-done.4
  3.8 1.6 %filter.2 = (f32[256,512]{1,0:T(8,128)S(1)}, f32[256,512]{1,0:T(8,128)S(1)}, bf16[256,192]{1,0:T(8,128)(2,1)S(1)}) custom-call(f32[64,2048]{1,0:T(8,128)S(1)} %copy-done.1, f32[1,2048]{1,0:T(1,128)S(1)} %bitcast.9, f32[1,2048]{1,0:T(1,128)S(1)} %bitcast.11, f32[256,128]{1,0:T(8,128)S(1)} %copy-done.10, bf16[256,192]{1,0:T(8,128)(2,1)S(1)} %copy-done.9, ...), custom_call_target="tpu_custom_call" | custom-call | flops 2000000000 | bytes 6000000 | tf_op jit(solution)/shard_map/filter/pallas_call | solution.py:702
  5.5 0.0 copy-start.11
  5.5 2.3 %filter.3 = (f32[256,1536]{1,0:T(8,128)S(1)}, f32[256,1536]{1,0:T(8,128)S(1)}) custom-call(f32[64,2048]{1,0:T(8,128)S(1)} %copy-done.1, f32[1,2048]{1,0:T(1,128)S(1)} %bitcast.10, f32[1,2048]{1,0:T(1,128)S(1)} %bitcast.12, f32[256,128]{1,0:T(8,128)S(1)} %copy-done.10, bf16[256,192]{1,0:T(8,128)(2,1)S(1)} %copy-done.9, ...), custom_call_target="tpu_custom_call" | custom-call | flops 2000000000 | bytes 6000000 | tf_op jit(solution)/shard_map/filter/pallas_call | solution.py:702
  7.9 1.3 %collective-permute-start = (bf16[528,128]{1,0:T(8,128)(2,1)S(1)}, bf16[528,128]{1,0:T(8,128)(2,1)S(1)}, u32[]{:S(2)}, u32[]{:S(2)}) collective-permute-start(bf16[528,128]{1,0:T(8,128)(2,1)S(1)} %get-tuple-element.28), channel_id=1, source_target_pairs={{0,16},{1,17},{2,18},{3,19},{4,20},{5,21},{6,22},{7,23},{8,24},{9,... | collective-permute-start | bytes 405512 | tf_op jit(solution)/shard_map/ppermute | solution.py:745
  9.2 0.0 collective-permute-done.1.rims_ref.one_ref
  9.2 4.0 %own.1 = (f32[128,2048]{1,0:T(8,128)S(1)}, f32[256,1536]{1,0:T(8,128)S(1)}, f32[128,512]{1,0:T(8,128)S(1)}, bf16[128,2048]{1,0:T(8,128)(2,1)}) custom-call(bf16[3,128,2048]{2,1,0:T(8,128)(2,1)S(1)} %copy-done, bf16[560,128]{1,0:T(8,128)(2,1)S(1)} %collective-permute-done.1.rims_ref.one_ref, ...), custom_call_target="tpu_custom_call", output_to_operand_aliasing={{3}: (10, {})} | custom-call | flops 4000000000 | bytes 12000000 | tf_op jit(solution)/shard_map/own/pallas_call | solution.py:746
  13.2 0.0 collective-permute-done.2.two_ref
  13.2 2.9 %join.1.sofar_ref = bf16[128,2048]{1,0:T(8,128)(2,1)} custom-call(bf16[560,128]{1,0:T(8,128)(2,1)S(1)} %collective-permute-done.1.rims_ref.one_ref, bf16[1296,128]{1,0:T(8,128)(2,1)S(1)} %collective-permute-done.2.two_ref, f32[256,1536]{1,0:T(8,128)S(1)} %get-tuple-element.38.refs_0_, ...), custom_call_target="tpu_custom_call", output_to_operand_aliasing={{}: (7, {})} | custom-call | flops 2000000000 | bytes 6000000 | tf_op jit(solution)/shard_map/join/pallas_call | solution.py:767
  16.1 0.0 collective-permute-done.coded_ref
  16.1 0.8 %last.1 = bf16[128,2048]{1,0:T(8,128)(2,1)} custom-call(bf16[528,128]{1,0:T(8,128)(2,1)S(1)} %collective-permute-done.coded_ref, f32[128,512]{1,0:T(8,128)S(1)} %get-tuple-element.35.base_ref, f32[128,2048]{1,0:T(8,128)S(1)} %get-tuple-element.36.refs_2_.right_ref, bf16[128,2048]{1,0:T(8,128)(2,1)} %join.1.sofar_ref), custom_call_target="tpu_custom_call", output_to_operand_aliasing={{}: (3, {})} | custom-call | flops 1000000000 | bytes 3000000 | tf_op jit(solution)/shard_map/last/pallas_call | solution.py:787
  (16 shorter events, 0.1 us)
Async XLA Ops:
  0.0 2.2 %copy-start = (bf16[3,128,2048]{2,1,0:T(8,128)(2,1)S(1)}, bf16[3,128,2048]{2,1,0:T(8,128)(2,1)}, u32[]{:S(2)}) copy-start(bf16[3,128,2048]{2,1,0:T(8,128)(2,1)} %projected_ref.7) | copy-start | bytes 4718596
  0.0 2.2 %copy-start.2 = (f32[7,3,2048]{2,0,1:T(8,128)S(1)}, f32[7,3,2048]{2,0,1:T(8,128)}, u32[]{:S(2)}) copy-start(f32[7,3,2048]{2,0,1:T(8,128)} %param.14) | copy-start | bytes 516100
  0.0 3.7 %copy-start.1 = (f32[64,2048]{1,0:T(8,128)S(1)}, f32[64,2048]{1,0:T(8,128)}, u32[]{:S(2)}) copy-start(f32[64,2048]{1,0:T(8,128)} %out_ref.3) | copy-start | bytes 1572868
  0.1 3.7 %copy-start.3 = (f32[64,64]{1,0:T(8,128)S(1)}, f32[64,64]{1,0:T(8,128)}, u32[]{:S(2)}) copy-start(f32[64,64]{1,0:T(8,128)} %refs_4_.2) | copy-start | bytes 49156
  0.1 3.7 %copy-start.4 = (f32[33,64]{1,0:T(8,128)S(1)}, f32[33,64]{1,0:T(8,128)}, u32[]{:S(2)}) copy-start(f32[33,64]{1,0:T(8,128)} %refs_1_.1) | copy-start | bytes 25348
  0.1 3.7 %copy-start.5 = (f32[2048]{0:T(1024)S(1)}, f32[2048]{0:T(1024)}, u32[]{:S(2)}) copy-start(f32[2048]{0:T(1024)} %param.20) | copy-start | bytes 24580
  0.1 3.7 %copy-start.6 = (f32[2048]{0:T(1024)S(1)}, f32[2048]{0:T(1024)}, u32[]{:S(2)}) copy-start(f32[2048]{0:T(1024)} %param.21) | copy-start | bytes 24580
  0.1 3.7 %copy-start.7 = (f32[64]{0:T(128)S(1)}, f32[64]{0:T(128)}, u32[]{:S(2)}) copy-start(f32[64]{0:T(128)} %param.16) | copy-start | bytes 772
  0.1 3.7 %copy-start.8 = (f32[64]{0:T(128)S(1)}, f32[64]{0:T(128)}, u32[]{:S(2)}) copy-start(f32[64]{0:T(128)} %param.17) | copy-start | bytes 772
  0.1 3.7 %copy-start.9 = (bf16[256,192]{1,0:T(8,128)(2,1)S(1)}, bf16[256,192]{1,0:T(8,128)(2,1)}, u32[]{:S(2)}) copy-start(bf16[256,192]{1,0:T(8,128)(2,1)} %constant.9.clone.forward_ref.refs_3_) | copy-start | bytes 294916
  0.1 3.7 %copy-start.10 = (f32[256,128]{1,0:T(8,128)S(1)}, f32[256,128]{1,0:T(8,128)}, u32[]{:S(2)}) copy-start(f32[256,128]{1,0:T(8,128)} %constant.8.clone.places_ref) | copy-start | bytes 393220
  0.2 3.7 %copy-start.12 = (f32[40,256]{1,0:T(8,128)S(1)}, f32[40,256]{1,0:T(8,128)}, u32[]{:S(2)}) copy-start(f32[40,256]{1,0:T(8,128)} %constant.10.clone.refs_0_) | copy-start | bytes 122884
  0.2 9.0 %collective-permute-start.1 = (bf16[560,128]{1,0:T(8,128)(2,1)S(1)}, bf16[560,128]{1,0:T(8,128)(2,1)S(1)}, u32[]{:S(2)}, u32[]{:S(2)}) collective-permute-start(bf16[560,128]{1,0:T(8,128)(2,1)S(1)} %get-tuple-element.29), channel_id=1, source_target_pairs={{0,16},{16,0},{1,17},{17,1},{2,18},{18,2},{3,19},{19,3},{4,20},{20... | collective-permute-start | bytes 430088 | tf_op jit(solution)/shard_map/ppermute | solution.py:687
  2.2 11.0 %collective-permute-start.2 = (bf16[1296,128]{1,0:T(8,128)(2,1)S(1)}, bf16[1296,128]{1,0:T(8,128)(2,1)S(1)}, u32[]{:S(2)}, u32[]{:S(2)}) collective-permute-start(bf16[1296,128]{1,0:T(8,128)(2,1)S(1)} %get-tuple-element.37), channel_id=1, source_target_pairs={{0,16},{16,0},{1,17},{17,1},{2,18},{18,2},{3,19},{19,3},{4,20},{20... | collective-permute-start | bytes 995336 | tf_op jit(solution)/shard_map/ppermute | solution.py:698
  5.5 2.4 %copy-start.11 = (bf16[128,384]{1,0:T(8,128)(2,1)S(1)}, bf16[128,384]{1,0:T(8,128)(2,1)}, u32[]{:S(2)}) copy-start(bf16[128,384]{1,0:T(8,128)(2,1)} %constant.11.clone.backward_ref.refs_4_) | copy-start | bytes 294916
  7.9 8.2 %collective-permute-start = (bf16[528,128]{1,0:T(8,128)(2,1)S(1)}, bf16[528,128]{1,0:T(8,128)(2,1)S(1)}, u32[]{:S(2)}, u32[]{:S(2)}) collective-permute-start(bf16[528,128]{1,0:T(8,128)(2,1)S(1)} %get-tuple-element.28), channel_id=1, source_target_pairs={{0,16},{1,17},{2,18},{3,19},{4,20},{5,21},{6,22},{7,23},{8,24},{9,... | collective-permute-start | bytes 405512 | tf_op jit(solution)/shard_map/ppermute | solution.py:745

commit v4 on v3

--- a/solution.py
+++ b/solution.py
@@ -207,14 +207,14 @@
     return pl.ds(pl.multiple_of(tile * 128 + row, 16), count)
 
 
-def place_level(peak, tile, peak_buf, levels_buf):
+def place_level(peak, tile, peak_buf, levels_buf, levels_first):
     for step in (1, 2, 4):
         peak = jnp.maximum(peak, pltpu.roll(peak, step, 0))
     level = jnp.maximum(peak, TINY)
     wide = level * 65537.0
     level = wide - (wide - level)
     peak_buf[:, tile_lanes(tile)] = SPAN / level
-    levels_buf[pl.ds(tile, 1), :] = level[0:1]
+    levels_buf[pl.ds(levels_first + tile, 1), :] = level[0:1]
 
 
 def put_coded(coded_ref, tile, row, value, gain):
@@ -251,7 +251,9 @@
     return jnp.sin(dot(mid_ref[...] * freq, layer)).T
 
 
-def encode_tiles(tiles, rows, streams, taps_ref, taps_first, coded_ref, driven_ref, strided_buf, peak_buf, levels_buf):
+def encode_tiles(
+    tiles, rows, streams, taps_ref, taps_first, coded_ref, driven_ref, strided_buf, peak_buf, levels_buf, levels_first=0
+):
     def drive(tile, number):
         cols = tile_lanes(tile)
         sums = [
@@ -267,12 +269,16 @@
         peak_buf[:, cols] = functools.reduce(jnp.maximum, [jnp.abs(value) for value in driven])
 
     each_tile(tiles, strided_buf.shape[0], drive)
-    code_tiles(tiles, rows, coded_ref, driven_ref, peak_buf, levels_buf)
-
-
-def code_tiles(tiles, rows, coded_ref, values_ref, peak_buf, levels_buf):
-    each_tile(tiles, 4, lambda tile, _: place_level(peak_buf[:, tile_lanes(tile)], tile, peak_buf, levels_buf))
-    coded_ref[tiles * rows : tiles * rows + 16] = levels_buf[...].astype(jnp.bfloat16)
+    code_tiles(tiles, rows, coded_ref, driven_ref, peak_buf, levels_buf, levels_first)
+
+
+def code_tiles(tiles, rows, coded_ref, values_ref, peak_buf, levels_buf, levels_first=0):
+    each_tile(
+        tiles, 4,
+        lambda tile, _: place_level(peak_buf[:, tile_lanes(tile)], tile, peak_buf, levels_buf, levels_first),
+    )
+    if levels_first == 0:
+        coded_ref[tiles * rows : tiles * rows + 16] = levels_buf[...].astype(jnp.bfloat16)
 
     def code(tile, _):
         cols = tile_lanes(tile)
@@ -285,7 +291,7 @@
 
 
 def first_kernel(
-    projected_ref, taps_ref, coded_ref, driven_ref, rows_buf, rim_buf, taps_buf, strided_buf, peak_buf, levels_buf, sems
+    projected_ref, taps_ref, coded_ref, driven_ref, levels_ref, rows_buf, rim_buf, taps_buf, strided_buf, peak_buf, sems
 ):
     rows, size = rows_buf.shape[1:]
     tiles = size // 128
@@ -301,16 +307,17 @@
         ]
         for copy in copies:
             copy.start()
-        for copy in copies:
+        for copy in copies[:3]:
             copy.wait()
+        levels_ref[...] = jnp.zeros_like(levels_ref)
         encode_tiles(
             tiles, rows, lambda way, tile: rows_buf[way, :, tile_lanes(tile)], taps_buf, 0, coded_ref, driven_ref,
-            strided_buf, peak_buf, levels_buf,
+            strided_buf, peak_buf, levels_ref, 16 - tiles,
         )
-
+        copies[3].wait()
         for at in range(3):
             for group in range(rim_buf.shape[2] // 1024):
-                there = tiles * rows + 16 + (3 * group + at) * 48
+                there = tiles * rows + (3 * group + at) * 48
                 values = [
                     rim_buf[at, :, (8 * group + way) * 128 : (8 * group + way + 1) * 128].astype(jnp.float32)[8:]
                     for way in range(8)
@@ -350,25 +357,34 @@
 
 
 def encode_kernel(
-    first, projected_ref, taps_ref, coded_ref, driven_ref, strided_buf, peak_buf, levels_buf
+    first, projected_ref, taps_ref, one_levels_ref, coded_ref, driven_ref, strided_buf, peak_buf, levels_buf
 ):
     rows, size = driven_ref.shape
 
     @pl.when(lax.axis_index("ctx") == 0)
     def _():
+        levels_buf[...] = one_levels_ref[...]
         encode_tiles(
             size // 128, rows, lambda way, tile: projected_ref[2 * way, :, tile_lanes(tile, first)], taps_ref, first,
             coded_ref, driven_ref, strided_buf, peak_buf, levels_buf,
         )
 
 
-def filter_kernel(first, fresh, out_ref, decay_ref, skip_ref, places_ref, forward_ref, *refs):
-    if fresh:
-        *layer_refs, near_ref, far_ref, halves_ref, raw_buf, parts_buf, spec_buf, scale_buf, scaled_buf = refs
-        second_high, second_low = halves(second_layer(*layer_refs, scaled_buf))
-        halves_ref[...] = jnp.concatenate([second_high, second_high, second_low], axis=1)
-    else:
-        halves_ref, near_ref, far_ref, raw_buf, parts_buf, spec_buf, scale_buf = refs
+def network_halves(layer_refs, halves_ref, scaled_buf):
+    second_high, second_low = halves(second_layer(*layer_refs, scaled_buf))
+    halves_ref[...] = jnp.concatenate([second_high, second_high, second_low], axis=1)
+
+
+def network_filter_kernel(first, *refs):
+    weight_refs, layer_refs, (near_ref, far_ref, halves_ref), bufs = refs[:5], refs[5:10], refs[10:13], refs[13:]
+    network_halves(layer_refs, halves_ref, bufs[-1])
+    filter_spectra(first, *weight_refs, halves_ref, near_ref, far_ref, *bufs[:-1])
+
+
+def filter_spectra(
+    first, out_ref, decay_ref, skip_ref, places_ref, forward_ref, halves_ref, near_ref, far_ref,
+    raw_buf, parts_buf, spec_buf, scale_buf,
+):
     rows, width = near_ref.shape[0] // 2, near_ref.shape[1]
     half = rows // 2
     out_high, out_low = halves(out_ref[:, first : first + width])
@@ -423,7 +439,7 @@
 
 def send_kernel(
     first, projected_ref, taps_ref, near_ref, far_ref, forward_ref, backward_ref, coded_ref, mixed_ref, gates_ref,
-    strided_buf, parts_buf, spec_buf, bins_buf, right_buf, conv_buf, peak_buf, levels_buf, mixed_buf, sems,
+    strided_buf, parts_buf, spec_buf, bins_buf, right_buf, conv_buf, peak_buf, levels_buf,
 ):
     rows, width = right_buf.shape
     tiles = width // 128
@@ -471,12 +487,12 @@
             put_rows(gates_ref, cols, short_sum(parts, None, taps_ref, 1, cols))
 
         each_tile(first // 128, strided_buf.shape[0], gate)
-        mix_out(mix, tiles, first, mixed_ref, mixed_buf, strided_buf.at[:, 0], sems)
+        mix_tiles(mix, tiles, mixed_ref, strided_buf.at[:, 0])
 
 
 def own_kernel(
     projected_ref, rims_ref, taps_ref, near_ref, last_near_ref, forward_ref, backward_ref, one_ref, two_ref, gates_ref,
-    _, right_ref, bins_ref, base_ref, mixed_ref,
+    behind_ref, right_ref, bins_ref, base_ref, mixed_ref,
     rims_buf, strided_buf, parts_buf, spec_buf, bins_buf, conv_buf, mixed_buf, sems,
 ):
     rows, width = right_ref.shape
@@ -487,6 +503,8 @@
     @pl.when(place == 0)
     def _():
         tiles = middle // 128
+        behind = pltpu.make_async_copy(behind_ref, mixed_ref.at[:, pl.ds(middle, width - middle)], sems.at[0])
+        behind.start()
         start = 0
         for ref in (one_ref, two_ref):
 
@@ -507,7 +525,11 @@
             cols = tile_lanes(tile)
             return [gates_ref[at : at + 16, cols] * conv_buf[at : at + 16, cols] for at in range(0, rows, 16)]
 
-        mix_out(mix, tiles, 0, mixed_ref, mixed_buf, strided_buf.at[:, 0], sems)
+        mix_tiles(mix, tiles, mixed_buf, strided_buf.at[:, 0])
+        ahead = pltpu.make_async_copy(mixed_buf, mixed_ref.at[:, pl.ds(0, middle)], sems.at[1])
+        ahead.start()
+        ahead.wait()
+        behind.wait()
 
     @pl.when(place != 0)
     def _():
@@ -534,7 +556,7 @@
                 for at, value in enumerate(folded_products(spec_buf, near_ref, row, cols, cols)):
                     bins_ref[at * half + row : at * half + row + 16, cols] = value
 
-        each_tile(middle // 128, 4, keep)
+        each_tile(middle // 128, 12, keep)
         behind = width - middle
 
         def finish(tile, _):
@@ -546,24 +568,11 @@
         backward_dots(backward_ref, bins_buf.at[:, :, 0:behind], base_ref)
 
 
-def mix_out(mix, tiles, first, mixed_ref, buf, strided_buf, sems):
-    parts = sems.shape[0]
-    copies = []
-    for part in range(parts):
-        start, count = part * (tiles // parts), tiles // parts
-
-        def one(tile, number, start=start):
-            buf[:, tile_lanes(start + tile)] = natural_rows(mix(start + tile), strided_buf.at[number]).astype(jnp.bfloat16)
-
-        each_tile(count, strided_buf.shape[0], one)
-        span = slice(start * 128, (start + count) * 128)
-        copy = pltpu.make_async_copy(
-            buf.at[:, span], mixed_ref.at[:, pl.ds(first + start * 128, count * 128)], sems.at[part]
-        )
-        copy.start()
-        copies.append(copy)
-    for copy in copies:
-        copy.wait()
+def mix_tiles(mix, tiles, mixed_ref, strided_buf):
+    def one(tile, number):
+        mixed_ref[:, tile_lanes(tile)] = natural_rows(mix(tile), strided_buf.at[number]).astype(jnp.bfloat16)
+
+    each_tile(tiles, strided_buf.shape[0], one)
 
 
 def read_levels(coded_ref, levels_buf, tiles, rows):
@@ -572,7 +581,7 @@
 
 def join_kernel(
     coded_refs, far_ref, own_bins_ref, right_ref, forward_ref, backward_ref, mixed_ref,
-    parts_buf, spec_buf, bins_buf, conv_buf, strided_buf, buf, levels_buf, sems,
+    parts_buf, spec_buf, bins_buf, conv_buf, strided_buf, levels_buf,
 ):
     rows, width = conv_buf.shape
     half = rows // 2
@@ -582,12 +591,13 @@
     def _():
         counts = [coded_refs[0].shape[0] // rows, coded_refs[1].shape[0] // rows]
         counts[0] = tiles - counts[1]
+        read_levels(coded_refs[1], levels_buf, counts[1], rows)
         for at, ref in enumerate(coded_refs):
             start = counts[0] * 128 * at
-            read_levels(ref, levels_buf.at[at], counts[at], rows)
-
-            def spread_out(tile, _, ref=ref, at=at, start=start):
-                decode = decoder(levels_buf.at[at], tile)
+            levels_first = 0 if at else 16 - counts[0]
+
+            def spread_out(tile, _, ref=ref, start=start, levels_first=levels_first):
+                decode = decoder(levels_buf, levels_first + tile)
                 for row in range(0, rows, 16):
                     value = decode(ref[tile_rows(tile, row), :])
                     put_halves(parts_buf, row // half, row % half, tile_lanes(tile, start), value)
@@ -604,35 +614,41 @@
                 ]
                 put_bins(bins_buf, row, cols, products)
 
-        each_tile(tiles, 4, add)
+        each_tile(tiles, 12, add)
         backward_dots(backward_ref, bins_buf, conv_buf)
 
         def mix(tile):
             cols = tile_lanes(tile)
             return [right_ref[at : at + 16, cols] * conv_buf[at : at + 16, cols] for at in range(0, rows, 16)]
 
-        mix_out(mix, tiles, 0, mixed_ref, buf, strided_buf, sems)
+        mix_tiles(mix, tiles, mixed_ref, strided_buf)
 
 
 def last_kernel(
-    first, coded_ref, base_ref, right_ref, sofar_ref, mixed_ref, strided_buf, buf, levels_buf, sems
+    first, coded_ref, base_ref, right_ref, ahead_ref, _, mixed_ref, strided_buf, buf, levels_buf, sems
 ):
     rows, width = base_ref.shape
     tiles = width // 128
 
     @pl.when(lax.axis_index("ctx") != 0)
     def _():
+        ahead = pltpu.make_async_copy(ahead_ref, mixed_ref.at[:, pl.ds(0, first)], sems.at[0])
+        ahead.start()
         read_levels(coded_ref, levels_buf, tiles, rows)
 
         def mix(tile):
-            cols = tile_lanes(tile)
             decode = decoder(levels_buf, tile)
             return [
-                right_ref[at : at + 16, tile_lanes(tile, first)] * (decode(coded_ref[tile_rows(tile, at), :]) + base_ref[at : at + 16, cols])
+                right_ref[at : at + 16, tile_lanes(tile, first)]
+                * (decode(coded_ref[tile_rows(tile, at), :]) + base_ref[at : at + 16, tile_lanes(tile)])
                 for at in range(0, rows, 16)
             ]
 
-        mix_out(mix, tiles, first, mixed_ref, buf, strided_buf, sems)
+        mix_tiles(mix, tiles, buf, strided_buf)
+        behind = pltpu.make_async_copy(buf, mixed_ref.at[:, pl.ds(first, width)], sems.at[1])
+        behind.start()
+        behind.wait()
+        ahead.wait()
 
 
 def params(mib=40):
@@ -672,60 +688,64 @@
     layers = (feats, pos_in, pos_bias[None, :], sine_freq[None, :], pos_mid)
     tile_bufs = [floats((2, 2, rows, 128)), floats((8, width)), floats((16, 128))]
     one, two = ahead
-    one_code, one_driven = pl.pallas_call(
+    one_code, one_driven, one_levels = pl.pallas_call(
         first_kernel,
         in_specs=[in_hbm] * 2,
-        out_specs=[in_vmem] * 2,
-        out_shape=message(one, width // 128 * 18) + arrays((rows, one)),
+        out_specs=[in_vmem] * 3,
+        out_shape=arrays((one // 128 * rows + width // 128 * 18, 128), dtype=jnp.bfloat16)
+        + arrays((rows, one), (16, 128)),
         scratch_shapes=[shorts((2, rows, one)), shorts((3, 16, width)), floats((3, TAPS, one))]
-        + tile_bufs
+        + tile_bufs[:2]
         + [pltpu.SemaphoreType.DMA((4,))],
         compiler_params=params(),
         cost_estimate=cost(1),
         name="first",
     )(*[pltpu.with_memory_space_constraint(array, pltpu.HBM) for array in (projected, taps)])
     one_code = lax.ppermute(one_code, "ctx", [(0, 1), (1, 0)])
+    weights = (pos_out, decay_rate[None, :], skip_gain[None, :], places, forward)
+    hidden = pos_mid.shape[1]
+
+    def spectra_bufs(size):
+        return [floats((total_len, size)), shorts((2, rows, 2 * size)), floats((2, rows, 2 * size)), floats((8, size))]
+
+    spectra = arrays((total_len, behind), (total_len, behind)) + arrays((total_len, 3 * hidden), dtype=jnp.bfloat16)
     two_code, two_driven = pl.pallas_call(
         functools.partial(encode_kernel, one),
-        in_specs=[in_vmem] * 2,
+        in_specs=[in_vmem] * 3,
         out_specs=[in_vmem] * 2,
         out_shape=message(two) + arrays((rows, two)),
         scratch_shapes=tile_bufs,
         compiler_params=params(),
         cost_estimate=cost(1),
         name="encode",
-    )(projected, taps)
+    )(projected, taps, one_levels)
     two_code = lax.ppermute(two_code, "ctx", [(0, 1), (1, 0)])
-
-    def spectra(first, size, *more):
-        fresh = len(more) > 1
-        return pl.pallas_call(
-            functools.partial(filter_kernel, first, fresh),
-            in_specs=[in_vmem] * (5 + len(more)),
-            out_specs=[in_vmem] * (2 + fresh),
-            out_shape=arrays((total_len, size), (total_len, size))
-            + arrays((total_len, 3 * pos_mid.shape[1]), dtype=jnp.bfloat16) * fresh,
-            scratch_shapes=[
-                floats((total_len, size)),
-                shorts((2, rows, 2 * size)),
-                floats((2, rows, 2 * size)),
-                floats((8, size)),
-            ]
-            + [floats((feats.shape[0], pos_in.shape[1]))] * fresh,
-            compiler_params=params(),
-            cost_estimate=cost(2),
-            name="filter",
-        )(pos_out, decay_rate[None, :], skip_gain[None, :], places, forward, *more)
-
-    last_near, last_far, second_halves = spectra(middle, behind, *layers)
-
-    near, far = spectra(0, middle, second_halves)
+    last_near, last_far, second_halves = pl.pallas_call(
+        functools.partial(network_filter_kernel, middle),
+        in_specs=[in_vmem] * 10,
+        out_specs=[in_vmem] * 3,
+        out_shape=spectra,
+        scratch_shapes=spectra_bufs(behind) + [floats((feats.shape[0], hidden))],
+        compiler_params=params(),
+        cost_estimate=cost(2),
+        name="filter",
+    )(*weights, *layers)
+    near, far = pl.pallas_call(
+        functools.partial(filter_spectra, 0),
+        in_specs=[in_vmem] * 6,
+        out_specs=[in_vmem] * 2,
+        out_shape=arrays((total_len, middle), (total_len, middle)),
+        scratch_shapes=spectra_bufs(middle),
+        compiler_params=params(),
+        cost_estimate=cost(2),
+        name="filter",
+    )(*weights, second_halves)
     last_near, near = lax.optimization_barrier((last_near, near))
-    last_code, mixed, gates = pl.pallas_call(
+    last_code, behind_mixed, gates = pl.pallas_call(
         functools.partial(send_kernel, middle),
         in_specs=[in_vmem] * 6,
-        out_specs=[in_vmem, in_hbm, in_vmem],
-        out_shape=message(behind) + arrays((rows, width), dtype=jnp.bfloat16) + arrays((rows, middle)),
+        out_specs=[in_vmem] * 3,
+        out_shape=message(behind) + arrays((rows, behind), dtype=jnp.bfloat16) + arrays((rows, middle)),
         scratch_shapes=[
             floats((2, 3, rows, 128)),
             shorts((2, rows, behind)),
@@ -735,8 +755,6 @@
             floats((rows, behind)),
             floats((8, behind)),
             floats((16, 128)),
-            shorts((rows, behind)),
-            pltpu.SemaphoreType.DMA((2,)),
         ],
         compiler_params=params(),
         cost_estimate=cost(2),
@@ -745,11 +763,10 @@
     last_code = lax.ppermute(last_code, "ctx", pairs)
     right, own_bins, last_base, mixed = pl.pallas_call(
         own_kernel,
-        in_specs=[in_vmem] * 10 + [in_hbm],
+        in_specs=[in_vmem] * 11,
         out_specs=[in_vmem] * 3 + [in_hbm],
         out_shape=arrays((rows, width), (total_len, middle), (rows, behind))
         + arrays((rows, width), dtype=jnp.bfloat16),
-        input_output_aliases={10: 3},
         scratch_shapes=[
             floats((3, 8, width)),
             floats((2, 3, rows, 128)),
@@ -763,33 +780,30 @@
         compiler_params=params(),
         cost_estimate=cost(4),
         name="own",
-    )(projected, one_code, taps, near, last_near, forward, backward, one_driven, two_driven, gates, mixed)
-    mixed = pl.pallas_call(
-        lambda one_ref, two_ref, *refs: join_kernel((one_ref, two_ref), *refs[:5], *refs[6:]),
-        in_specs=[in_vmem] * 7 + [in_hbm],
-        out_specs=in_hbm,
-        out_shape=jax.ShapeDtypeStruct((rows, width), jnp.bfloat16),
-        input_output_aliases={7: 0},
+    )(projected, one_code, taps, near, last_near, forward, backward, one_driven, two_driven, gates, behind_mixed)
+    ahead_mixed = pl.pallas_call(
+        lambda one_ref, two_ref, *refs: join_kernel((one_ref, two_ref), *refs),
+        in_specs=[in_vmem] * 7,
+        out_specs=in_vmem,
+        out_shape=jax.ShapeDtypeStruct((rows, middle), jnp.bfloat16),
         scratch_shapes=[
             shorts((2, rows, middle)),
             floats((2, rows, middle)),
             shorts((2, 2 * rows, middle)),
             floats((rows, middle)),
             floats((4, rows, 128)),
-            shorts((rows, middle)),
-            floats((2, 16, 128)),
-            pltpu.SemaphoreType.DMA((3,)),
+            floats((16, 128)),
         ],
         compiler_params=params(),
         cost_estimate=cost(2),
         name="join",
-    )(one_code, two_code, far, own_bins, right, forward, backward, mixed)
+    )(one_code, two_code, far, own_bins, right, forward, backward)
     return pl.pallas_call(
         functools.partial(last_kernel, middle),
-        in_specs=[in_vmem] * 3 + [in_hbm],
+        in_specs=[in_vmem] * 4 + [in_hbm],
         out_specs=in_hbm,
         out_shape=jax.ShapeDtypeStruct((rows, width), jnp.bfloat16),
-        input_output_aliases={3: 0},
+        input_output_aliases={4: 0},
         scratch_shapes=[
             floats((4, rows, 128)),
             shorts((rows, behind)),
@@ -799,7 +813,7 @@
         compiler_params=params(),
         cost_estimate=cost(1),
         name="last",
-    )(last_code, last_base, right, mixed)
+    )(last_code, last_base, right, ahead_mixed, mixed)
 
 
 def turn_table(outer_ids, inner_ids, modulus):

time: 17.1 us -> 16.6 us (0.971)
  Pallas kernels: 11.7 us -> 10.9 us
  waiting for transfers between devices: 0.04 us -> 0.45 us
    pallas_call x1, Pallas kernels: 2.89 us -> 2.25 us  [one_way(): pl.pallas_call(lambda one_ref, two_ref, *refs: join_kernel((one_ref, two_...]
    ppermute x1, waiting for transfers between devices: 0.04 us -> 0.33 us  [one_way(): two_code = lax.ppermute(two_code, 'ctx', [(0, 1), (1, 0)])]
    pallas_call x3, Pallas kernels: 7.92 us -> 7.68 us  [the longest x1 3.77 us: one_way(): pl.pallas_call(own_kernel, in_specs=[in_vmem] * 11, out_specs=[in_vmem] *...]
  transfers between devices with their start and end apart: 3 -> 3, of which waited for: 0 -> 2; matrix products, arithmetic and copies ran while one was open for 0% -> 0% of each run, Pallas kernels for 64% -> 60%
where the time goes in v4:
time: 16.6 us; the launch traced here: 16.5 us
  Pallas kernels  10.9 us (66%)
  starting transfers between devices  4.87 us (29%)
  waiting for transfers between devices  0.45 us (3%)
  between operations  0.21 us (1%)
    pallas_call x1, Pallas kernels, one_way(): pl.pallas_call(own_kernel, in_specs=[in_vmem] * 11, out_specs=[in_vmem] *...  3.77 us
    pallas_call x1, Pallas kernels, one_way(): pl.pallas_call(functools.partial(filter_spectra, 0), in_specs=[in_vmem] *...  2.3 us
    pallas_call x1, Pallas kernels, one_way(): pl.pallas_call(lambda one_ref, two_ref, *refs: join_kernel((one_ref, two_...  2.25 us
    ppermute x1, starting transfers between devices, one_way(): one_code = lax.ppermute(one_code, 'ctx', [(0, 1), (1, 0)])  1.89 us
    ppermute x1, starting transfers between devices, one_way(): two_code = lax.ppermute(two_code, 'ctx', [(0, 1), (1, 0)])  1.69 us
    pallas_call x1, Pallas kernels, one_way(): pl.pallas_call(functools.partial(network_filter_kernel, middle), in_specs...  1.61 us
    ppermute x1, starting transfers between devices, one_way(): last_code = lax.ppermute(last_code, 'ctx', pairs)  1.29 us
    pallas_call x1, Pallas kernels, one_way(): pl.pallas_call(functools.partial(last_kernel, middle), in_specs=[in_vmem]...  0.84 us
  transfers between devices with their start and end apart: 3, of which 2 were waited for; matrix products, arithmetic and copies ran while one was open for 0% of the time, Pallas kernels for 60%

profile of v4, /device:TPU:6, one launch (start us, length us, event | category | flops | bytes accessed | tf_op | source)
XLA Modules:
  0.0 16.5 jit_solution(815484191470121193)
XLA Ops:
  0.0 1.9 %collective-permute-start.1 = (bf16[544,128]{1,0:T(8,128)(2,1)S(1)}, bf16[544,128]{1,0:T(8,128)(2,1)S(1)}, u32[]{:S(2)}, u32[]{:S(2)}) collective-permute-start(bf16[544,128]{1,0:T(8,128)(2,1)S(1)} %get-tuple-element.30), channel_id=1, source_target_pairs={{0,16},{16,0},{1,17},{17,1},{2,18},{18,2},{3,19},{19,3},{4,20},{20... | collective-permute-start | bytes 417800 | tf_op jit(solution)/shard_map/ppermute | solution.py:704
  2.0 0.0 copy-start.4
  2.0 0.0 copy-start.5
  2.0 0.0 copy-start.6
  2.0 0.0 copy-start.7
  2.0 0.0 copy-start.8
  2.0 0.0 copy-start.9
  2.0 0.0 copy-start.10
  2.0 0.0 copy-start.12
  2.1 1.7 %collective-permute-start.2 = (bf16[1296,128]{1,0:T(8,128)(2,1)S(1)}, bf16[1296,128]{1,0:T(8,128)(2,1)S(1)}, u32[]{:S(2)}, u32[]{:S(2)}) collective-permute-start(bf16[1296,128]{1,0:T(8,128)(2,1)S(1)} %get-tuple-element.39), channel_id=1, source_target_pairs={{0,16},{16,0},{1,17},{17,1},{2,18},{18,2},{3,19},{19,3},{4,20},{20... | collective-permute-start | bytes 995336 | tf_op jit(solution)/shard_map/ppermute | solution.py:722
  3.8 0.0 copy-done.5
  3.8 0.0 copy-done.6
  3.8 0.0 copy-done.7
  3.8 0.0 copy-done.8
  3.8 1.6 %filter.2 = (f32[256,512]{1,0:T(8,128)S(1)}, f32[256,512]{1,0:T(8,128)S(1)}, bf16[256,192]{1,0:T(8,128)(2,1)S(1)}) custom-call(f32[64,2048]{1,0:T(8,128)S(1)} %copy-done.1, f32[1,2048]{1,0:T(1,128)S(1)} %bitcast.9, f32[1,2048]{1,0:T(1,128)S(1)} %bitcast.11, f32[256,128]{1,0:T(8,128)S(1)} %copy-done.10, bf16[256,192]{1,0:T(8,128)(2,1)S(1)} %copy-done.9, ...), custom_call_target="tpu_custom_call" | custom-call | flops 2000000000 | bytes 6000000 | tf_op jit(solution)/shard_map/filter/pallas_call | solution.py:723
  5.5 0.0 copy-start.11
  5.5 2.3 %filter.3 = (f32[256,1536]{1,0:T(8,128)S(1)}, f32[256,1536]{1,0:T(8,128)S(1)}) custom-call(f32[64,2048]{1,0:T(8,128)S(1)} %copy-done.1, f32[1,2048]{1,0:T(1,128)S(1)} %bitcast.10, f32[1,2048]{1,0:T(1,128)S(1)} %bitcast.12, f32[256,128]{1,0:T(8,128)S(1)} %copy-done.10, bf16[256,192]{1,0:T(8,128)(2,1)S(1)} %copy-done.9, ...), custom_call_target="tpu_custom_call" | custom-call | flops 2000000000 | bytes 6000000 | tf_op jit(solution)/shard_map/filter/pallas_call | solution.py:733
  7.8 1.3 %collective-permute-start = (bf16[528,128]{1,0:T(8,128)(2,1)S(1)}, bf16[528,128]{1,0:T(8,128)(2,1)S(1)}, u32[]{:S(2)}, u32[]{:S(2)}) collective-permute-start(bf16[528,128]{1,0:T(8,128)(2,1)S(1)} %get-tuple-element.29), channel_id=1, source_target_pairs={{0,16},{1,17},{2,18},{3,19},{4,20},{5,21},{6,22},{7,23},{8,24},{9,... | collective-permute-start | bytes 405512 | tf_op jit(solution)/shard_map/ppermute | solution.py:763
  9.1 0.0 collective-permute-done.1.rims_ref.one_ref
  9.1 3.8 %own.1 = (f32[128,2048]{1,0:T(8,128)S(1)}, f32[256,1536]{1,0:T(8,128)S(1)}, f32[128,512]{1,0:T(8,128)S(1)}, bf16[128,2048]{1,0:T(8,128)(2,1)}) custom-call(bf16[3,128,2048]{2,1,0:T(8,128)(2,1)S(1)} %copy-done, bf16[544,128]{1,0:T(8,128)(2,1)S(1)} %collective-permute-done.1.rims_ref.one_ref, f32[3,7,2048]{2,1,0:T(8,128)S(1)} %bitcast.8, ...), custom_call_target="tpu_custom_call" | custom-call | flops 4000000000 | bytes 12000000 | tf_op jit(solution)/shard_map/own/pallas_call | solution.py:764
  12.9 0.3 %collective-permute-done.2.two_ref = bf16[1296,128]{1,0:T(8,128)(2,1)S(1)} collective-permute-done((bf16[1296,128]{1,0:T(8,128)(2,1)S(1)}, bf16[1296,128]{1,0:T(8,128)(2,1)S(1)}, u32[]{:S(2)}, u32[]{:S(2)}) %collective-permute-start.2) | collective-permute-done | bytes 331808 | tf_op jit(solution)/shard_map/ppermute | solution.py:722
  13.2 2.3 %join.1.ahead_ref = bf16[128,1536]{1,0:T(8,128)(2,1)S(1)} custom-call(bf16[544,128]{1,0:T(8,128)(2,1)S(1)} %collective-permute-done.1.rims_ref.one_ref, bf16[1296,128]{1,0:T(8,128)(2,1)S(1)} %collective-permute-done.2.two_ref, f32[256,1536]{1,0:T(8,128)S(1)} %get-tuple-element.40.refs_0_, f32[256,1536]{1,0:T(8,128)S(1)} %get-tuple-element.41.refs_1_, ...), custom_call_target="tpu_custom_call" | custom-call | flops 2000000000 | bytes 6000000 | tf_op jit(solution)/shard_map/join/pallas_call | solution.py:784
  15.5 0.1 collective-permute-done.coded_ref
  15.6 0.8 %last.1 = bf16[128,2048]{1,0:T(8,128)(2,1)} custom-call(bf16[528,128]{1,0:T(8,128)(2,1)S(1)} %collective-permute-done.coded_ref, f32[128,512]{1,0:T(8,128)S(1)} %get-tuple-element.37.base_ref, f32[128,2048]{1,0:T(8,128)S(1)} %get-tuple-element.38.refs_2_.right_ref, bf16[128,1536]{1,0:T(8,128)(2,1)S(1)} %join.1.ahead_ref, ...), custom_call_target="tpu_custom_call", output_to_operand_aliasing={{}: (4, {})} | custom-call | flops 1000000000 | bytes 3000000 | tf_op jit(solution)/shard_map/last/pallas_call | solution.py:801
  (16 shorter events, 0.1 us)
Async XLA Ops:
  0.0 1.9 %copy-start = (bf16[3,128,2048]{2,1,0:T(8,128)(2,1)S(1)}, bf16[3,128,2048]{2,1,0:T(8,128)(2,1)}, u32[]{:S(2)}) copy-start(bf16[3,128,2048]{2,1,0:T(8,128)(2,1)} %projected_ref.7) | copy-start | bytes 4718596
  0.0 1.9 %copy-start.2 = (f32[7,3,2048]{2,0,1:T(8,128)S(1)}, f32[7,3,2048]{2,0,1:T(8,128)}, u32[]{:S(2)}) copy-start(f32[7,3,2048]{2,0,1:T(8,128)} %param.14) | copy-start | bytes 516100
  0.0 9.1 %collective-permute-start.1 = (bf16[544,128]{1,0:T(8,128)(2,1)S(1)}, bf16[544,128]{1,0:T(8,128)(2,1)S(1)}, u32[]{:S(2)}, u32[]{:S(2)}) collective-permute-start(bf16[544,128]{1,0:T(8,128)(2,1)S(1)} %get-tuple-element.30), channel_id=1, source_target_pairs={{0,16},{16,0},{1,17},{17,1},{2,18},{18,2},{3,19},{19,3},{4,20},{20... | collective-permute-start | bytes 417800 | tf_op jit(solution)/shard_map/ppermute | solution.py:704
  1.9 1.8 %copy-start.1 = (f32[64,2048]{1,0:T(8,128)S(1)}, f32[64,2048]{1,0:T(8,128)}, u32[]{:S(2)}) copy-start(f32[64,2048]{1,0:T(8,128)} %out_ref.1) | copy-start | bytes 1572868
  1.9 1.8 %copy-start.3 = (f32[64,64]{1,0:T(8,128)S(1)}, f32[64,64]{1,0:T(8,128)}, u32[]{:S(2)}) copy-start(f32[64,64]{1,0:T(8,128)} %refs_9_.1) | copy-start | bytes 49156
  2.0 1.8 %copy-start.4 = (f32[33,64]{1,0:T(8,128)S(1)}, f32[33,64]{1,0:T(8,128)}, u32[]{:S(2)}) copy-start(f32[33,64]{1,0:T(8,128)} %refs_6_.1) | copy-start | bytes 25348
  2.0 1.8 %copy-start.5 = (f32[2048]{0:T(1024)S(1)}, f32[2048]{0:T(1024)}, u32[]{:S(2)}) copy-start(f32[2048]{0:T(1024)} %param.20) | copy-start | bytes 24580
  2.0 1.8 %copy-start.6 = (f32[2048]{0:T(1024)S(1)}, f32[2048]{0:T(1024)}, u32[]{:S(2)}) copy-start(f32[2048]{0:T(1024)} %param.21) | copy-start | bytes 24580
  2.0 1.8 %copy-start.7 = (f32[64]{0:T(128)S(1)}, f32[64]{0:T(128)}, u32[]{:S(2)}) copy-start(f32[64]{0:T(128)} %param.16) | copy-start | bytes 772
  2.0 1.8 %copy-start.8 = (f32[64]{0:T(128)S(1)}, f32[64]{0:T(128)}, u32[]{:S(2)}) copy-start(f32[64]{0:T(128)} %param.17) | copy-start | bytes 772
  2.0 1.8 %copy-start.9 = (bf16[256,192]{1,0:T(8,128)(2,1)S(1)}, bf16[256,192]{1,0:T(8,128)(2,1)}, u32[]{:S(2)}) copy-start(bf16[256,192]{1,0:T(8,128)(2,1)} %constant.9.clone.refs_4_.forward_ref.refs_3_) | copy-start | bytes 294916
  2.0 1.8 %copy-start.10 = (f32[256,128]{1,0:T(8,128)S(1)}, f32[256,128]{1,0:T(8,128)}, u32[]{:S(2)}) copy-start(f32[256,128]{1,0:T(8,128)} %constant.8.clone.refs_3_.places_ref) | copy-start | bytes 393220
  2.0 1.8 %copy-start.12 = (f32[40,256]{1,0:T(8,128)S(1)}, f32[40,256]{1,0:T(8,128)}, u32[]{:S(2)}) copy-start(f32[40,256]{1,0:T(8,128)} %constant.10.clone.refs_5_) | copy-start | bytes 122884
  2.1 11.2 %collective-permute-start.2 = (bf16[1296,128]{1,0:T(8,128)(2,1)S(1)}, bf16[1296,128]{1,0:T(8,128)(2,1)S(1)}, u32[]{:S(2)}, u32[]{:S(2)}) collective-permute-start(bf16[1296,128]{1,0:T(8,128)(2,1)S(1)} %get-tuple-element.39), channel_id=1, source_target_pairs={{0,16},{16,0},{1,17},{17,1},{2,18},{18,2},{3,19},{19,3},{4,20},{20... | collective-permute-start | bytes 995336 | tf_op jit(solution)/shard_map/ppermute | solution.py:722
  5.5 2.3 %copy-start.11 = (bf16[128,384]{1,0:T(8,128)(2,1)S(1)}, bf16[128,384]{1,0:T(8,128)(2,1)}, u32[]{:S(2)}) copy-start(bf16[128,384]{1,0:T(8,128)(2,1)} %constant.11.clone.backward_ref.refs_4_) | copy-start | bytes 294916
  7.8 7.8 %collective-permute-start = (bf16[528,128]{1,0:T(8,128)(2,1)S(1)}, bf16[528,128]{1,0:T(8,128)(2,1)S(1)}, u32[]{:S(2)}, u32[]{:S(2)}) collective-permute-start(bf16[528,128]{1,0:T(8,128)(2,1)S(1)} %get-tuple-element.29), channel_id=1, source_target_pairs={{0,16},{1,17},{2,18},{3,19},{4,20},{5,21},{6,22},{7,23},{8,24},{9,... | collective-permute-start | bytes 405512 | tf_op jit(solution)/shard_map/ppermute | solution.py:763

commit v5 on v4

--- a/solution.py
+++ b/solution.py
@@ -405,7 +405,7 @@
             total = total + pltpu.roll(total, step, 0)
         scale_buf[:, cols] = 1.0 / jnp.sqrt(total + 1e-05)
 
-    each_tile(width // 128, 4, decay)
+    each_tile(width // 128, 12, decay)
     forward_dots(forward_ref, parts_buf, spec_buf)
 
     def shape(tile, _):
@@ -423,7 +423,7 @@
                 near_ref[at * half + row : at * half + row + 16, cols] = low[at]
                 far_ref[at * half + row : at * half + row + 16, cols] = high[at] + turned[at]
 
-    each_tile(width // 128, 4, shape)
+    each_tile(width // 128, 12, shape)
 
 
 def driven_parts(driven, parts_buf, cols):
@@ -438,10 +438,13 @@
 
 
 def send_kernel(
-    first, projected_ref, taps_ref, near_ref, far_ref, forward_ref, backward_ref, coded_ref, mixed_ref, gates_ref,
-    strided_buf, parts_buf, spec_buf, bins_buf, right_buf, conv_buf, peak_buf, levels_buf,
+    first, projected_ref, taps_ref, near_ref, far_ref, forward_ref, backward_ref, ahead_near_ref, one_ref, two_ref,
+    coded_ref, mixed_ref, gates_ref, ahead_bins_ref,
+    strided_buf, parts_buf, spec_buf, bins_buf, right_buf, conv_buf, peak_buf, levels_buf, ahead_parts_buf,
+    ahead_spec_buf,
 ):
     rows, width = right_buf.shape
+    half = rows // 2
     tiles = width // 128
 
     @pl.when(lax.axis_index("ctx") == 0)
@@ -487,11 +490,28 @@
             put_rows(gates_ref, cols, short_sum(parts, None, taps_ref, 1, cols))
 
         each_tile(first // 128, strided_buf.shape[0], gate)
+        start = 0
+        for ref in (one_ref, two_ref):
+
+            def recall(tile, _, ref=ref, start=start):
+                for row in range(0, rows, 16):
+                    value = ref[row : row + 16, tile_lanes(tile)]
+                    put_halves(ahead_parts_buf, row // half, row % half, tile_lanes(tile, start), value)
+
+            each_tile(ref.shape[1] // 128, 4, recall)
+            start += ref.shape[1]
+        forward_dots(forward_ref, ahead_parts_buf, ahead_spec_buf)
+        each_tile(
+            first // 128, 4,
+            lambda tile, _: filtered(
+                ahead_spec_buf, ahead_near_ref, ahead_bins_ref, tile_lanes(tile), tile_lanes(tile)
+            ),
+        )
         mix_tiles(mix, tiles, mixed_ref, strided_buf.at[:, 0])
 
 
 def own_kernel(
-    projected_ref, rims_ref, taps_ref, near_ref, last_near_ref, forward_ref, backward_ref, one_ref, two_ref, gates_ref,
+    projected_ref, rims_ref, taps_ref, near_ref, last_near_ref, forward_ref, backward_ref, gates_ref, ahead_bins_ref,
     behind_ref, right_ref, bins_ref, base_ref, mixed_ref,
     rims_buf, strided_buf, parts_buf, spec_buf, bins_buf, conv_buf, mixed_buf, sems,
 ):
@@ -505,21 +525,7 @@
         tiles = middle // 128
         behind = pltpu.make_async_copy(behind_ref, mixed_ref.at[:, pl.ds(middle, width - middle)], sems.at[0])
         behind.start()
-        start = 0
-        for ref in (one_ref, two_ref):
-
-            def recall(tile, _, ref=ref, start=start):
-                for row in range(0, rows, 16):
-                    value = ref[row : row + 16, tile_lanes(tile)]
-                    put_halves(parts_buf, row // half, row % half, tile_lanes(tile, start), value)
-
-            each_tile(ref.shape[1] // 128, 4, recall)
-            start += ref.shape[1]
-        forward_dots(forward_ref, parts_buf.at[:, :, 0:middle], spec_buf.at[:, :, 0:middle])
-        each_tile(
-            tiles, 4, lambda tile, _: filtered(spec_buf, near_ref, bins_buf, tile_lanes(tile), tile_lanes(tile))
-        )
-        backward_dots(backward_ref, bins_buf, conv_buf)
+        backward_dots(backward_ref, ahead_bins_ref, conv_buf)
 
         def mix(tile):
             cols = tile_lanes(tile)
@@ -565,7 +571,7 @@
                 put_bins(bins_buf, row, cols, folded_products(spec_buf, last_near_ref, row, there, cols))
 
         each_tile(behind // 128, 4, finish)
-        backward_dots(backward_ref, bins_buf.at[:, :, 0:behind], base_ref)
+        backward_dots(backward_ref, bins_buf, base_ref)
 
 
 def mix_tiles(mix, tiles, mixed_ref, strided_buf):
@@ -741,11 +747,14 @@
         name="filter",
     )(*weights, second_halves)
     last_near, near = lax.optimization_barrier((last_near, near))
-    last_code, behind_mixed, gates = pl.pallas_call(
+    last_code, behind_mixed, gates, ahead_bins = pl.pallas_call(
         functools.partial(send_kernel, middle),
-        in_specs=[in_vmem] * 6,
-        out_specs=[in_vmem] * 3,
-        out_shape=message(behind) + arrays((rows, behind), dtype=jnp.bfloat16) + arrays((rows, middle)),
+        in_specs=[in_vmem] * 9,
+        out_specs=[in_vmem] * 4,
+        out_shape=message(behind)
+        + arrays((rows, behind), dtype=jnp.bfloat16)
+        + arrays((rows, middle))
+        + arrays((2, 2 * rows, middle), dtype=jnp.bfloat16),
         scratch_shapes=[
             floats((2, 3, rows, 128)),
             shorts((2, rows, behind)),
@@ -755,15 +764,17 @@
             floats((rows, behind)),
             floats((8, behind)),
             floats((16, 128)),
+            shorts((2, rows, middle)),
+            floats((2, rows, middle)),
         ],
         compiler_params=params(),
         cost_estimate=cost(2),
         name="send",
-    )(projected, taps, last_near, last_far, forward, backward)
+    )(projected, taps, last_near, last_far, forward, backward, near, one_driven, two_driven)
     last_code = lax.ppermute(last_code, "ctx", pairs)
     right, own_bins, last_base, mixed = pl.pallas_call(
         own_kernel,
-        in_specs=[in_vmem] * 11,
+        in_specs=[in_vmem] * 10,
         out_specs=[in_vmem] * 3 + [in_hbm],
         out_shape=arrays((rows, width), (total_len, middle), (rows, behind))
         + arrays((rows, width), dtype=jnp.bfloat16),
@@ -772,7 +783,7 @@
             floats((2, 3, rows, 128)),
             shorts((2, rows, width)),
             floats((2, rows, width)),
-            shorts((2, 2 * rows, middle)),
+            shorts((2, 2 * rows, behind)),
             floats((rows, middle)),
             shorts((rows, middle)),
             pltpu.SemaphoreType.DMA((2,)),
@@ -780,7 +791,7 @@
         compiler_params=params(),
         cost_estimate=cost(4),
         name="own",
-    )(projected, one_code, taps, near, last_near, forward, backward, one_driven, two_driven, gates, behind_mixed)
+    )(projected, one_code, taps, near, last_near, forward, backward, gates, ahead_bins, behind_mixed)
     ahead_mixed = pl.pallas_call(
         lambda one_ref, two_ref, *refs: join_kernel((one_ref, two_ref), *refs),
         in_specs=[in_vmem] * 7,

time: 16.6 us -> 16.6 us (level)
  Pallas kernels: 10.9 us -> 9.98 us
  waiting for transfers between devices: 0.45 us -> 1.33 us
    pallas_call x1, Pallas kernels: 2.3 us -> 1.46 us  [one_way(): pl.pallas_call(functools.partial(filter_spectra, 0), in_specs=[in_vmem] *...]
    ppermute x1, waiting for transfers between devices: 0.33 us -> 0.93 us  [one_way(): two_code = lax.ppermute(two_code, 'ctx', [(0, 1), (1, 0)])]
    ppermute x1, waiting for transfers between devices: 0.12 us -> 0.39 us  [one_way(): last_code = lax.ppermute(last_code, 'ctx', pairs)]
  transfers between devices with their start and end apart: 3 -> 3, of which waited for: 2 -> 2; matrix products, arithmetic and copies ran while one was open for 0% -> 0% of each run, Pallas kernels for 60% -> 55%
where the time goes in v5:
time: 16.6 us; the launch traced here: 16.5 us
  Pallas kernels  9.98 us (60%)
  starting transfers between devices  4.87 us (29%)
  waiting for transfers between devices  1.33 us (8%)
  between operations  0.21 us (1%)
    pallas_call x1, Pallas kernels, one_way(): pl.pallas_call(own_kernel, in_specs=[in_vmem] * 10, out_specs=[in_vmem] *...  3.78 us
    pallas_call x1, Pallas kernels, one_way(): pl.pallas_call(lambda one_ref, two_ref, *refs: join_kernel((one_ref, two_...  2.22 us
    ppermute x1, starting transfers between devices, one_way(): one_code = lax.ppermute(one_code, 'ctx', [(0, 1), (1, 0)])  1.89 us
    ppermute x1, starting transfers between devices, one_way(): two_code = lax.ppermute(two_code, 'ctx', [(0, 1), (1, 0)])  1.69 us
    pallas_call x1, Pallas kernels, one_way(): pl.pallas_call(functools.partial(network_filter_kernel, middle), in_specs...  1.61 us
    pallas_call x1, Pallas kernels, one_way(): pl.pallas_call(functools.partial(filter_spectra, 0), in_specs=[in_vmem] *...  1.46 us
    ppermute x1, starting transfers between devices, one_way(): last_code = lax.ppermute(last_code, 'ctx', pairs)  1.29 us
    ppermute x1, waiting for transfers between devices, one_way(): two_code = lax.ppermute(two_code, 'ctx', [(0, 1), (1, 0)])  0.93 us
  transfers between devices with their start and end apart: 3, of which 2 were waited for; matrix products, arithmetic and copies ran while one was open for 0% of the time, Pallas kernels for 55%

profile of v5, /device:TPU:6, one launch (start us, length us, event | category | flops | bytes accessed | tf_op | source)
XLA Modules:
  0.0 16.5 jit_solution(14784826114703511530)
XLA Ops:
  0.0 1.9 %collective-permute-start.1 = (bf16[544,128]{1,0:T(8,128)(2,1)S(1)}, bf16[544,128]{1,0:T(8,128)(2,1)S(1)}, u32[]{:S(2)}, u32[]{:S(2)}) collective-permute-start(bf16[544,128]{1,0:T(8,128)(2,1)S(1)} %get-tuple-element.35), channel_id=1, source_target_pairs={{0,16},{16,0},{1,17},{17,1},{2,18},{18,2},{3,19},{19,3},{4,20},{20... | collective-permute-start | bytes 417800 | tf_op jit(solution)/shard_map/ppermute | solution.py:710
  2.0 0.0 copy-start.4
  2.0 0.0 copy-start.5
  2.0 0.0 copy-start.6
  2.0 0.0 copy-start.7
  2.0 0.0 copy-start.8
  2.0 0.0 copy-start.9
  2.0 0.0 copy-start.10
  2.0 0.0 copy-start.12
  2.1 1.7 %collective-permute-start.2 = (bf16[1296,128]{1,0:T(8,128)(2,1)S(1)}, bf16[1296,128]{1,0:T(8,128)(2,1)S(1)}, u32[]{:S(2)}, u32[]{:S(2)}) collective-permute-start(bf16[1296,128]{1,0:T(8,128)(2,1)S(1)} %get-tuple-element.41), channel_id=1, source_target_pairs={{0,16},{16,0},{1,17},{17,1},{2,18},{18,2},{3,19},{19,3},{4,20},{20... | collective-permute-start | bytes 995336 | tf_op jit(solution)/shard_map/ppermute | solution.py:728
  3.8 0.0 copy-done.5
  3.8 0.0 copy-done.6
  3.8 0.0 copy-done.7
  3.8 0.0 copy-done.8
  3.8 1.6 %filter.2 = (f32[256,512]{1,0:T(8,128)S(1)}, f32[256,512]{1,0:T(8,128)S(1)}, bf16[256,192]{1,0:T(8,128)(2,1)S(1)}) custom-call(f32[64,2048]{1,0:T(8,128)S(1)} %copy-done.1, f32[1,2048]{1,0:T(1,128)S(1)} %bitcast.9, f32[1,2048]{1,0:T(1,128)S(1)} %bitcast.11, f32[256,128]{1,0:T(8,128)S(1)} %copy-done.10, bf16[256,192]{1,0:T(8,128)(2,1)S(1)} %copy-done.9, ...), custom_call_target="tpu_custom_call" | custom-call | flops 2000000000 | bytes 6000000 | tf_op jit(solution)/shard_map/filter/pallas_call | solution.py:729
  5.5 0.0 copy-start.11
  5.5 1.5 %filter.3 = (f32[256,1536]{1,0:T(8,128)S(1)}, f32[256,1536]{1,0:T(8,128)S(1)}) custom-call(f32[64,2048]{1,0:T(8,128)S(1)} %copy-done.1, f32[1,2048]{1,0:T(1,128)S(1)} %bitcast.10, f32[1,2048]{1,0:T(1,128)S(1)} %bitcast.12, f32[256,128]{1,0:T(8,128)S(1)} %copy-done.10, bf16[256,192]{1,0:T(8,128)(2,1)S(1)} %copy-done.9, ...), custom_call_target="tpu_custom_call" | custom-call | flops 2000000000 | bytes 6000000 | tf_op jit(solution)/shard_map/filter/pallas_call | solution.py:739
  7.0 1.3 %collective-permute-start = (bf16[528,128]{1,0:T(8,128)(2,1)S(1)}, bf16[528,128]{1,0:T(8,128)(2,1)S(1)}, u32[]{:S(2)}, u32[]{:S(2)}) collective-permute-start(bf16[528,128]{1,0:T(8,128)(2,1)S(1)} %get-tuple-element.34), channel_id=1, source_target_pairs={{0,16},{1,17},{2,18},{3,19},{4,20},{5,21},{6,22},{7,23},{8,24},{9,... | collective-permute-start | bytes 405512 | tf_op jit(solution)/shard_map/ppermute | solution.py:774
  8.3 0.0 collective-permute-done.1.rims_ref.one_ref
  8.3 3.8 %own.1 = (f32[128,2048]{1,0:T(8,128)S(1)}, f32[256,1536]{1,0:T(8,128)S(1)}, f32[128,512]{1,0:T(8,128)S(1)}, bf16[128,2048]{1,0:T(8,128)(2,1)}) custom-call(bf16[3,128,2048]{2,1,0:T(8,128)(2,1)S(1)} %copy-done, bf16[544,128]{1,0:T(8,128)(2,1)S(1)} %collective-permute-done.1.rims_ref.one_ref, f32[3,7,2048]{2,1,0:T(8,128)S(1)} %bitcast.8, ...), custom_call_target="tpu_custom_call" | custom-call | flops 4000000000 | bytes 12000000 | tf_op jit(solution)/shard_map/own/pallas_call | solution.py:775
  12.1 0.9 %collective-permute-done.2.two_ref = bf16[1296,128]{1,0:T(8,128)(2,1)S(1)} collective-permute-done((bf16[1296,128]{1,0:T(8,128)(2,1)S(1)}, bf16[1296,128]{1,0:T(8,128)(2,1)S(1)}, u32[]{:S(2)}, u32[]{:S(2)}) %collective-permute-start.2) | collective-permute-done | bytes 331808 | tf_op jit(solution)/shard_map/ppermute | solution.py:728
  13.0 2.2 %join.1.ahead_ref = bf16[128,1536]{1,0:T(8,128)(2,1)S(1)} custom-call(bf16[544,128]{1,0:T(8,128)(2,1)S(1)} %collective-permute-done.1.rims_ref.one_ref, bf16[1296,128]{1,0:T(8,128)(2,1)S(1)} %collective-permute-done.2.two_ref, f32[256,1536]{1,0:T(8,128)S(1)} %get-tuple-element.42.refs_0_, f32[256,1536]{1,0:T(8,128)S(1)} %get-tuple-element.43.refs_1_, ...), custom_call_target="tpu_custom_call" | custom-call | flops 2000000000 | bytes 6000000 | tf_op jit(solution)/shard_map/join/pallas_call | solution.py:795
  15.2 0.4 %collective-permute-done.coded_ref = bf16[528,128]{1,0:T(8,128)(2,1)S(1)} collective-permute-done((bf16[528,128]{1,0:T(8,128)(2,1)S(1)}, bf16[528,128]{1,0:T(8,128)(2,1)S(1)}, u32[]{:S(2)}, u32[]{:S(2)}) %collective-permute-start) | collective-permute-done | bytes 135200 | tf_op jit(solution)/shard_map/ppermute | solution.py:774
  15.6 0.8 %last.1 = bf16[128,2048]{1,0:T(8,128)(2,1)} custom-call(bf16[528,128]{1,0:T(8,128)(2,1)S(1)} %collective-permute-done.coded_ref, f32[128,512]{1,0:T(8,128)S(1)} %get-tuple-element.39.base_ref, f32[128,2048]{1,0:T(8,128)S(1)} %get-tuple-element.40.refs_2_.right_ref, bf16[128,1536]{1,0:T(8,128)(2,1)S(1)} %join.1.ahead_ref, ...), custom_call_target="tpu_custom_call", output_to_operand_aliasing={{}: (4, {})} | custom-call | flops 1000000000 | bytes 3000000 | tf_op jit(solution)/shard_map/last/pallas_call | solution.py:812
  (16 shorter events, 0.1 us)
Async XLA Ops:
  0.0 1.9 %copy-start = (bf16[3,128,2048]{2,1,0:T(8,128)(2,1)S(1)}, bf16[3,128,2048]{2,1,0:T(8,128)(2,1)}, u32[]{:S(2)}) copy-start(bf16[3,128,2048]{2,1,0:T(8,128)(2,1)} %projected_ref.7) | copy-start | bytes 4718596
  0.0 1.9 %copy-start.2 = (f32[7,3,2048]{2,0,1:T(8,128)S(1)}, f32[7,3,2048]{2,0,1:T(8,128)}, u32[]{:S(2)}) copy-start(f32[7,3,2048]{2,0,1:T(8,128)} %param.14) | copy-start | bytes 516100
  0.0 8.2 %collective-permute-start.1 = (bf16[544,128]{1,0:T(8,128)(2,1)S(1)}, bf16[544,128]{1,0:T(8,128)(2,1)S(1)}, u32[]{:S(2)}, u32[]{:S(2)}) collective-permute-start(bf16[544,128]{1,0:T(8,128)(2,1)S(1)} %get-tuple-element.35), channel_id=1, source_target_pairs={{0,16},{16,0},{1,17},{17,1},{2,18},{18,2},{3,19},{19,3},{4,20},{20... | collective-permute-start | bytes 417800 | tf_op jit(solution)/shard_map/ppermute | solution.py:710
  1.9 1.8 %copy-start.1 = (f32[64,2048]{1,0:T(8,128)S(1)}, f32[64,2048]{1,0:T(8,128)}, u32[]{:S(2)}) copy-start(f32[64,2048]{1,0:T(8,128)} %out_ref.1) | copy-start | bytes 1572868
  1.9 1.8 %copy-start.3 = (f32[64,64]{1,0:T(8,128)S(1)}, f32[64,64]{1,0:T(8,128)}, u32[]{:S(2)}) copy-start(f32[64,64]{1,0:T(8,128)} %refs_9_.1) | copy-start | bytes 49156
  2.0 1.8 %copy-start.4 = (f32[33,64]{1,0:T(8,128)S(1)}, f32[33,64]{1,0:T(8,128)}, u32[]{:S(2)}) copy-start(f32[33,64]{1,0:T(8,128)} %refs_6_.1) | copy-start | bytes 25348
  2.0 1.8 %copy-start.5 = (f32[2048]{0:T(1024)S(1)}, f32[2048]{0:T(1024)}, u32[]{:S(2)}) copy-start(f32[2048]{0:T(1024)} %param.20) | copy-start | bytes 24580
  2.0 1.8 %copy-start.6 = (f32[2048]{0:T(1024)S(1)}, f32[2048]{0:T(1024)}, u32[]{:S(2)}) copy-start(f32[2048]{0:T(1024)} %param.21) | copy-start | bytes 24580
  2.0 1.8 %copy-start.7 = (f32[64]{0:T(128)S(1)}, f32[64]{0:T(128)}, u32[]{:S(2)}) copy-start(f32[64]{0:T(128)} %param.16) | copy-start | bytes 772
  2.0 1.8 %copy-start.8 = (f32[64]{0:T(128)S(1)}, f32[64]{0:T(128)}, u32[]{:S(2)}) copy-start(f32[64]{0:T(128)} %param.17) | copy-start | bytes 772
  2.0 1.8 %copy-start.9 = (bf16[256,192]{1,0:T(8,128)(2,1)S(1)}, bf16[256,192]{1,0:T(8,128)(2,1)}, u32[]{:S(2)}) copy-start(bf16[256,192]{1,0:T(8,128)(2,1)} %constant.9.clone.refs_4_.forward_ref.refs_3_) | copy-start | bytes 294916
  2.0 1.8 %copy-start.10 = (f32[256,128]{1,0:T(8,128)S(1)}, f32[256,128]{1,0:T(8,128)}, u32[]{:S(2)}) copy-start(f32[256,128]{1,0:T(8,128)} %constant.8.clone.refs_3_.places_ref) | copy-start | bytes 393220
  2.0 1.8 %copy-start.12 = (f32[40,256]{1,0:T(8,128)S(1)}, f32[40,256]{1,0:T(8,128)}, u32[]{:S(2)}) copy-start(f32[40,256]{1,0:T(8,128)} %constant.10.clone.refs_5_) | copy-start | bytes 122884
  2.1 10.9 %collective-permute-start.2 = (bf16[1296,128]{1,0:T(8,128)(2,1)S(1)}, bf16[1296,128]{1,0:T(8,128)(2,1)S(1)}, u32[]{:S(2)}, u32[]{:S(2)}) collective-permute-start(bf16[1296,128]{1,0:T(8,128)(2,1)S(1)} %get-tuple-element.41), channel_id=1, source_target_pairs={{0,16},{16,0},{1,17},{17,1},{2,18},{18,2},{3,19},{19,3},{4,20},{20... | collective-permute-start | bytes 995336 | tf_op jit(solution)/shard_map/ppermute | solution.py:728
  5.5 1.5 %copy-start.11 = (bf16[128,384]{1,0:T(8,128)(2,1)S(1)}, bf16[128,384]{1,0:T(8,128)(2,1)}, u32[]{:S(2)}) copy-start(bf16[128,384]{1,0:T(8,128)(2,1)} %constant.11.clone.backward_ref.refs_4_) | copy-start | bytes 294916
  7.0 8.6 %collective-permute-start = (bf16[528,128]{1,0:T(8,128)(2,1)S(1)}, bf16[528,128]{1,0:T(8,128)(2,1)S(1)}, u32[]{:S(2)}, u32[]{:S(2)}) collective-permute-start(bf16[528,128]{1,0:T(8,128)(2,1)S(1)} %get-tuple-element.34), channel_id=1, source_target_pairs={{0,16},{1,17},{2,18},{3,19},{4,20},{5,21},{6,22},{7,23},{8,24},{9,... | collective-permute-start | bytes 405512 | tf_op jit(solution)/shard_map/ppermute | solution.py:774

commit v6 on v5

--- a/solution.py
+++ b/solution.py
@@ -205,6 +205,10 @@
 
 def tile_rows(tile, row, count=16):
     return pl.ds(pl.multiple_of(tile * 128 + row, 16), count)
+
+
+def natural_tile(ref, cols, buf):
+    return natural_rows([ref[at : at + 16, cols] for at in range(0, ref.shape[0], 16)], buf)
 
 
 def place_level(peak, tile, peak_buf, levels_buf, levels_first):
@@ -467,13 +471,14 @@
         )
         backward_dots(backward_ref, bins_buf, conv_buf)
 
-        def peaks(tile, _):
+        def peaks(tile, number):
             cols = tile_lanes(tile)
+            conv_buf[:, cols] = natural_tile(conv_buf, cols, strided_buf.at[number, 0])
             peak_buf[:, cols] = functools.reduce(
                 jnp.maximum, [jnp.abs(conv_buf[row : row + 8, cols]) for row in range(0, rows, 8)]
             )
 
-        each_tile(tiles, 4, peaks)
+        each_tile(tiles, strided_buf.shape[0], peaks)
         code_tiles(tiles, rows, coded_ref, conv_buf, peak_buf, levels_buf)
         each_tile(
             tiles, 4, lambda tile, _: filtered(spec_buf, near_ref, bins_buf, tile_lanes(tile), tile_lanes(tile))
@@ -512,7 +517,7 @@
 
 def own_kernel(
     projected_ref, rims_ref, taps_ref, near_ref, last_near_ref, forward_ref, backward_ref, gates_ref, ahead_bins_ref,
-    behind_ref, right_ref, bins_ref, base_ref, mixed_ref,
+    behind_ref, right_ref, bins_ref, base_ref, last_right_ref, mixed_ref,
     rims_buf, strided_buf, parts_buf, spec_buf, bins_buf, conv_buf, mixed_buf, sems,
 ):
     rows, width = right_ref.shape
@@ -573,6 +578,13 @@
         each_tile(behind // 128, 4, finish)
         backward_dots(backward_ref, bins_buf, base_ref)
 
+        def reorder(tile, number):
+            cols = tile_lanes(tile)
+            base_ref[:, cols] = natural_tile(base_ref, cols, strided_buf.at[number, 0])
+            last_right_ref[:, cols] = natural_tile(right_ref, tile_lanes(tile, middle), strided_buf.at[number, 1])
+
+        each_tile(behind // 128, strided_buf.shape[0], reorder)
+
 
 def mix_tiles(mix, tiles, mixed_ref, strided_buf):
     def one(tile, number):
@@ -631,7 +643,7 @@
 
 
 def last_kernel(
-    first, coded_ref, base_ref, right_ref, ahead_ref, _, mixed_ref, strided_buf, buf, levels_buf, sems
+    first, coded_ref, base_ref, right_ref, ahead_ref, _, mixed_ref, buf, levels_buf, sems
 ):
     rows, width = base_ref.shape
     tiles = width // 128
@@ -642,15 +654,14 @@
         ahead.start()
         read_levels(coded_ref, levels_buf, tiles, rows)
 
-        def mix(tile):
+        def mix(tile, _):
+            cols = tile_lanes(tile)
             decode = decoder(levels_buf, tile)
-            return [
-                right_ref[at : at + 16, tile_lanes(tile, first)]
-                * (decode(coded_ref[tile_rows(tile, at), :]) + base_ref[at : at + 16, tile_lanes(tile)])
-                for at in range(0, rows, 16)
-            ]
-
-        mix_tiles(mix, tiles, buf, strided_buf)
+            for at in range(0, rows, 16):
+                conv = decode(coded_ref[tile_rows(tile, at), :]) + base_ref[at : at + 16, cols]
+                buf[at : at + 16, cols] = (right_ref[at : at + 16, cols] * conv).astype(jnp.bfloat16)
+
+        each_tile(tiles, 4, mix)
         behind = pltpu.make_async_copy(buf, mixed_ref.at[:, pl.ds(first, width)], sems.at[1])
         behind.start()
         behind.wait()
@@ -772,11 +783,11 @@
         name="send",
     )(projected, taps, last_near, last_far, forward, backward, near, one_driven, two_driven)
     last_code = lax.ppermute(last_code, "ctx", pairs)
-    right, own_bins, last_base, mixed = pl.pallas_call(
+    right, own_bins, last_base, last_right, mixed = pl.pallas_call(
         own_kernel,
         in_specs=[in_vmem] * 10,
-        out_specs=[in_vmem] * 3 + [in_hbm],
-        out_shape=arrays((rows, width), (total_len, middle), (rows, behind))
+        out_specs=[in_vmem] * 4 + [in_hbm],
+        out_shape=arrays((rows, width), (total_len, middle), (rows, behind), (rows, behind))
         + arrays((rows, width), dtype=jnp.bfloat16),
         scratch_shapes=[
             floats((3, 8, width)),
@@ -816,7 +827,6 @@
         out_shape=jax.ShapeDtypeStruct((rows, width), jnp.bfloat16),
         input_output_aliases={4: 0},
         scratch_shapes=[
-            floats((4, rows, 128)),
             shorts((rows, behind)),
             floats((16, 128)),
             pltpu.SemaphoreType.DMA((2,)),
@@ -824,7 +834,7 @@
         compiler_params=params(),
         cost_estimate=cost(1),
         name="last",
-    )(last_code, last_base, right, ahead_mixed, mixed)
+    )(last_code, last_base, last_right, ahead_mixed, mixed)
 
 
 def turn_table(outer_ids, inner_ids, modulus):
@@ -915,7 +925,9 @@
 
 
 def body(projected, *others):
-    if lax.axis_size("ctx") == 2:
+    _, rows, width = projected.shape
+    laid_out = rows % 32 == 0 and 64 <= rows <= 128 and width in (1024, 2048)
+    if lax.axis_size("ctx") == 2 and laid_out:
         return one_way(projected, *others)
     return exchanged(projected, *others)
 

time: 16.6 us -> 16.6 us (level)
  waiting for transfers between devices: 1.33 us -> 1.03 us
  Pallas kernels: 9.98 us -> 10.2 us
    ppermute x1, waiting for transfers between devices: 0.93 us -> 0.48 us  [one_way(): two_code = lax.ppermute(two_code, 'ctx', [(0, 1), (1, 0)])]
    pallas_call x1, Pallas kernels: 3.78 us -> 4.02 us  [one_way(): pl.pallas_call(own_kernel, in_specs=[in_vmem] * 10, out_specs=[in_vmem] *...]
  transfers between devices with their start and end apart: 3 -> 3, of which waited for: 2 -> 2; matrix products, arithmetic and copies ran while one was open for 0% -> 0% of each run, Pallas kernels for 55% -> 57%
where the time goes in v6:
time: 16.6 us; the launch traced here: 16.4 us
  Pallas kernels  10.2 us (61%)
  starting transfers between devices  4.87 us (29%)
  waiting for transfers between devices  1.03 us (6%)
  between operations  0.21 us (1%)
    pallas_call x1, Pallas kernels, one_way(): pl.pallas_call(own_kernel, in_specs=[in_vmem] * 10, out_specs=[in_vmem] *...  4.02 us
    pallas_call x1, Pallas kernels, one_way(): pl.pallas_call(lambda one_ref, two_ref, *refs: join_kernel((one_ref, two_...  2.27 us
    ppermute x1, starting transfers between devices, one_way(): one_code = lax.ppermute(one_code, 'ctx', [(0, 1), (1, 0)])  1.89 us
    ppermute x1, starting transfers between devices, one_way(): two_code = lax.ppermute(two_code, 'ctx', [(0, 1), (1, 0)])  1.69 us
    pallas_call x1, Pallas kernels, one_way(): pl.pallas_call(functools.partial(network_filter_kernel, middle), in_specs...  1.61 us
    pallas_call x1, Pallas kernels, one_way(): pl.pallas_call(functools.partial(filter_spectra, 0), in_specs=[in_vmem] *...  1.46 us
    ppermute x1, starting transfers between devices, one_way(): last_code = lax.ppermute(last_code, 'ctx', pairs)  1.29 us
    pallas_call x1, Pallas kernels, one_way(): pl.pallas_call(functools.partial(last_kernel, middle), in_specs=[in_vmem]...  0.8 us
  transfers between devices with their start and end apart: 3, of which 2 were waited for; matrix products, arithmetic and copies ran while one was open for 0% of the time, Pallas kernels for 57%

profile of v6, /device:TPU:6, one launch (start us, length us, event | category | flops | bytes accessed | tf_op | source)
XLA Modules:
  0.0 16.4 jit_solution(10462289060544044007)
XLA Ops:
  0.0 1.9 %collective-permute-start.1 = (bf16[544,128]{1,0:T(8,128)(2,1)S(1)}, bf16[544,128]{1,0:T(8,128)(2,1)S(1)}, u32[]{:S(2)}, u32[]{:S(2)}) collective-permute-start(bf16[544,128]{1,0:T(8,128)(2,1)S(1)} %get-tuple-element.36), channel_id=1, source_target_pairs={{0,16},{16,0},{1,17},{17,1},{2,18},{18,2},{3,19},{19,3},{4,20},{20... | collective-permute-start | bytes 417800 | tf_op jit(solution)/shard_map/ppermute | solution.py:721
  2.0 0.0 copy-start.4
  2.0 0.0 copy-start.5
  2.0 0.0 copy-start.6
  2.0 0.0 copy-start.7
  2.0 0.0 copy-start.8
  2.0 0.0 copy-start.9
  2.0 0.0 copy-start.10
  2.0 0.0 copy-start.12
  2.1 1.7 %collective-permute-start.2 = (bf16[1296,128]{1,0:T(8,128)(2,1)S(1)}, bf16[1296,128]{1,0:T(8,128)(2,1)S(1)}, u32[]{:S(2)}, u32[]{:S(2)}) collective-permute-start(bf16[1296,128]{1,0:T(8,128)(2,1)S(1)} %get-tuple-element.42), channel_id=1, source_target_pairs={{0,16},{16,0},{1,17},{17,1},{2,18},{18,2},{3,19},{19,3},{4,20},{20... | collective-permute-start | bytes 995336 | tf_op jit(solution)/shard_map/ppermute | solution.py:739
  3.8 0.0 copy-done.5
  3.8 0.0 copy-done.6
  3.8 0.0 copy-done.7
  3.8 0.0 copy-done.8
  3.8 1.6 %filter.2 = (f32[256,512]{1,0:T(8,128)S(1)}, f32[256,512]{1,0:T(8,128)S(1)}, bf16[256,192]{1,0:T(8,128)(2,1)S(1)}) custom-call(f32[64,2048]{1,0:T(8,128)S(1)} %copy-done.1, f32[1,2048]{1,0:T(1,128)S(1)} %bitcast.9, f32[1,2048]{1,0:T(1,128)S(1)} %bitcast.11, f32[256,128]{1,0:T(8,128)S(1)} %copy-done.10, bf16[256,192]{1,0:T(8,128)(2,1)S(1)} %copy-done.9, ...), custom_call_target="tpu_custom_call" | custom-call | flops 2000000000 | bytes 6000000 | tf_op jit(solution)/shard_map/filter/pallas_call | solution.py:740
  5.5 0.0 copy-start.11
  5.5 1.5 %filter.3 = (f32[256,1536]{1,0:T(8,128)S(1)}, f32[256,1536]{1,0:T(8,128)S(1)}) custom-call(f32[64,2048]{1,0:T(8,128)S(1)} %copy-done.1, f32[1,2048]{1,0:T(1,128)S(1)} %bitcast.10, f32[1,2048]{1,0:T(1,128)S(1)} %bitcast.12, f32[256,128]{1,0:T(8,128)S(1)} %copy-done.10, bf16[256,192]{1,0:T(8,128)(2,1)S(1)} %copy-done.9, ...), custom_call_target="tpu_custom_call" | custom-call | flops 2000000000 | bytes 6000000 | tf_op jit(solution)/shard_map/filter/pallas_call | solution.py:750
  7.0 1.3 %collective-permute-start = (bf16[528,128]{1,0:T(8,128)(2,1)S(1)}, bf16[528,128]{1,0:T(8,128)(2,1)S(1)}, u32[]{:S(2)}, u32[]{:S(2)}) collective-permute-start(bf16[528,128]{1,0:T(8,128)(2,1)S(1)} %get-tuple-element.35), channel_id=1, source_target_pairs={{0,16},{1,17},{2,18},{3,19},{4,20},{5,21},{6,22},{7,23},{8,24},{9,... | collective-permute-start | bytes 405512 | tf_op jit(solution)/shard_map/ppermute | solution.py:785
  8.3 0.0 collective-permute-done.1.rims_ref.one_ref
  8.3 4.0 %own.1 = (f32[128,2048]{1,0:T(8,128)S(1)}, f32[256,1536]{1,0:T(8,128)S(1)}, f32[128,512]{1,0:T(8,128)S(1)}, f32[128,512]{1,0:T(8,128)S(1)}, bf16[128,2048]{1,0:T(8,128)(2,1)}) custom-call(bf16[3,128,2048]{2,1,0:T(8,128)(2,1)S(1)} %copy-done, bf16[544,128]{1,0:T(8,128)(2,1)S(1)} %collective-permute-done.1.rims_ref.one_ref, f32[3,7,2048]{2,1,0:T(8,128)S(1)} %bitcast.8, ...), custom_call_target="tpu_custom_call" | custom-call | flops 4000000000 | bytes 12000000 | tf_op jit(solution)/shard_map/own/pallas_call | solution.py:786
  12.3 0.5 %collective-permute-done.2.two_ref = bf16[1296,128]{1,0:T(8,128)(2,1)S(1)} collective-permute-done((bf16[1296,128]{1,0:T(8,128)(2,1)S(1)}, bf16[1296,128]{1,0:T(8,128)(2,1)S(1)}, u32[]{:S(2)}, u32[]{:S(2)}) %collective-permute-start.2) | collective-permute-done | bytes 331808 | tf_op jit(solution)/shard_map/ppermute | solution.py:739
  12.8 2.3 %join.1.ahead_ref = bf16[128,1536]{1,0:T(8,128)(2,1)S(1)} custom-call(bf16[544,128]{1,0:T(8,128)(2,1)S(1)} %collective-permute-done.1.rims_ref.one_ref, bf16[1296,128]{1,0:T(8,128)(2,1)S(1)} %collective-permute-done.2.two_ref, f32[256,1536]{1,0:T(8,128)S(1)} %get-tuple-element.43.refs_0_, f32[256,1536]{1,0:T(8,128)S(1)} %get-tuple-element.44.refs_1_, ...), custom_call_target="tpu_custom_call" | custom-call | flops 2000000000 | bytes 6000000 | tf_op jit(solution)/shard_map/join/pallas_call | solution.py:806
  15.1 0.5 %collective-permute-done.coded_ref = bf16[528,128]{1,0:T(8,128)(2,1)S(1)} collective-permute-done((bf16[528,128]{1,0:T(8,128)(2,1)S(1)}, bf16[528,128]{1,0:T(8,128)(2,1)S(1)}, u32[]{:S(2)}, u32[]{:S(2)}) %collective-permute-start) | collective-permute-done | bytes 135200 | tf_op jit(solution)/shard_map/ppermute | solution.py:785
  15.6 0.8 %last.1 = bf16[128,2048]{1,0:T(8,128)(2,1)} custom-call(bf16[528,128]{1,0:T(8,128)(2,1)S(1)} %collective-permute-done.coded_ref, f32[128,512]{1,0:T(8,128)S(1)} %get-tuple-element.40.base_ref, f32[128,512]{1,0:T(8,128)S(1)} %get-tuple-element.41.right_ref, bf16[128,1536]{1,0:T(8,128)(2,1)S(1)} %join.1.ahead_ref, ...), custom_call_target="tpu_custom_call", output_to_operand_aliasing={{}: (4, {})} | custom-call | flops 1000000000 | bytes 3000000 | tf_op jit(solution)/shard_map/last/pallas_call | solution.py:823
  (16 shorter events, 0.1 us)
Async XLA Ops:
  0.0 1.9 %copy-start = (bf16[3,128,2048]{2,1,0:T(8,128)(2,1)S(1)}, bf16[3,128,2048]{2,1,0:T(8,128)(2,1)}, u32[]{:S(2)}) copy-start(bf16[3,128,2048]{2,1,0:T(8,128)(2,1)} %projected_ref.7) | copy-start | bytes 4718596
  0.0 1.9 %copy-start.2 = (f32[7,3,2048]{2,0,1:T(8,128)S(1)}, f32[7,3,2048]{2,0,1:T(8,128)}, u32[]{:S(2)}) copy-start(f32[7,3,2048]{2,0,1:T(8,128)} %param.14) | copy-start | bytes 516100
  0.0 8.2 %collective-permute-start.1 = (bf16[544,128]{1,0:T(8,128)(2,1)S(1)}, bf16[544,128]{1,0:T(8,128)(2,1)S(1)}, u32[]{:S(2)}, u32[]{:S(2)}) collective-permute-start(bf16[544,128]{1,0:T(8,128)(2,1)S(1)} %get-tuple-element.36), channel_id=1, source_target_pairs={{0,16},{16,0},{1,17},{17,1},{2,18},{18,2},{3,19},{19,3},{4,20},{20... | collective-permute-start | bytes 417800 | tf_op jit(solution)/shard_map/ppermute | solution.py:721
  1.9 1.8 %copy-start.1 = (f32[64,2048]{1,0:T(8,128)S(1)}, f32[64,2048]{1,0:T(8,128)}, u32[]{:S(2)}) copy-start(f32[64,2048]{1,0:T(8,128)} %out_ref.1) | copy-start | bytes 1572868
  1.9 1.8 %copy-start.3 = (f32[64,64]{1,0:T(8,128)S(1)}, f32[64,64]{1,0:T(8,128)}, u32[]{:S(2)}) copy-start(f32[64,64]{1,0:T(8,128)} %refs_9_.1) | copy-start | bytes 49156
  2.0 1.8 %copy-start.4 = (f32[33,64]{1,0:T(8,128)S(1)}, f32[33,64]{1,0:T(8,128)}, u32[]{:S(2)}) copy-start(f32[33,64]{1,0:T(8,128)} %refs_6_.1) | copy-start | bytes 25348
  2.0 1.8 %copy-start.5 = (f32[2048]{0:T(1024)S(1)}, f32[2048]{0:T(1024)}, u32[]{:S(2)}) copy-start(f32[2048]{0:T(1024)} %param.20) | copy-start | bytes 24580
  2.0 1.8 %copy-start.6 = (f32[2048]{0:T(1024)S(1)}, f32[2048]{0:T(1024)}, u32[]{:S(2)}) copy-start(f32[2048]{0:T(1024)} %param.21) | copy-start | bytes 24580
  2.0 1.8 %copy-start.7 = (f32[64]{0:T(128)S(1)}, f32[64]{0:T(128)}, u32[]{:S(2)}) copy-start(f32[64]{0:T(128)} %param.16) | copy-start | bytes 772
  2.0 1.8 %copy-start.8 = (f32[64]{0:T(128)S(1)}, f32[64]{0:T(128)}, u32[]{:S(2)}) copy-start(f32[64]{0:T(128)} %param.17) | copy-start | bytes 772
  2.0 1.8 %copy-start.9 = (bf16[256,192]{1,0:T(8,128)(2,1)S(1)}, bf16[256,192]{1,0:T(8,128)(2,1)}, u32[]{:S(2)}) copy-start(bf16[256,192]{1,0:T(8,128)(2,1)} %constant.9.clone.refs_4_.forward_ref.refs_3_) | copy-start | bytes 294916
  2.0 1.8 %copy-start.10 = (f32[256,128]{1,0:T(8,128)S(1)}, f32[256,128]{1,0:T(8,128)}, u32[]{:S(2)}) copy-start(f32[256,128]{1,0:T(8,128)} %constant.8.clone.refs_3_.places_ref) | copy-start | bytes 393220
  2.0 1.8 %copy-start.12 = (f32[40,256]{1,0:T(8,128)S(1)}, f32[40,256]{1,0:T(8,128)}, u32[]{:S(2)}) copy-start(f32[40,256]{1,0:T(8,128)} %constant.10.clone.refs_5_) | copy-start | bytes 122884
  2.1 10.7 %collective-permute-start.2 = (bf16[1296,128]{1,0:T(8,128)(2,1)S(1)}, bf16[1296,128]{1,0:T(8,128)(2,1)S(1)}, u32[]{:S(2)}, u32[]{:S(2)}) collective-permute-start(bf16[1296,128]{1,0:T(8,128)(2,1)S(1)} %get-tuple-element.42), channel_id=1, source_target_pairs={{0,16},{16,0},{1,17},{17,1},{2,18},{18,2},{3,19},{19,3},{4,20},{20... | collective-permute-start | bytes 995336 | tf_op jit(solution)/shard_map/ppermute | solution.py:739
  5.5 1.5 %copy-start.11 = (bf16[128,384]{1,0:T(8,128)(2,1)S(1)}, bf16[128,384]{1,0:T(8,128)(2,1)}, u32[]{:S(2)}) copy-start(bf16[128,384]{1,0:T(8,128)(2,1)} %constant.11.clone.backward_ref.refs_4_) | copy-start | bytes 294916
  7.0 8.6 %collective-permute-start = (bf16[528,128]{1,0:T(8,128)(2,1)S(1)}, bf16[528,128]{1,0:T(8,128)(2,1)S(1)}, u32[]{:S(2)}, u32[]{:S(2)}) collective-permute-start(bf16[528,128]{1,0:T(8,128)(2,1)S(1)} %get-tuple-element.35), channel_id=1, source_target_pairs={{0,16},{1,17},{2,18},{3,19},{4,20},{5,21},{6,22},{7,23},{8,24},{9,... | collective-permute-start | bytes 405512 | tf_op jit(solution)/shard_map/ppermute | solution.py:785

commit v7 on v6

--- a/solution.py
+++ b/solution.py
@@ -682,7 +682,7 @@
     _, rows, width = projected.shape
     half = rows // 2
     total_len = 2 * rows
-    ahead = [width // 8, width * 5 // 8]
+    ahead = [width // 16, width * 11 // 16]
     middle = sum(ahead)
     behind = width - middle
     forward, backward = odd_tables(rows)
@@ -926,7 +926,7 @@
 
 def body(projected, *others):
     _, rows, width = projected.shape
-    laid_out = rows % 32 == 0 and 64 <= rows <= 128 and width in (1024, 2048)
+    laid_out = rows % 32 == 0 and 64 <= rows <= 128 and width == 2048
     if lax.axis_size("ctx") == 2 and laid_out:
         return one_way(projected, *others)
     return exchanged(projected, *others)

time: 16.6 us -> 16.6 us (level)
  starting transfers between devices: 4.87 us -> 5.07 us
  waiting for transfers between devices: 1.03 us -> 0.85 us
    ppermute x1, starting transfers between devices: 1.69 us -> 2.05 us  [one_way(): two_code = lax.ppermute(two_code, 'ctx', [(0, 1), (1, 0)])]
    ppermute x1, waiting for transfers between devices: 0.48 us -> 0.17 us  [one_way(): two_code = lax.ppermute(two_code, 'ctx', [(0, 1), (1, 0)])]
where the time goes in v7:
time: 16.6 us; the launch traced here: 16.4 us
  Pallas kernels  10.2 us (61%)
  starting transfers between devices  5.07 us (31%)
  waiting for transfers between devices  0.85 us (5%)
  between operations  0.21 us (1%)
    pallas_call x1, Pallas kernels, one_way(): pl.pallas_call(own_kernel, in_specs=[in_vmem] * 10, out_specs=[in_vmem] *...  4 us
    pallas_call x1, Pallas kernels, one_way(): pl.pallas_call(lambda one_ref, two_ref, *refs: join_kernel((one_ref, two_...  2.3 us
    ppermute x1, starting transfers between devices, one_way(): two_code = lax.ppermute(two_code, 'ctx', [(0, 1), (1, 0)])  2.05 us
    ppermute x1, starting transfers between devices, one_way(): one_code = lax.ppermute(one_code, 'ctx', [(0, 1), (1, 0)])  1.73 us
    pallas_call x1, Pallas kernels, one_way(): pl.pallas_call(functools.partial(network_filter_kernel, middle), in_specs...  1.62 us
    pallas_call x1, Pallas kernels, one_way(): pl.pallas_call(functools.partial(filter_spectra, 0), in_specs=[in_vmem] *...  1.43 us
    ppermute x1, starting transfers between devices, one_way(): last_code = lax.ppermute(last_code, 'ctx', pairs)  1.29 us
    pallas_call x1, Pallas kernels, one_way(): pl.pallas_call(functools.partial(last_kernel, middle), in_specs=[in_vmem]...  0.8 us
  transfers between devices with their start and end apart: 3, of which 2 were waited for; matrix products, arithmetic and copies ran while one was open for 0% of the time, Pallas kernels for 57%

profile of v7, /device:TPU:6, one launch (start us, length us, event | category | flops | bytes accessed | tf_op | source)
XLA Modules:
  0.0 16.4 jit_solution(9413051086509554281)
XLA Ops:
  0.0 1.7 %collective-permute-start.1 = (bf16[416,128]{1,0:T(8,128)(2,1)S(1)}, bf16[416,128]{1,0:T(8,128)(2,1)S(1)}, u32[]{:S(2)}, u32[]{:S(2)}) collective-permute-start(bf16[416,128]{1,0:T(8,128)(2,1)S(1)} %get-tuple-element.36), channel_id=1, source_target_pairs={{0,16},{16,0},{1,17},{17,1},{2,18},{18,2},{3,19},{19,3},{4,20},{20... | collective-permute-start | bytes 319496 | tf_op jit(solution)/shard_map/ppermute | solution.py:721
  1.8 0.0 copy-done
  1.8 0.0 copy-done.2
  1.8 0.0 copy-start.4
  1.8 0.0 copy-start.5
  1.8 0.0 copy-start.6
  1.8 0.0 copy-start.7
  1.8 0.0 copy-start.8
  1.8 0.0 copy-start.9
  1.9 0.0 copy-start.10
  1.9 0.0 copy-start.12
  1.9 2.1 %collective-permute-start.2 = (bf16[1424,128]{1,0:T(8,128)(2,1)S(1)}, bf16[1424,128]{1,0:T(8,128)(2,1)S(1)}, u32[]{:S(2)}, u32[]{:S(2)}) collective-permute-start(bf16[1424,128]{1,0:T(8,128)(2,1)S(1)} %get-tuple-element.42), channel_id=1, source_target_pairs={{0,16},{16,0},{1,17},{17,1},{2,18},{18,2},{3,19},{19,3},{4,20},{20... | collective-permute-start | bytes 1093640 | tf_op jit(solution)/shard_map/ppermute | solution.py:739
  4.0 0.0 copy-done.1
  4.0 0.0 copy-done.5
  4.0 1.6 %filter.2 = (f32[256,512]{1,0:T(8,128)S(1)}, f32[256,512]{1,0:T(8,128)S(1)}, bf16[256,192]{1,0:T(8,128)(2,1)S(1)}) custom-call(f32[64,2048]{1,0:T(8,128)S(1)} %copy-done.1, f32[1,2048]{1,0:T(1,128)S(1)} %bitcast.9, f32[1,2048]{1,0:T(1,128)S(1)} %bitcast.11, f32[256,128]{1,0:T(8,128)S(1)} %copy-done.10, bf16[256,192]{1,0:T(8,128)(2,1)S(1)} %copy-done.9, ...), custom_call_target="tpu_custom_call" | custom-call | flops 2000000000 | bytes 6000000 | tf_op jit(solution)/shard_map/filter/pallas_call | solution.py:740
  5.7 0.0 copy-start.11
  5.7 1.4 %filter.3 = (f32[256,1536]{1,0:T(8,128)S(1)}, f32[256,1536]{1,0:T(8,128)S(1)}) custom-call(f32[64,2048]{1,0:T(8,128)S(1)} %copy-done.1, f32[1,2048]{1,0:T(1,128)S(1)} %bitcast.10, f32[1,2048]{1,0:T(1,128)S(1)} %bitcast.12, f32[256,128]{1,0:T(8,128)S(1)} %copy-done.10, bf16[256,192]{1,0:T(8,128)(2,1)S(1)} %copy-done.9, ...), custom_call_target="tpu_custom_call" | custom-call | flops 2000000000 | bytes 6000000 | tf_op jit(solution)/shard_map/filter/pallas_call | solution.py:750
  7.2 1.3 %collective-permute-start = (bf16[528,128]{1,0:T(8,128)(2,1)S(1)}, bf16[528,128]{1,0:T(8,128)(2,1)S(1)}, u32[]{:S(2)}, u32[]{:S(2)}) collective-permute-start(bf16[528,128]{1,0:T(8,128)(2,1)S(1)} %get-tuple-element.35), channel_id=1, source_target_pairs={{0,16},{1,17},{2,18},{3,19},{4,20},{5,21},{6,22},{7,23},{8,24},{9,... | collective-permute-start | bytes 405512 | tf_op jit(solution)/shard_map/ppermute | solution.py:785
  8.5 0.0 collective-permute-done.1.rims_ref.one_ref
  8.5 4.0 %own.1 = (f32[128,2048]{1,0:T(8,128)S(1)}, f32[256,1536]{1,0:T(8,128)S(1)}, f32[128,512]{1,0:T(8,128)S(1)}, f32[128,512]{1,0:T(8,128)S(1)}, bf16[128,2048]{1,0:T(8,128)(2,1)}) custom-call(bf16[3,128,2048]{2,1,0:T(8,128)(2,1)S(1)} %copy-done, bf16[416,128]{1,0:T(8,128)(2,1)S(1)} %collective-permute-done.1.rims_ref.one_ref, f32[3,7,2048]{2,1,0:T(8,128)S(1)} %bitcast.8, ...), custom_call_target="tpu_custom_call" | custom-call | flops 4000000000 | bytes 12000000 | tf_op jit(solution)/shard_map/own/pallas_call | solution.py:786
  12.5 0.2 %collective-permute-done.2.two_ref = bf16[1424,128]{1,0:T(8,128)(2,1)S(1)} collective-permute-done((bf16[1424,128]{1,0:T(8,128)(2,1)S(1)}, bf16[1424,128]{1,0:T(8,128)(2,1)S(1)}, u32[]{:S(2)}, u32[]{:S(2)}) %collective-permute-start.2) | collective-permute-done | bytes 364576 | tf_op jit(solution)/shard_map/ppermute | solution.py:739
  12.6 2.3 %join.1.ahead_ref = bf16[128,1536]{1,0:T(8,128)(2,1)S(1)} custom-call(bf16[416,128]{1,0:T(8,128)(2,1)S(1)} %collective-permute-done.1.rims_ref.one_ref, bf16[1424,128]{1,0:T(8,128)(2,1)S(1)} %collective-permute-done.2.two_ref, f32[256,1536]{1,0:T(8,128)S(1)} %get-tuple-element.43.refs_0_, f32[256,1536]{1,0:T(8,128)S(1)} %get-tuple-element.44.refs_1_, ...), custom_call_target="tpu_custom_call" | custom-call | flops 2000000000 | bytes 6000000 | tf_op jit(solution)/shard_map/join/pallas_call | solution.py:806
  14.9 0.7 %collective-permute-done.coded_ref = bf16[528,128]{1,0:T(8,128)(2,1)S(1)} collective-permute-done((bf16[528,128]{1,0:T(8,128)(2,1)S(1)}, bf16[528,128]{1,0:T(8,128)(2,1)S(1)}, u32[]{:S(2)}, u32[]{:S(2)}) %collective-permute-start) | collective-permute-done | bytes 135200 | tf_op jit(solution)/shard_map/ppermute | solution.py:785
  15.6 0.8 %last.1 = bf16[128,2048]{1,0:T(8,128)(2,1)} custom-call(bf16[528,128]{1,0:T(8,128)(2,1)S(1)} %collective-permute-done.coded_ref, f32[128,512]{1,0:T(8,128)S(1)} %get-tuple-element.40.base_ref, f32[128,512]{1,0:T(8,128)S(1)} %get-tuple-element.41.right_ref, bf16[128,1536]{1,0:T(8,128)(2,1)S(1)} %join.1.ahead_ref, ...), custom_call_target="tpu_custom_call", output_to_operand_aliasing={{}: (4, {})} | custom-call | flops 1000000000 | bytes 3000000 | tf_op jit(solution)/shard_map/last/pallas_call | solution.py:823
  (16 shorter events, 0.1 us)
Async XLA Ops:
  0.0 1.8 %copy-start = (bf16[3,128,2048]{2,1,0:T(8,128)(2,1)S(1)}, bf16[3,128,2048]{2,1,0:T(8,128)(2,1)}, u32[]{:S(2)}) copy-start(bf16[3,128,2048]{2,1,0:T(8,128)(2,1)} %projected_ref.7) | copy-start | bytes 4718596
  0.0 1.8 %copy-start.2 = (f32[7,3,2048]{2,0,1:T(8,128)S(1)}, f32[7,3,2048]{2,0,1:T(8,128)}, u32[]{:S(2)}) copy-start(f32[7,3,2048]{2,0,1:T(8,128)} %param.14) | copy-start | bytes 516100
  0.0 8.4 %collective-permute-start.1 = (bf16[416,128]{1,0:T(8,128)(2,1)S(1)}, bf16[416,128]{1,0:T(8,128)(2,1)S(1)}, u32[]{:S(2)}, u32[]{:S(2)}) collective-permute-start(bf16[416,128]{1,0:T(8,128)(2,1)S(1)} %get-tuple-element.36), channel_id=1, source_target_pairs={{0,16},{16,0},{1,17},{17,1},{2,18},{18,2},{3,19},{19,3},{4,20},{20... | collective-permute-start | bytes 319496 | tf_op jit(solution)/shard_map/ppermute | solution.py:721
  1.8 2.2 %copy-start.1 = (f32[64,2048]{1,0:T(8,128)S(1)}, f32[64,2048]{1,0:T(8,128)}, u32[]{:S(2)}) copy-start(f32[64,2048]{1,0:T(8,128)} %out_ref.1) | copy-start | bytes 1572868
  1.8 2.2 %copy-start.3 = (f32[64,64]{1,0:T(8,128)S(1)}, f32[64,64]{1,0:T(8,128)}, u32[]{:S(2)}) copy-start(f32[64,64]{1,0:T(8,128)} %refs_9_.1) | copy-start | bytes 49156
  1.8 2.2 %copy-start.4 = (f32[33,64]{1,0:T(8,128)S(1)}, f32[33,64]{1,0:T(8,128)}, u32[]{:S(2)}) copy-start(f32[33,64]{1,0:T(8,128)} %refs_6_.1) | copy-start | bytes 25348
  1.8 2.2 %copy-start.5 = (f32[2048]{0:T(1024)S(1)}, f32[2048]{0:T(1024)}, u32[]{:S(2)}) copy-start(f32[2048]{0:T(1024)} %param.20) | copy-start | bytes 24580
  1.8 2.2 %copy-start.6 = (f32[2048]{0:T(1024)S(1)}, f32[2048]{0:T(1024)}, u32[]{:S(2)}) copy-start(f32[2048]{0:T(1024)} %param.21) | copy-start | bytes 24580
  1.8 2.2 %copy-start.7 = (f32[64]{0:T(128)S(1)}, f32[64]{0:T(128)}, u32[]{:S(2)}) copy-start(f32[64]{0:T(128)} %param.16) | copy-start | bytes 772
  1.8 2.2 %copy-start.8 = (f32[64]{0:T(128)S(1)}, f32[64]{0:T(128)}, u32[]{:S(2)}) copy-start(f32[64]{0:T(128)} %param.17) | copy-start | bytes 772
  1.8 2.2 %copy-start.9 = (bf16[256,192]{1,0:T(8,128)(2,1)S(1)}, bf16[256,192]{1,0:T(8,128)(2,1)}, u32[]{:S(2)}) copy-start(bf16[256,192]{1,0:T(8,128)(2,1)} %constant.9.clone.refs_4_.forward_ref.refs_3_) | copy-start | bytes 294916
  1.9 2.2 %copy-start.10 = (f32[256,128]{1,0:T(8,128)S(1)}, f32[256,128]{1,0:T(8,128)}, u32[]{:S(2)}) copy-start(f32[256,128]{1,0:T(8,128)} %constant.8.clone.refs_3_.places_ref) | copy-start | bytes 393220
  1.9 2.2 %copy-start.12 = (f32[40,256]{1,0:T(8,128)S(1)}, f32[40,256]{1,0:T(8,128)}, u32[]{:S(2)}) copy-start(f32[40,256]{1,0:T(8,128)} %constant.10.clone.refs_5_) | copy-start | bytes 122884
  1.9 10.7 %collective-permute-start.2 = (bf16[1424,128]{1,0:T(8,128)(2,1)S(1)}, bf16[1424,128]{1,0:T(8,128)(2,1)S(1)}, u32[]{:S(2)}, u32[]{:S(2)}) collective-permute-start(bf16[1424,128]{1,0:T(8,128)(2,1)S(1)} %get-tuple-element.42), channel_id=1, source_target_pairs={{0,16},{16,0},{1,17},{17,1},{2,18},{18,2},{3,19},{19,3},{4,20},{20... | collective-permute-start | bytes 1093640 | tf_op jit(solution)/shard_map/ppermute | solution.py:739
  5.7 1.5 %copy-start.11 = (bf16[128,384]{1,0:T(8,128)(2,1)S(1)}, bf16[128,384]{1,0:T(8,128)(2,1)}, u32[]{:S(2)}) copy-start(bf16[128,384]{1,0:T(8,128)(2,1)} %constant.11.clone.backward_ref.refs_4_) | copy-start | bytes 294916
  7.2 8.5 %collective-permute-start = (bf16[528,128]{1,0:T(8,128)(2,1)S(1)}, bf16[528,128]{1,0:T(8,128)(2,1)S(1)}, u32[]{:S(2)}, u32[]{:S(2)}) collective-permute-start(bf16[528,128]{1,0:T(8,128)(2,1)S(1)} %get-tuple-element.35), channel_id=1, source_target_pairs={{0,16},{1,17},{2,18},{3,19},{4,20},{5,21},{6,22},{7,23},{8,24},{9,... | collective-permute-start | bytes 405512 | tf_op jit(solution)/shard_map/ppermute | solution.py:785

commit v8 on v6

--- a/solution.py
+++ b/solution.py
@@ -442,10 +442,9 @@
 
 
 def send_kernel(
-    first, projected_ref, taps_ref, near_ref, far_ref, forward_ref, backward_ref, ahead_near_ref, one_ref, two_ref,
-    coded_ref, mixed_ref, gates_ref, ahead_bins_ref,
+    first, projected_ref, taps_ref, near_ref, far_ref, forward_ref, backward_ref, one_ref, two_ref,
+    coded_ref, mixed_ref, gates_ref, ahead_spec_ref,
     strided_buf, parts_buf, spec_buf, bins_buf, right_buf, conv_buf, peak_buf, levels_buf, ahead_parts_buf,
-    ahead_spec_buf,
 ):
     rows, width = right_buf.shape
     half = rows // 2
@@ -505,20 +504,14 @@
 
             each_tile(ref.shape[1] // 128, 4, recall)
             start += ref.shape[1]
-        forward_dots(forward_ref, ahead_parts_buf, ahead_spec_buf)
-        each_tile(
-            first // 128, 4,
-            lambda tile, _: filtered(
-                ahead_spec_buf, ahead_near_ref, ahead_bins_ref, tile_lanes(tile), tile_lanes(tile)
-            ),
-        )
+        forward_dots(forward_ref, ahead_parts_buf, ahead_spec_ref)
         mix_tiles(mix, tiles, mixed_ref, strided_buf.at[:, 0])
 
 
 def own_kernel(
-    projected_ref, rims_ref, taps_ref, near_ref, last_near_ref, forward_ref, backward_ref, gates_ref, ahead_bins_ref,
+    projected_ref, rims_ref, taps_ref, near_ref, last_near_ref, forward_ref, backward_ref, gates_ref, ahead_spec_ref,
     behind_ref, right_ref, bins_ref, base_ref, last_right_ref, mixed_ref,
-    rims_buf, strided_buf, parts_buf, spec_buf, bins_buf, conv_buf, mixed_buf, sems,
+    rims_buf, strided_buf, parts_buf, spec_buf, bins_buf, conv_buf, mixed_buf, ahead_bins_buf, sems,
 ):
     rows, width = right_ref.shape
     half = rows // 2
@@ -530,7 +523,11 @@
         tiles = middle // 128
         behind = pltpu.make_async_copy(behind_ref, mixed_ref.at[:, pl.ds(middle, width - middle)], sems.at[0])
         behind.start()
-        backward_dots(backward_ref, ahead_bins_ref, conv_buf)
+        each_tile(
+            tiles, 4,
+            lambda tile, _: filtered(ahead_spec_ref, near_ref, ahead_bins_buf, tile_lanes(tile), tile_lanes(tile)),
+        )
+        backward_dots(backward_ref, ahead_bins_buf, conv_buf)
 
         def mix(tile):
             cols = tile_lanes(tile)
@@ -758,14 +755,13 @@
         name="filter",
     )(*weights, second_halves)
     last_near, near = lax.optimization_barrier((last_near, near))
-    last_code, behind_mixed, gates, ahead_bins = pl.pallas_call(
+    last_code, behind_mixed, gates, ahead_spec = pl.pallas_call(
         functools.partial(send_kernel, middle),
-        in_specs=[in_vmem] * 9,
+        in_specs=[in_vmem] * 8,
         out_specs=[in_vmem] * 4,
         out_shape=message(behind)
         + arrays((rows, behind), dtype=jnp.bfloat16)
-        + arrays((rows, middle))
-        + arrays((2, 2 * rows, middle), dtype=jnp.bfloat16),
+        + arrays((rows, middle), (2, rows, middle)),
         scratch_shapes=[
             floats((2, 3, rows, 128)),
             shorts((2, rows, behind)),
@@ -776,12 +772,11 @@
             floats((8, behind)),
             floats((16, 128)),
             shorts((2, rows, middle)),
-            floats((2, rows, middle)),
         ],
         compiler_params=params(),
         cost_estimate=cost(2),
         name="send",
-    )(projected, taps, last_near, last_far, forward, backward, near, one_driven, two_driven)
+    )(projected, taps, last_near, last_far, forward, backward, one_driven, two_driven)
     last_code = lax.ppermute(last_code, "ctx", pairs)
     right, own_bins, last_base, last_right, mixed = pl.pallas_call(
         own_kernel,
@@ -797,12 +792,13 @@
             shorts((2, 2 * rows, behind)),
             floats((rows, middle)),
             shorts((rows, middle)),
+            shorts((2, 2 * rows, middle)),
             pltpu.SemaphoreType.DMA((2,)),
         ],
         compiler_params=params(),
         cost_estimate=cost(4),
         name="own",
-    )(projected, one_code, taps, near, last_near, forward, backward, gates, ahead_bins, behind_mixed)
+    )(projected, one_code, taps, near, last_near, forward, backward, gates, ahead_spec, behind_mixed)
     ahead_mixed = pl.pallas_call(
         lambda one_ref, two_ref, *refs: join_kernel((one_ref, two_ref), *refs),
         in_specs=[in_vmem] * 7,

time: 16.6 us -> 16.7 us (level)
    ppermute x1, waiting for transfers between devices: 0.55 us -> 0.02 us  [one_way(): last_code = lax.ppermute(last_code, 'ctx', pairs)]
    ppermute x1, waiting for transfers between devices: 0.48 us -> 0.98 us  [one_way(): two_code = lax.ppermute(two_code, 'ctx', [(0, 1), (1, 0)])]
  transfers between devices with their start and end apart: 3 -> 3, of which waited for: 2 -> 1; matrix products, arithmetic and copies ran while one was open for 0% -> 0% of each run, Pallas kernels for 57% -> 57%
where the time goes in v8:
time: 16.7 us; the launch traced here: 16.4 us
  Pallas kernels  10.3 us (62%)
  starting transfers between devices  4.87 us (29%)
  waiting for transfers between devices  1.01 us (6%)
  between operations  0.21 us (1%)
    pallas_call x1, Pallas kernels, one_way(): pl.pallas_call(own_kernel, in_specs=[in_vmem] * 10, out_specs=[in_vmem] *...  4.05 us
    pallas_call x1, Pallas kernels, one_way(): pl.pallas_call(lambda one_ref, two_ref, *refs: join_kernel((one_ref, two_...  2.27 us
    ppermute x1, starting transfers between devices, one_way(): one_code = lax.ppermute(one_code, 'ctx', [(0, 1), (1, 0)])  1.89 us
    ppermute x1, starting transfers between devices, one_way(): two_code = lax.ppermute(two_code, 'ctx', [(0, 1), (1, 0)])  1.69 us
    pallas_call x1, Pallas kernels, one_way(): pl.pallas_call(functools.partial(network_filter_kernel, middle), in_specs...  1.61 us
    pallas_call x1, Pallas kernels, one_way(): pl.pallas_call(functools.partial(filter_spectra, 0), in_specs=[in_vmem] *...  1.45 us
    ppermute x1, starting transfers between devices, one_way(): last_code = lax.ppermute(last_code, 'ctx', pairs)  1.29 us
    ppermute x1, waiting for transfers between devices, one_way(): two_code = lax.ppermute(two_code, 'ctx', [(0, 1), (1, 0)])  0.98 us
  transfers between devices with their start and end apart: 3, of which 1 were waited for; matrix products, arithmetic and copies ran while one was open for 0% of the time, Pallas kernels for 57%

profile of v8, /device:TPU:6, one launch (start us, length us, event | category | flops | bytes accessed | tf_op | source)
XLA Modules:
  0.0 16.4 jit_solution(15731106970071244524)
XLA Ops:
  0.0 1.9 %collective-permute-start.1 = (bf16[544,128]{1,0:T(8,128)(2,1)S(1)}, bf16[544,128]{1,0:T(8,128)(2,1)S(1)}, u32[]{:S(2)}, u32[]{:S(2)}) collective-permute-start(bf16[544,128]{1,0:T(8,128)(2,1)S(1)} %get-tuple-element.35), channel_id=1, source_target_pairs={{0,16},{16,0},{1,17},{17,1},{2,18},{18,2},{3,19},{19,3},{4,20},{20... | collective-permute-start | bytes 417800 | tf_op jit(solution)/shard_map/ppermute | solution.py:718
  1.9 0.0 copy-done
  1.9 0.0 copy-done.2
  2.0 0.0 copy-start.4
  2.0 0.0 copy-start.5
  2.0 0.0 copy-start.6
  2.0 0.0 copy-start.7
  2.0 0.0 copy-start.8
  2.0 0.0 copy-start.9
  2.0 0.0 copy-start.10
  2.0 0.0 copy-start.12
  2.1 1.7 %collective-permute-start.2 = (bf16[1296,128]{1,0:T(8,128)(2,1)S(1)}, bf16[1296,128]{1,0:T(8,128)(2,1)S(1)}, u32[]{:S(2)}, u32[]{:S(2)}) collective-permute-start(bf16[1296,128]{1,0:T(8,128)(2,1)S(1)} %get-tuple-element.42), channel_id=1, source_target_pairs={{0,16},{16,0},{1,17},{17,1},{2,18},{18,2},{3,19},{19,3},{4,20},{20... | collective-permute-start | bytes 995336 | tf_op jit(solution)/shard_map/ppermute | solution.py:736
  3.8 0.0 copy-done.3
  3.8 0.0 copy-done.5
  3.8 1.6 %filter.2 = (f32[256,512]{1,0:T(8,128)S(1)}, f32[256,512]{1,0:T(8,128)S(1)}, bf16[256,192]{1,0:T(8,128)(2,1)S(1)}) custom-call(f32[64,2048]{1,0:T(8,128)S(1)} %copy-done.1, f32[1,2048]{1,0:T(1,128)S(1)} %bitcast.9, f32[1,2048]{1,0:T(1,128)S(1)} %bitcast.11, f32[256,128]{1,0:T(8,128)S(1)} %copy-done.10, bf16[256,192]{1,0:T(8,128)(2,1)S(1)} %copy-done.9, ...), custom_call_target="tpu_custom_call" | custom-call | flops 2000000000 | bytes 6000000 | tf_op jit(solution)/shard_map/filter/pallas_call | solution.py:737
  5.5 0.0 copy-start.11
  5.5 1.5 %filter.3 = (f32[256,1536]{1,0:T(8,128)S(1)}, f32[256,1536]{1,0:T(8,128)S(1)}) custom-call(f32[64,2048]{1,0:T(8,128)S(1)} %copy-done.1, f32[1,2048]{1,0:T(1,128)S(1)} %bitcast.10, f32[1,2048]{1,0:T(1,128)S(1)} %bitcast.12, f32[256,128]{1,0:T(8,128)S(1)} %copy-done.10, bf16[256,192]{1,0:T(8,128)(2,1)S(1)} %copy-done.9, ...), custom_call_target="tpu_custom_call" | custom-call | flops 2000000000 | bytes 6000000 | tf_op jit(solution)/shard_map/filter/pallas_call | solution.py:747
  7.0 1.3 %collective-permute-start = (bf16[528,128]{1,0:T(8,128)(2,1)S(1)}, bf16[528,128]{1,0:T(8,128)(2,1)S(1)}, u32[]{:S(2)}, u32[]{:S(2)}) collective-permute-start(bf16[528,128]{1,0:T(8,128)(2,1)S(1)} %get-tuple-element.34), channel_id=1, source_target_pairs={{0,16},{1,17},{2,18},{3,19},{4,20},{5,21},{6,22},{7,23},{8,24},{9,... | collective-permute-start | bytes 405512 | tf_op jit(solution)/shard_map/ppermute | solution.py:780
  8.3 0.0 collective-permute-done.1.rims_ref.one_ref
  8.3 4.0 %own.1 = (f32[128,2048]{1,0:T(8,128)S(1)}, f32[256,1536]{1,0:T(8,128)S(1)}, f32[128,512]{1,0:T(8,128)S(1)}, f32[128,512]{1,0:T(8,128)S(1)}, bf16[128,2048]{1,0:T(8,128)(2,1)}) custom-call(bf16[3,128,2048]{2,1,0:T(8,128)(2,1)S(1)} %copy-done, bf16[544,128]{1,0:T(8,128)(2,1)S(1)} %collective-permute-done.1.rims_ref.one_ref, f32[3,7,2048]{2,1,0:T(8,128)S(1)} %bitcast.8, ...), custom_call_target="tpu_custom_call" | custom-call | flops 4000000000 | bytes 12000000 | tf_op jit(solution)/shard_map/own/pallas_call | solution.py:781
  12.3 1.0 %collective-permute-done.2.two_ref = bf16[1296,128]{1,0:T(8,128)(2,1)S(1)} collective-permute-done((bf16[1296,128]{1,0:T(8,128)(2,1)S(1)}, bf16[1296,128]{1,0:T(8,128)(2,1)S(1)}, u32[]{:S(2)}, u32[]{:S(2)}) %collective-permute-start.2) | collective-permute-done | bytes 331808 | tf_op jit(solution)/shard_map/ppermute | solution.py:736
  13.3 2.3 %join.1.ahead_ref = bf16[128,1536]{1,0:T(8,128)(2,1)S(1)} custom-call(bf16[544,128]{1,0:T(8,128)(2,1)S(1)} %collective-permute-done.1.rims_ref.one_ref, bf16[1296,128]{1,0:T(8,128)(2,1)S(1)} %collective-permute-done.2.two_ref, f32[256,1536]{1,0:T(8,128)S(1)} %get-tuple-element.43.refs_0_, f32[256,1536]{1,0:T(8,128)S(1)} %get-tuple-element.44.refs_1_, ...), custom_call_target="tpu_custom_call" | custom-call | flops 2000000000 | bytes 6000000 | tf_op jit(solution)/shard_map/join/pallas_call | solution.py:802
  15.6 0.0 collective-permute-done.coded_ref
  15.6 0.8 %last.1 = bf16[128,2048]{1,0:T(8,128)(2,1)} custom-call(bf16[528,128]{1,0:T(8,128)(2,1)S(1)} %collective-permute-done.coded_ref, f32[128,512]{1,0:T(8,128)S(1)} %get-tuple-element.40.base_ref, f32[128,512]{1,0:T(8,128)S(1)} %get-tuple-element.41.right_ref, bf16[128,1536]{1,0:T(8,128)(2,1)S(1)} %join.1.ahead_ref, ...), custom_call_target="tpu_custom_call", output_to_operand_aliasing={{}: (4, {})} | custom-call | flops 1000000000 | bytes 3000000 | tf_op jit(solution)/shard_map/last/pallas_call | solution.py:819
  (16 shorter events, 0.1 us)
Async XLA Ops:
  0.0 1.9 %copy-start = (bf16[3,128,2048]{2,1,0:T(8,128)(2,1)S(1)}, bf16[3,128,2048]{2,1,0:T(8,128)(2,1)}, u32[]{:S(2)}) copy-start(bf16[3,128,2048]{2,1,0:T(8,128)(2,1)} %projected_ref.7) | copy-start | bytes 4718596
  0.0 1.9 %copy-start.2 = (f32[7,3,2048]{2,0,1:T(8,128)S(1)}, f32[7,3,2048]{2,0,1:T(8,128)}, u32[]{:S(2)}) copy-start(f32[7,3,2048]{2,0,1:T(8,128)} %param.14) | copy-start | bytes 516100
  0.0 8.2 %collective-permute-start.1 = (bf16[544,128]{1,0:T(8,128)(2,1)S(1)}, bf16[544,128]{1,0:T(8,128)(2,1)S(1)}, u32[]{:S(2)}, u32[]{:S(2)}) collective-permute-start(bf16[544,128]{1,0:T(8,128)(2,1)S(1)} %get-tuple-element.35), channel_id=1, source_target_pairs={{0,16},{16,0},{1,17},{17,1},{2,18},{18,2},{3,19},{19,3},{4,20},{20... | collective-permute-start | bytes 417800 | tf_op jit(solution)/shard_map/ppermute | solution.py:718
  1.9 1.8 %copy-start.1 = (f32[64,2048]{1,0:T(8,128)S(1)}, f32[64,2048]{1,0:T(8,128)}, u32[]{:S(2)}) copy-start(f32[64,2048]{1,0:T(8,128)} %out_ref.1) | copy-start | bytes 1572868
  1.9 1.8 %copy-start.3 = (f32[64,64]{1,0:T(8,128)S(1)}, f32[64,64]{1,0:T(8,128)}, u32[]{:S(2)}) copy-start(f32[64,64]{1,0:T(8,128)} %refs_9_.1) | copy-start | bytes 49156
  2.0 1.8 %copy-start.4 = (f32[33,64]{1,0:T(8,128)S(1)}, f32[33,64]{1,0:T(8,128)}, u32[]{:S(2)}) copy-start(f32[33,64]{1,0:T(8,128)} %refs_6_.1) | copy-start | bytes 25348
  2.0 1.8 %copy-start.5 = (f32[2048]{0:T(1024)S(1)}, f32[2048]{0:T(1024)}, u32[]{:S(2)}) copy-start(f32[2048]{0:T(1024)} %param.20) | copy-start | bytes 24580
  2.0 1.8 %copy-start.6 = (f32[2048]{0:T(1024)S(1)}, f32[2048]{0:T(1024)}, u32[]{:S(2)}) copy-start(f32[2048]{0:T(1024)} %param.21) | copy-start | bytes 24580
  2.0 1.8 %copy-start.7 = (f32[64]{0:T(128)S(1)}, f32[64]{0:T(128)}, u32[]{:S(2)}) copy-start(f32[64]{0:T(128)} %param.16) | copy-start | bytes 772
  2.0 1.8 %copy-start.8 = (f32[64]{0:T(128)S(1)}, f32[64]{0:T(128)}, u32[]{:S(2)}) copy-start(f32[64]{0:T(128)} %param.17) | copy-start | bytes 772
  2.0 1.8 %copy-start.9 = (bf16[256,192]{1,0:T(8,128)(2,1)S(1)}, bf16[256,192]{1,0:T(8,128)(2,1)}, u32[]{:S(2)}) copy-start(bf16[256,192]{1,0:T(8,128)(2,1)} %constant.9.clone.refs_4_.forward_ref.refs_3_) | copy-start | bytes 294916
  2.0 1.8 %copy-start.10 = (f32[256,128]{1,0:T(8,128)S(1)}, f32[256,128]{1,0:T(8,128)}, u32[]{:S(2)}) copy-start(f32[256,128]{1,0:T(8,128)} %constant.8.clone.refs_3_.places_ref) | copy-start | bytes 393220
  2.0 1.8 %copy-start.12 = (f32[40,256]{1,0:T(8,128)S(1)}, f32[40,256]{1,0:T(8,128)}, u32[]{:S(2)}) copy-start(f32[40,256]{1,0:T(8,128)} %constant.10.clone.refs_5_) | copy-start | bytes 122884
  2.1 11.2 %collective-permute-start.2 = (bf16[1296,128]{1,0:T(8,128)(2,1)S(1)}, bf16[1296,128]{1,0:T(8,128)(2,1)S(1)}, u32[]{:S(2)}, u32[]{:S(2)}) collective-permute-start(bf16[1296,128]{1,0:T(8,128)(2,1)S(1)} %get-tuple-element.42), channel_id=1, source_target_pairs={{0,16},{16,0},{1,17},{17,1},{2,18},{18,2},{3,19},{19,3},{4,20},{20... | collective-permute-start | bytes 995336 | tf_op jit(solution)/shard_map/ppermute | solution.py:736
  5.5 1.5 %copy-start.11 = (bf16[128,384]{1,0:T(8,128)(2,1)S(1)}, bf16[128,384]{1,0:T(8,128)(2,1)}, u32[]{:S(2)}) copy-start(bf16[128,384]{1,0:T(8,128)(2,1)} %constant.11.clone.backward_ref.refs_4_) | copy-start | bytes 294916
  7.0 8.6 %collective-permute-start = (bf16[528,128]{1,0:T(8,128)(2,1)S(1)}, bf16[528,128]{1,0:T(8,128)(2,1)S(1)}, u32[]{:S(2)}, u32[]{:S(2)}) collective-permute-start(bf16[528,128]{1,0:T(8,128)(2,1)S(1)} %get-tuple-element.34), channel_id=1, source_target_pairs={{0,16},{1,17},{2,18},{3,19},{4,20},{5,21},{6,22},{7,23},{8,24},{9,... | collective-permute-start | bytes 405512 | tf_op jit(solution)/shard_map/ppermute | solution.py:780
